TPU v7x, 32 devices: a whole 2x2x4 slice. The times are simulated.
32 devices in a mesh: grp: 2 (over x), ctx: 4 (over y, core), head: 4 (over z).
Axes of the slice: x: 2, y: 2, z: 4, core: 2. Of those that a mesh axis runs over, the one named last changes fastest.
Arguments:
- queries: bfloat16 [8192, 4096], P(('grp', 'ctx'), 'head'), parts along dimension 0, may hold values from -6 to 6
- keys: bfloat16 [8192, 4096], P(('grp', 'ctx'), 'head'), parts along dimension 0, may hold values from -6 to 6
- values: bfloat16 [8192, 4096], P(('grp', 'ctx'), 'head'), parts along dimension 0, may hold values from -6 to 6
- init_state: float32 [64, 128, 128], P(('grp', 'head')), parts along dimension 0, may hold values from -192 to 192
- out_grad: bfloat16 [8192, 4096], P(('grp', 'ctx'), 'head'), parts along dimension 0, may hold values from -6 to 6
Outputs:
- output: bfloat16 [8192, 4096], P(('grp', 'ctx'), 'head'), parts along dimension 0
- query_grad: bfloat16 [8192, 4096], P(('grp', 'ctx'), 'head'), parts along dimension 0
- key_grad: bfloat16 [8192, 4096], P(('grp', 'ctx'), 'head'), parts along dimension 0
- value_grad: bfloat16 [8192, 4096], P(('grp', 'ctx'), 'head'), parts along dimension 0
- state_grad: float32 [64, 128, 128], P(('grp', 'head')), parts along dimension 0
There are 2 independent parts, one for each index of `grp`. A program takes and returns all parts, laid end to end along the dimension named above; each array names one. Nothing has to cross between parts.
All inputs are finite; a program needn't handle non-finite values.
Results may differ from a plain program's by a relative error of at most 0.0058.
Values sent between devices are 32-bit elements; how exact they have to be, the bound alone decides.
No kernel may reach another device: no remote copies, remote signals or barrier semaphores. Data moves between devices by JAX's collectives and lax.ppermute only.
A program may use at most 128 MiB of HBM per device.

v0:
```python
import jax
import jax.numpy as jnp
from jax import lax
from jax.sharding import PartitionSpec as P


def shards(queries, keys, values, init_state, out_grad):
    rows = queries.shape[0]
    heads = init_state.shape[0]
    dim = init_state.shape[1]
    q_loc = queries.reshape(rows, heads, dim)
    k_loc = keys.reshape(rows, heads, dim)
    v_loc = values.reshape(rows, heads, dim)
    upstream = out_grad.reshape(rows, heads, dim).astype(jnp.float32)
    block_state = jnp.einsum("thd,the->hde", k_loc, v_loc, preferred_element_type=jnp.float32)
    every_state = lax.all_gather(block_state[None], "ctx", axis=0, tiled=True)
    place = lax.axis_index("ctx")
    order = jnp.arange(every_state.shape[0])
    earlier = jnp.sum(jnp.where((order < place)[:, None, None, None], every_state, 0.0), axis=0)
    prefix_b = (init_state + earlier).astype(jnp.bfloat16)
    causal = (jnp.arange(rows)[:, None] >= jnp.arange(rows)[None, :])[None]
    raw = jnp.einsum("thd,shd->hts", q_loc, k_loc, preferred_element_type=jnp.float32)
    scores = jnp.where(causal, raw, 0.0).astype(jnp.bfloat16)
    attended = jnp.einsum("thd,hde->the", q_loc, prefix_b, preferred_element_type=jnp.float32)
    attended = attended + jnp.einsum(
        "hts,she->the", scores, v_loc, preferred_element_type=jnp.float32
    )
    inv_rms = lax.rsqrt(jnp.mean(attended * attended, axis=-1, keepdims=True) + 1e-06)
    normed = attended * inv_rms
    output = normed.astype(jnp.bfloat16).reshape(rows, heads * dim)
    grad_att = (
        inv_rms * (upstream - normed * jnp.mean(upstream * normed, axis=-1, keepdims=True))
    ).astype(jnp.bfloat16)
    block_grad = jnp.einsum("thd,the->hde", q_loc, grad_att, preferred_element_type=jnp.float32)
    every_grad = lax.all_gather(block_grad[None], "ctx", axis=0, tiled=True)
    later = jnp.sum(jnp.where((order > place)[:, None, None, None], every_grad, 0.0), axis=0)
    state_grad = jnp.sum(every_grad, axis=0)
    suffix_b = later.astype(jnp.bfloat16)
    grad_raw = jnp.einsum("the,she->hts", grad_att, v_loc, preferred_element_type=jnp.float32)
    grad_scores = jnp.where(causal, grad_raw, 0.0).astype(jnp.bfloat16)
    query_grad = jnp.einsum("the,hde->thd", grad_att, prefix_b, preferred_element_type=jnp.float32)
    query_grad = query_grad + jnp.einsum(
        "hts,shd->thd", grad_scores, k_loc, preferred_element_type=jnp.float32
    )
    key_grad = jnp.einsum("hts,thd->shd", grad_scores, q_loc, preferred_element_type=jnp.float32)
    key_grad = key_grad + jnp.einsum(
        "she,hde->shd", v_loc, suffix_b, preferred_element_type=jnp.float32
    )
    value_grad = jnp.einsum("hts,the->she", scores, grad_att, preferred_element_type=jnp.float32)
    value_grad = value_grad + jnp.einsum(
        "shd,hde->she", k_loc, suffix_b, preferred_element_type=jnp.float32
    )
    flat = (rows, heads * dim)
    return (
        output,
        query_grad.astype(jnp.bfloat16).reshape(flat),
        key_grad.astype(jnp.bfloat16).reshape(flat),
        value_grad.astype(jnp.bfloat16).reshape(flat),
        state_grad,
    )


def solution(mesh):
    placed = (
        P(("grp", "ctx"), "head"),
        P(("grp", "ctx"), "head"),
        P(("grp", "ctx"), "head"),
        P(("grp", "head"), None, None),
        P(("grp", "ctx"), "head"),
    )
    return jax.shard_map(
        shards,
        mesh=mesh,
        in_specs=placed,
        out_specs=(
            P(("grp", "ctx"), "head"),
            P(("grp", "ctx"), "head"),
            P(("grp", "ctx"), "head"),
            P(("grp", "ctx"), "head"),
            P(("grp", "head"), None, None),
        ),
        check_vma=False,
    )
```

profile of v0, /device:TPU:0, one launch (start us, length us, event | category | flops | bytes accessed | tf_op | source)
XLA Modules:
  0.0 147.8 jit_solution(8208181806434422570)
XLA Ops:
  7.2 0.0 copy-start
  7.2 0.0 all-gather.5.cloned.1.call-start
  7.2 3.7 %copy.64 = bf16[128,8,8,128]{3,2,1,0:T(8,128)(2,1)} copy(bf16[128,8,8,128]{3,1,2,0:T(8,128)(2,1)} %bitcast.108) | data formatting | bytes 4194304
  10.9 4.1 %copy.32 = bf16[1024,8,128]{0,2,1:T(8,128)(2,1)} copy(bf16[1024,8,128]{2,1,0:T(8,128)(2,1)} %bitcast.107) | data formatting | bytes 4194304 | tf_op jit(solution)/shard_map/reshape | solution.py:12
  15.0 0.0 copy-done
  15.0 3.1 %fusion.14 = f32[8,128,128]{2,1,0:T(8,128)} fusion(bf16[1024,8,128]{0,2,1:T(8,128)(2,1)} %copy.32, bf16[1024,1024]{1,0:T(8,128)(2,1)S(1)} %copy-done), kind=kOutput, calls=%fused_computation.25 | convolution fusion | flops 268435456 | bytes 4718592 | tf_op jit(solution)/shard_map/thd,the->hde/dot_general | solution.py:15
  18.2 0.0 all-gather.5.cloned.1.call-update
  18.2 0.0 all-gather.7.cloned.1.call-start
  18.2 4.1 %copy.39 = f32[1024,1024]{0,1:T(8,128)} copy(bf16[1024,1024]{1,0:T(8,128)(2,1)} %param.9) | data formatting | bytes 6291456 | tf_op jit(solution)/shard_map/convert_element_type | solution.py:14
  22.4 0.3 iota_compare_fusion
  22.7 10.2 %select_convert_fusion.1 = bf16[8,1024,1024]{2,1,0:T(8,128)(2,1)} fusion(pred[1024,1024]{1,0:T(8,128)(4,1)S(1)} %iota_compare_fusion, bf16[1024,1024]{1,0:T(8,128)(2,1)} %param.6, bf16[1024,1024]{1,0:T(8,128)(2,1)} %param.5), kind=kOutput, calls=%fused_computation.1 | convolution fusion | flops 2164260864 | bytes 22020096 | tf_op jit(solution)/shard_map/thd,shd->hts/dot_general | solution.py:22
  32.9 10.7 %all-gather.5.cloned.1.call-done = f32[32,128,128]{2,1,0:T(8,128)} async-done(((f32[8,128,128]{2,1,0:T(8,128)}), f32[32,128,128]{2,1,0:T(8,128)}) %all-gather.5.cloned.1.call-update) | async-done | bytes 2097168 | tf_op jit(solution)/shard_map/all_gather | solution.py:16
  43.6 0.0 copy-start.8
  43.6 0.0 copy-start.5
  43.6 2.1 %select_reduce_fusion.1 = f32[8,128,128]{2,1,0:T(8,128)S(1)} fusion(f32[4,8,128,128]{3,2,1,0:T(8,128)} %bitcast.112, pred[4]{0:T(512)(128)(4,1)S(1)} %iota_compare_fusion.2), kind=kLoop, calls=%fused_computation.28 | loop fusion | flops 917504 | bytes 2621444 | tf_op jit(solution)/shard_map/reduce_sum | solution.py:19
  45.7 0.0 copy-done.8
  45.7 0.1 add_convert_fusion.1
  45.8 0.3 copy-done.5
  46.0 2.7 %fusion.7 = f32[8,128,1024]{2,1,0:T(8,128)} fusion(bf16[8,128,128]{2,1,0:T(8,128)(2,1)S(1)} %add_convert_fusion.1, bf16[1024,1024]{1,0:T(8,128)(2,1)S(1)} %copy-done.5), kind=kOutput, calls=%fused_computation.18 | convolution fusion | flops 268435456 | bytes 6553600 | tf_op jit(solution)/shard_map/thd,hde->the/dot_general | solution.py:24
  48.7 9.9 %multiply_reduce_fusion.1 = (f32[1024,8]{0,1:T(8,128)S(1)}, f32[1024,8,128]{0,2,1:T(8,128)S(1)}) fusion(bf16[8,1024,1024]{2,1,0:T(8,128)(2,1)} %select_convert_fusion.1, f32[8,128,1024]{2,1,0:T(8,128)} %fusion.7, bf16[1024,1024]{1,0:T(8,128)(2,1)S(1)} %copy-done), kind=kOutput, calls=%fused_computation.10 | convolution fusion | flops 2150621184 | bytes 27295744 | tf_op jit(solution)/shard_map/hts,she->the/dot_general | solution.py:25
  58.7 0.0 copy-start.1
  58.7 3.4 %multiply_reduce_fusion = f32[1024,8]{0,1:T(8,128)S(1)} fusion(f32[1024,8,128]{0,2,1:T(8,128)S(1)} %get-tuple-element.20, f32[1024,8]{0,1:T(8,128)S(1)} %add_rsqrt_fusion, f32[1024,1024]{0,1:T(8,128)} %copy.39), kind=kLoop, calls=%fused_computation.9 | loop fusion | flops 3137536 | bytes 8454144 | tf_op jit(solution)/shard_map/reduce_sum | solution.py:32
  62.2 0.0 copy-done.1
  62.2 0.0 copy-start.6
  62.2 2.7 %multiply_convert_fusion = (bf16[1024,8,128]{0,2,1:T(8,128)(2,1)S(1)}, bf16[1024,8,128]{0,2,1:T(8,128)(2,1)}) fusion(f32[1024,8,128]{0,2,1:T(8,128)S(1)} %get-tuple-element.20, f32[1024,8]{0,1:T(8,128)S(1)} %broadcast_multiply_fusion, f32[1024,8]{0,1:T(8,128)S(1)} %add_rsqrt_fusion, f32[1024,1024]{0,1:T(8,128)S(1)} %copy-done.1), kind=kLoop, calls=%fused_computation.8 | loop fusion | flops 6291456 | bytes 12648448 | tf_op jit(solution)/shard_map/convert_element_type | solution.py:33
  64.9 0.0 copy-start.2
  64.9 1.3 copy-done.2
  66.2 0.0 copy-done.6
  66.2 1.6 %fusion.26 = f32[8,128,128]{1,2,0:T(8,128)} fusion(bf16[1024,8,128]{0,2,1:T(8,128)(2,1)S(1)} %get-tuple-element.17, bf16[1024,1024]{1,0:T(8,128)(2,1)S(1)} %copy-done.6), kind=kOutput, calls=%fused_computation.39 | convolution fusion | flops 268435456 | bytes 4718592 | tf_op jit(solution)/shard_map/thd,the->hde/dot_general | solution.py:34
  67.7 0.0 copy-start.3
  67.7 10.3 %select_convert_fusion = bf16[8,1024,1024]{2,1,0:T(8,128)(2,1)} fusion(pred[1024,1024]{1,0:T(8,128)(4,1)S(1)} %iota_compare_fusion, bf16[1024,8,128]{0,2,1:T(8,128)(2,1)} %copy-done.2, bf16[1024,1024]{1,0:T(8,128)(2,1)S(1)} %copy-done), kind=kOutput, calls=%fused_computation | convolution fusion | flops 2164260864 | bytes 22020096 | tf_op jit(solution)/shard_map/the,she->hts/dot_general | solution.py:39
  78.0 0.0 copy-done.3
  78.0 2.8 %fusion.32 = f32[8,128,1024]{2,1,0:T(8,128)} fusion(bf16[8,128,128]{2,1,0:T(8,128)(2,1)S(1)} %add_convert_fusion.1, bf16[1024,8,128]{0,2,1:T(8,128)(2,1)S(1)} %copy-done.3), kind=kOutput, calls=%fused_computation.48 | convolution fusion | flops 268435456 | bytes 6553600 | tf_op jit(solution)/shard_map/the,hde->thd/dot_general | solution.py:41
  80.8 0.0 copy-done.9
  80.8 1.0 copy.46
  81.8 0.0 all-gather.7.cloned.1.call-update
  81.8 11.8 %fusion.1 = bf16[1024,8,128]{0,2,1:T(8,128)(2,1)} fusion(f32[8,128,1024]{2,1,0:T(8,128)} %fusion.32, bf16[8,1024,1024]{2,1,0:T(8,128)(2,1)} %select_convert_fusion, bf16[1024,8,128]{0,2,1:T(8,128)(2,1)} %copy.32), kind=kOutput, calls=%fused_computation.5 | convolution fusion | flops 2149580800 | bytes 25165824 | tf_op jit(solution)/shard_map/hts,shd->thd/dot_general | solution.py:42
  93.6 4.0 %copy.52 = bf16[1024,1024]{1,0:T(8,128)(2,1)} copy(bf16[1024,1024]{0,1:T(8,128)(2,1)} %bitcast.105) | data formatting | bytes 4194304
  97.6 3.9 %copy.51 = bf16[1024,1024]{1,0:T(8,128)(2,1)} copy(bf16[1024,1024]{0,1:T(8,128)(2,1)} %bitcast.109) | data formatting | bytes 4194304
  101.5 10.9 %fusion.33 = f32[8,128,1024]{2,1,0:T(8,128)} fusion(bf16[1024,8,128]{0,2,1:T(8,128)(2,1)} %copy-done.2, bf16[8,1024,1024]{2,1,0:T(8,128)(2,1)} %select_convert_fusion.1), kind=kOutput, calls=%fused_computation.49 | convolution fusion | flops 2147483648 | bytes 23068672 | tf_op jit(solution)/shard_map/hts,the->she/dot_general | solution.py:49
  112.4 2.7 %fusion.31 = (f32[8,128,128]{2,1,0:T(8,128)}, bf16[8,128,128]{2,1,0:T(8,128)(2,1)S(1)}) fusion(f32[4,8,128,128]{3,2,1,0:T(8,128)} %bitcast.111, pred[4]{0:T(512)(128)(4,1)S(1)} %iota_compare_fusion.1), kind=kLoop, calls=%fused_computation.47 | loop fusion | flops 1310720 | bytes 2883588 | tf_op jit(solution)/shard_map/reduce_sum | solution.py:37
  115.1 2.9 %fusion.11 = f32[8,128,1024]{2,1,0:T(8,128)} fusion(bf16[8,128,128]{2,1,0:T(8,128)(2,1)S(1)} %get-tuple-element.16, bf16[1024,1024]{1,0:T(8,128)(2,1)S(1)} %copy-done), kind=kOutput, calls=%fused_computation.22 | convolution fusion | flops 268435456 | bytes 6553600 | tf_op jit(solution)/shard_map/she,hde->shd/dot_general | solution.py:46
  118.0 0.6 copy-done.4
  118.6 0.9 copy-done.7
  119.5 2.1 %add_convert_fusion = bf16[8,128,1024]{2,1,0:T(8,128)(2,1)} fusion(f32[8,128,1024]{2,1,0:T(8,128)S(1)} %copy-done.4, bf16[8,128,128]{2,1,0:T(8,128)(2,1)S(1)} %get-tuple-element.16, bf16[1024,1024]{1,0:T(8,128)(2,1)S(1)} %copy-done.7), kind=kOutput, calls=%fused_computation.7 | convolution fusion | flops 270532608 | bytes 8650752 | tf_op jit(solution)/shard_map/shd,hde->she/dot_general | solution.py:50
  121.6 3.9 %copy.54 = bf16[1024,1024]{1,0:T(8,128)(2,1)} copy(bf16[1024,1024]{0,1:T(8,128)(2,1)} %bitcast.110) | data formatting | bytes 4194304
  125.6 11.4 %fusion = bf16[1024,8,128]{0,2,1:T(8,128)(2,1)} fusion(f32[8,128,1024]{2,1,0:T(8,128)} %fusion.11, bf16[8,1024,1024]{2,1,0:T(8,128)(2,1)} %select_convert_fusion, bf16[1024,1024]{1,0:T(8,128)(2,1)} %param.5), kind=kOutput, calls=%fused_computation.3 | convolution fusion | flops 2149580800 | bytes 25165824 | tf_op jit(solution)/shard_map/hts,thd->shd/dot_general | solution.py:45
  137.0 3.9 %copy.53 = bf16[1024,1024]{1,0:T(8,128)(2,1)} copy(bf16[1024,1024]{0,1:T(8,128)(2,1)} %bitcast.106) | data formatting | bytes 4194304
  (8 shorter events, 0.0 us)
Async XLA Ops:
  7.2 7.8 %copy-start = (bf16[1024,1024]{1,0:T(8,128)(2,1)S(1)}, bf16[1024,1024]{1,0:T(8,128)(2,1)}, u32[]{:S(2)}) copy-start(bf16[1024,1024]{1,0:T(8,128)(2,1)} %param.7) | copy-start | bytes 6291460
  7.2 36.4 %all-gather.5.cloned.1.call-start = ((), (), s32[]{:S(2)}) async-start(), calls=%async_computation | async-start | bytes 2621440 | tf_op jit(solution)/shard_map/all_gather | solution.py:16
  18.2 94.2 %all-gather.7.cloned.1.call-start = ((), (), s32[]{:S(2)}) async-start(), calls=%async_computation.1 | async-start | bytes 2621440 | tf_op jit(solution)/shard_map/all_gather | solution.py:35
  43.6 2.1 %copy-start.8 = (f32[8,128,128]{2,1,0:T(8,128)S(1)}, f32[8,128,128]{2,1,0:T(8,128)}, u32[]{:S(2)}) copy-start(f32[8,128,128]{2,1,0:T(8,128)} %param.8) | copy-start | bytes 1572868
  43.6 2.4 %copy-start.5 = (bf16[1024,1024]{1,0:T(8,128)(2,1)S(1)}, bf16[1024,1024]{1,0:T(8,128)(2,1)}, u32[]{:S(2)}) copy-start(bf16[1024,1024]{1,0:T(8,128)(2,1)} %param.5) | copy-start | bytes 6291460
  58.7 3.5 %copy-start.1 = (f32[1024,1024]{0,1:T(8,128)S(1)}, f32[1024,1024]{0,1:T(8,128)}, u32[]{:S(2)}) copy-start(f32[1024,1024]{0,1:T(8,128)} %copy.39) | copy-start | bytes 12582916
  62.2 4.0 %copy-start.6 = (bf16[1024,1024]{1,0:T(8,128)(2,1)S(1)}, bf16[1024,1024]{1,0:T(8,128)(2,1)}, u32[]{:S(2)}) copy-start(bf16[1024,1024]{1,0:T(8,128)(2,1)} %param.5) | copy-start | bytes 6291460
  64.9 1.3 copy-start.2
  67.7 10.3 %copy-start.3 = (bf16[1024,8,128]{0,2,1:T(8,128)(2,1)S(1)}, bf16[1024,8,128]{0,2,1:T(8,128)(2,1)}, u32[]{:S(2)}) copy-start(bf16[1024,8,128]{0,2,1:T(8,128)(2,1)} %copy-done.2) | copy-start | bytes 6291460
  78.0 2.8 %copy-start.9 = (f32[8,128,128]{1,2,0:T(8,128)S(1)}, f32[8,128,128]{1,2,0:T(8,128)}, u32[]{:S(2)}) copy-start(f32[8,128,128]{1,2,0:T(8,128)} %fusion.26) | copy-start | bytes 1572868
  115.1 3.5 %copy-start.4 = (f32[8,128,1024]{2,1,0:T(8,128)S(1)}, f32[8,128,1024]{2,1,0:T(8,128)}, u32[]{:S(2)}) copy-start(f32[8,128,1024]{2,1,0:T(8,128)} %fusion.33) | copy-start | bytes 12582916
  115.1 4.4 %copy-start.7 = (bf16[1024,1024]{1,0:T(8,128)(2,1)S(1)}, bf16[1024,1024]{1,0:T(8,128)(2,1)}, u32[]{:S(2)}) copy-start(bf16[1024,1024]{1,0:T(8,128)(2,1)} %param.6) | copy-start | bytes 6291460
Sparse Core Ops, SparseCore 0:
  18.3 25.2 all-gather.4
  81.9 22.5 all-gather.6
where the time goes:
time: 148 us
  matrix products  79.7 us (54%)
  local copies, waits for them, and re-layouts  31.8 us (21%)
  between operations  14.1 us (10%)
  other arithmetic  11.3 us (8%)
  waiting for transfers between devices  10.7 us (7%)
    unnamed x25, local copies, waits for them, and re-layouts  22.6 us
    dot_general x1, matrix products, shards(): jnp.einsum('hts,shd->thd', grad_scores, k_loc, preferred_element_type=jnp...  11.8 us
    dot_general x1, matrix products, shards(): jnp.einsum('hts,thd->shd', grad_scores, q_loc, preferred_element_type=jnp...  11.4 us
    dot_general x1, matrix products, shards(): jnp.einsum('hts,the->she', scores, grad_att, preferred_element_type=jnp.f...  10.9 us
    all_gather x1, waiting for transfers between devices, shards(): every_state = lax.all_gather(block_state[None], 'ctx', axis=0, tiled=True)  10.7 us
    dot_general x1, matrix products, shards(): jnp.einsum('the,she->hts', grad_att, v_loc, preferred_element_type=jnp.fl...  10.3 us
    dot_general x1, matrix products, shards(): jnp.einsum('thd,shd->hts', q_loc, k_loc, preferred_element_type=jnp.float32)  10.2 us
    dot_general x1, matrix products, shards(): jnp.einsum('hts,she->the', scores, v_loc, preferred_element_type=jnp.floa...  9.93 us
  transfers between devices with their start and end apart: 2, of which 1 were waited for; matrix products, arithmetic and copies ran while one was open for 31% of the time, Pallas kernels for 0%

commit v1 on v0

v1 whole, which is shorter than its diff:
```python
import functools

import jax
import jax.numpy as jnp
from jax import lax
from jax.experimental import pallas as pl
from jax.experimental.pallas import tpu as pltpu
from jax.sharding import PartitionSpec as P

F32 = jnp.float32
BF16 = jnp.bfloat16
EPS = 1e-06


def mm(a, b):
    return lax.dot_general(a, b, (((1,), (0,)), ((), ())), preferred_element_type=F32)


def mm_rt(a, b):
    return lax.dot_general(a, b, (((1,), (1,)), ((), ())), preferred_element_type=F32)


def mm_lt(a, b):
    return lax.dot_general(a, b, (((0,), (0,)), ((), ())), preferred_element_type=F32)


def chunk_of(rows):
    return 256 if rows % 256 == 0 else rows


def params(mib):
    return pltpu.CompilerParams(vmem_limit_bytes=mib * 1024 * 1024)


def state_kernel(dim, size, k_ref, v_ref, total_ref, before_ref):
    heads = total_ref.shape[0]
    for h in range(heads):
        cols = slice(h * dim, (h + 1) * dim)
        run = None
        for c in range(k_ref.shape[0] // size):
            rows = slice(c * size, (c + 1) * size)
            before_ref[h, c] = jnp.zeros((dim, dim), BF16) if run is None else run.astype(BF16)
            term = mm_lt(k_ref[rows, cols], v_ref[rows, cols])
            run = term if run is None else run + term
        total_ref[h] = run


def inner_kernel(dim, size, q_ref, k_ref, v_ref, before_ref, att_ref):
    heads = before_ref.shape[0]
    keep = lax.broadcasted_iota(jnp.int32, (size, size), 0) >= lax.broadcasted_iota(
        jnp.int32, (size, size), 1
    )
    for h in range(heads):
        cols = slice(h * dim, (h + 1) * dim)
        for c in range(q_ref.shape[0] // size):
            rows = slice(c * size, (c + 1) * size)
            q, k, v = q_ref[rows, cols], k_ref[rows, cols], v_ref[rows, cols]
            scores = jnp.where(keep, mm_rt(q, k), 0.0).astype(BF16)
            att = mm(scores, v)
            if c > 0:
                att = att + mm(q, before_ref[h, c])
            att_ref[rows, cols] = att


def norm_kernel(
    dim, size, att_ref, q_ref, g_ref, prefix_ref, out_ref, ga_ref, total_ref, after_ref
):
    heads = prefix_ref.shape[0]
    for h in range(heads):
        cols = slice(h * dim, (h + 1) * dim)
        prefix = prefix_ref[h]
        run = None
        for c in reversed(range(q_ref.shape[0] // size)):
            rows = slice(c * size, (c + 1) * size)
            q = q_ref[rows, cols]
            att = att_ref[rows, cols] + mm(q, prefix)
            inv = lax.rsqrt(jnp.mean(att * att, axis=-1, keepdims=True) + EPS)
            normed = att * inv
            out_ref[rows, cols] = normed.astype(BF16)
            up = g_ref[rows, cols].astype(F32)
            along = jnp.mean(up * normed, axis=-1, keepdims=True)
            ga = (inv * (up - normed * along)).astype(BF16)
            ga_ref[rows, cols] = ga
            after_ref[h, c] = jnp.zeros((dim, dim), BF16) if run is None else run.astype(BF16)
            term = mm_lt(q, ga)
            run = term if run is None else run + term
        total_ref[h] = run


def back_kernel(
    dim, size, q_ref, k_ref, v_ref, ga_ref, prefix_ref, before_ref, after_ref, qg_ref, kg_ref, vg_ref
):
    heads = prefix_ref.shape[0]
    row = lax.broadcasted_iota(jnp.int32, (size, size), 0)
    col = lax.broadcasted_iota(jnp.int32, (size, size), 1)
    keep, keep_t = row >= col, row <= col
    chunks = q_ref.shape[0] // size
    for h in range(heads):
        cols = slice(h * dim, (h + 1) * dim)
        prefix = prefix_ref[h]
        for c in range(chunks):
            rows = slice(c * size, (c + 1) * size)
            q, k, v, ga = q_ref[rows, cols], k_ref[rows, cols], v_ref[rows, cols], ga_ref[rows, cols]
            grad = jnp.where(keep, mm_rt(ga, v), 0.0).astype(BF16)
            qg = mm(grad, k) + mm_rt(ga, prefix)
            if c > 0:
                qg = qg + mm_rt(ga, before_ref[h, c])
            qg_ref[rows, cols] = qg.astype(BF16)
            scores_t = jnp.where(keep_t, mm_rt(k, q), 0.0).astype(BF16)
            vg = mm(scores_t, ga)
            kg = mm_lt(grad, q)
            if c < chunks - 1:
                after = after_ref[h, c]
                vg = vg + mm(k, after)
                kg = kg + mm_rt(v, after)
            vg_ref[rows, cols] = vg
            kg_ref[rows, cols] = kg


def last_kernel(dim, k_ref, v_ref, suffix_ref, kp_ref, vp_ref, kg_ref, vg_ref):
    for h in range(suffix_ref.shape[0]):
        cols = slice(h * dim, (h + 1) * dim)
        suffix = suffix_ref[h]
        kg_ref[:, cols] = (kp_ref[:, cols] + mm_rt(v_ref[:, cols], suffix)).astype(BF16)
        vg_ref[:, cols] = (vp_ref[:, cols] + mm(k_ref[:, cols], suffix)).astype(BF16)


def across(own, n):
    place = lax.axis_index("ctx")
    if n % 2 or own.shape[0] % 2:
        every = lax.all_gather(own, "ctx", axis=0)
        order = jnp.arange(n)[:, None, None, None]
        return (
            jnp.sum(jnp.where(order < place, every, 0.0), axis=0),
            jnp.sum(jnp.where(order > place, every, 0.0), axis=0),
        )
    half, pairs = own.shape[0] // 2, n // 2
    first = place % 2 == 0
    pair = place // 2
    swap = [(i, i ^ 1) for i in range(n)]
    shift = [(i, (i + 2) % n) for i in range(n)]
    near = lax.ppermute(own, "ctx", swap)
    both = own + near
    mine = jnp.where(first, both[:half], both[half:])
    moving, far = mine, []
    for _ in range(pairs - 1):
        moving = lax.ppermute(moving, "ctx", shift)
        far.append(moving)
    earlier, later = jnp.zeros_like(own), jnp.zeros_like(own)
    if pairs == 2:
        other = lax.ppermute(far[0], "ctx", swap)
        full = jnp.where(
            first, jnp.concatenate([far[0], other]), jnp.concatenate([other, far[0]])
        )
        earlier, later = jnp.where(pair > 0, full, 0.0), jnp.where(pair > 0, 0.0, full)
    elif pairs > 2:
        low = sum(jnp.where(pair >= j + 1, r, 0.0) for j, r in enumerate(far))
        high = sum(jnp.where(pair >= j + 1, 0.0, r) for j, r in enumerate(far))
        sums = jnp.stack([low, high])
        other = lax.ppermute(sums, "ctx", swap)
        full = jnp.where(
            first, jnp.concatenate([sums, other], 1), jnp.concatenate([other, sums], 1)
        )
        earlier, later = full[0], full[1]
    return earlier + jnp.where(first, 0.0, near), later + jnp.where(first, near, 0.0)


def shards(n, queries, keys, values, init_state, out_grad):
    rows, width = queries.shape
    heads, dim = init_state.shape[:2]
    size = chunk_of(rows)
    chunks = rows // size
    per = 2 if heads % 2 == 0 else 1
    grid = (heads // per,)
    tall = pl.BlockSpec((rows, per * dim), lambda i: (0, i))
    state = pl.BlockSpec((per, dim, dim), lambda i: (i, 0, 0))
    states = pl.BlockSpec((per, chunks, dim, dim), lambda i: (i, 0, 0, 0))
    tall_b = jax.ShapeDtypeStruct((rows, width), BF16)
    tall_f = jax.ShapeDtypeStruct((rows, width), F32)
    state_f = jax.ShapeDtypeStruct((heads, dim, dim), F32)
    states_b = jax.ShapeDtypeStruct((heads, chunks, dim, dim), BF16)
    small = 2 * heads * rows * dim * dim
    square = 2 * heads * rows * size * dim

    def call(body, name, ins, outs, flops, nbytes, mib=16):
        return pl.pallas_call(
            body,
            grid=grid,
            in_specs=[s for s in ins],
            out_specs=[s for s, _ in outs],
            out_shape=[t for _, t in outs],
            compiler_params=params(mib),
            cost_estimate=pl.CostEstimate(flops=flops, bytes_accessed=nbytes, transcendentals=0),
            name=name,
        )

    piece = rows * width * 2
    block_state, before = call(
        functools.partial(state_kernel, dim, size),
        "states",
        [tall, tall],
        [(state, state_f), (states, states_b)],
        small,
        2 * piece,
    )(keys, values)
    (inner,) = call(
        functools.partial(inner_kernel, dim, size),
        "inner",
        [tall, tall, tall, states],
        [(tall, tall_f)],
        2 * square + small,
        5 * piece,
    )(queries, keys, values, before)
    earlier, _ = across(block_state, n)
    prefix_b = (init_state + earlier).astype(BF16)
    output, grad_att, block_grad, after = call(
        functools.partial(norm_kernel, dim, size),
        "norm",
        [tall, tall, tall, state],
        [(tall, tall_b), (tall, tall_b), (state, state_f), (states, states_b)],
        2 * small,
        6 * piece,
    )(inner, queries, out_grad, prefix_b)
    earlier_grad, later_grad = across(block_grad, n)
    state_grad = earlier_grad + block_grad + later_grad
    suffix_b = later_grad.astype(BF16)
    query_grad, key_part, value_part = call(
        functools.partial(back_kernel, dim, size),
        "back",
        [tall, tall, tall, tall, state, states, states],
        [(tall, tall_b), (tall, tall_f), (tall, tall_f)],
        5 * square + 3 * small,
        9 * piece,
        24,
    )(queries, keys, values, grad_att, prefix_b, before, after)
    key_grad, value_grad = call(
        functools.partial(last_kernel, dim),
        "last",
        [tall, tall, state, tall, tall],
        [(tall, tall_b), (tall, tall_b)],
        2 * small,
        8 * piece,
    )(keys, values, suffix_b, key_part, value_part)
    return output, query_grad, key_grad, value_grad, state_grad


def solution(mesh):
    wide = P(("grp", "ctx"), "head")
    deep = P(("grp", "head"), None, None)
    return jax.shard_map(
        functools.partial(shards, mesh.shape["ctx"]),
        mesh=mesh,
        in_specs=(wide, wide, wide, deep, wide),
        out_specs=(wide, wide, wide, wide, deep),
        check_vma=False,
    )
```

time: 148 us -> 65.5 us (0.44)
  matrix products: 79.7 us -> 0 us
  Pallas kernels: 0 us -> 31.8 us
  local copies, waits for them, and re-layouts: 31.8 us -> 6.38 us
  between operations: 14.1 us -> 0.72 us
  other arithmetic: 11.3 us -> 3.49 us
  waiting for transfers between devices: 10.7 us -> 16.9 us
  starting transfers between devices: 0.08 us -> 5.91 us
    dot_general x12 -> x0, matrix products: 79.7 us -> none  [the longest x1 11.8 us: shards(): jnp.einsum('hts,shd->thd', grad_scores, k_loc, preferred_element_type=jnp...]
    pallas_call x0 -> x5, Pallas kernels: none -> 31.8 us  [the longest x1 12.2 us: shards(): call(functools.partial(back_kernel, dim, size), 'back', [tall, tall, tall...]
    ppermute x0 -> x6, waiting for transfers between devices: none -> 16.9 us  [the longest x2 13.4 us: across(): moving = lax.ppermute(moving, 'ctx', shift)]
    unnamed x25 -> x18, local copies, waits for them, and re-layouts: 22.6 us -> 6.38 us
    all_gather x2 -> x0, waiting for transfers between devices: 10.7 us -> none  [the longest x1 10.7 us: shards(): every_state = lax.all_gather(block_state[None], 'ctx', axis=0, tiled=True)]
    reduce_sum x3 -> x0, other arithmetic: 8.24 us -> none  [the longest x1 3.45 us: shards(): jnp.mean(upstream * normed, axis=-1, keepdims=True)]
    ppermute x0 -> x6, starting transfers between devices: none -> 5.91 us  [the longest x2 4.77 us: across(): moving = lax.ppermute(moving, 'ctx', shift)]
    convert_element_type x1 -> x0, local copies, waits for them, and re-layouts: 4.13 us -> none  [shards(): upstream = out_grad.reshape(rows, heads, dim).astype(jnp.float32)]
  transfers between devices with their start and end apart: 2 -> 6, of which waited for: 1 -> 4; matrix products, arithmetic and copies ran while one was open for 31% -> 0% of each run, Pallas kernels for 0% -> 27%
where the time goes in v1:
time: 65.5 us; the launch traced here: 65.2 us
  Pallas kernels  31.8 us (49%)
  waiting for transfers between devices  16.9 us (26%)
  local copies, waits for them, and re-layouts  6.38 us (10%)
  starting transfers between devices  5.91 us (9%)
  other arithmetic  3.49 us (5%)
  between operations  0.72 us (1%)
    ppermute x2, waiting for transfers between devices, across(): moving = lax.ppermute(moving, 'ctx', shift)  13.4 us
    pallas_call x1, Pallas kernels, shards(): call(functools.partial(back_kernel, dim, size), 'back', [tall, tall, tall...  12.2 us
    pallas_call x1, Pallas kernels, shards(): call(functools.partial(norm_kernel, dim, size), 'norm', [tall, tall, tall...  7.04 us
    unnamed x18, local copies, waits for them, and re-layouts  6.38 us
    pallas_call x1, Pallas kernels, shards(): call(functools.partial(inner_kernel, dim, size), 'inner', [tall, tall, ta...  5.58 us
    ppermute x2, starting transfers between devices, across(): moving = lax.ppermute(moving, 'ctx', shift)  4.77 us
    pallas_call x1, Pallas kernels, shards(): call(functools.partial(last_kernel, dim), 'last', [tall, tall, state, tal...  4.18 us
    ppermute x2, waiting for transfers between devices, across(): near = lax.ppermute(own, 'ctx', swap)  3.42 us
  transfers between devices with their start and end apart: 6, of which 4 were waited for; matrix products, arithmetic and copies ran while one was open for 0% of the time, Pallas kernels for 27%

profile of v1, /device:TPU:0, one launch (start us, length us, event | category | flops | bytes accessed | tf_op | source)
XLA Modules:
  0.0 65.2 jit_solution(1923120357308572841)
XLA Ops:
  0.6 0.0 copy-start
  0.6 1.6 %copy-done = bf16[1024,1024]{1,0:T(8,128)(2,1)S(1)} copy-done((bf16[1024,1024]{1,0:T(8,128)(2,1)S(1)}, bf16[1024,1024]{1,0:T(8,128)(2,1)}, u32[]{:S(2)}) %copy-start) | copy-done | bytes 2097176
  2.2 0.0 copy-start.2
  2.2 1.6 %copy-done.2 = bf16[1024,1024]{1,0:T(8,128)(2,1)S(1)} copy-done((bf16[1024,1024]{1,0:T(8,128)(2,1)S(1)}, bf16[1024,1024]{1,0:T(8,128)(2,1)}, u32[]{:S(2)}) %copy-start.2) | copy-done | bytes 2097176
  3.8 2.8 %states.1 = (f32[8,128,128]{2,1,0:T(8,128)}, bf16[8,4,128,128]{3,2,1,0:T(8,128)(2,1)S(1)}) custom-call(bf16[1024,1024]{1,0:T(8,128)(2,1)S(1)} %copy-done, bf16[1024,1024]{1,0:T(8,128)(2,1)S(1)} %copy-done.2), custom_call_target="tpu_custom_call" | custom-call | flops 268435456 | bytes 4194304 | tf_op jit(solution)/shard_map/states/pallas_call | solution.py:198
  6.6 0.0 copy-start.1
  6.6 0.5 collective-permute-start
  7.1 1.9 %collective-permute-done = f32[8,128,128]{2,1,0:T(8,128)} collective-permute-done((f32[8,128,128]{2,1,0:T(8,128)}, f32[8,128,128]{2,1,0:T(8,128)}, u32[]{:S(2)}, u32[]{:S(2)}) %collective-permute-start) | collective-permute-done | bytes 524320 | tf_op jit(solution)/shard_map/ppermute | solution.py:142
  8.9 1.3 %add.31 = f32[8,128,128]{2,1,0:T(8,128)S(1)} add(f32[8,128,128]{2,1,0:T(8,128)} %get-tuple-element.17, f32[8,128,128]{2,1,0:T(8,128)} %collective-permute-done) | non-fusion elementwise | flops 131072 | bytes 1572864 | tf_op jit(solution)/shard_map/add | solution.py:143
  10.2 3.0 %collective-permute-start.1 = (f32[4,128,128]{2,1,0:T(8,128)S(1)}, f32[4,128,128]{2,1,0:T(8,128)S(1)}, u32[]{:S(2)}, u32[]{:S(2)}) collective-permute-start(f32[4,128,128]{2,1,0:T(8,128)S(1)} %slice_select_fusion.1), channel_id=1, source_target_pairs={{0,8},{4,12},{8,0},{12,4},{1,9},{5,13},{9,1},{13,5},{2,10},{6,14},... | collective-permute-start | bytes 786440 | tf_op jit(solution)/shard_map/ppermute | solution.py:147
  13.2 6.6 %collective-permute-done.1 = f32[4,128,128]{2,1,0:T(8,128)S(1)} collective-permute-done((f32[4,128,128]{2,1,0:T(8,128)S(1)}, f32[4,128,128]{2,1,0:T(8,128)S(1)}, u32[]{:S(2)}, u32[]{:S(2)}) %collective-permute-start.1) | collective-permute-done | bytes 262176 | tf_op jit(solution)/shard_map/ppermute | solution.py:147
  19.8 0.0 collective-permute-start.2
  19.8 0.0 copy-done.1
  19.8 0.0 copy-start.3
  19.8 1.6 %copy-done.3 = bf16[1024,1024]{1,0:T(8,128)(2,1)S(1)} copy-done((bf16[1024,1024]{1,0:T(8,128)(2,1)S(1)}, bf16[1024,1024]{1,0:T(8,128)(2,1)}, u32[]{:S(2)}) %copy-start.3) | copy-done | bytes 2097176
  21.4 0.0 copy-start.5
  21.4 1.6 %copy-done.5 = bf16[1024,1024]{1,0:T(8,128)(2,1)S(1)} copy-done((bf16[1024,1024]{1,0:T(8,128)(2,1)S(1)}, bf16[1024,1024]{1,0:T(8,128)(2,1)}, u32[]{:S(2)}) %copy-start.5) | copy-done | bytes 2097176
  23.0 0.0 copy-start.8
  23.0 0.0 copy-start.7
  23.0 5.6 %inner.1.att_ref = f32[1024,1024]{1,0:T(8,128)S(1)} custom-call(bf16[1024,1024]{1,0:T(8,128)(2,1)S(1)} %copy-done.5, bf16[1024,1024]{1,0:T(8,128)(2,1)S(1)} %copy-done.1, bf16[1024,1024]{1,0:T(8,128)(2,1)S(1)} %copy-done.3, bf16[8,4,128,128]{3,2,1,0:T(8,128)(2,1)S(1)} %get-tuple-element.16.before_ref), custom_call_target="tpu_custom_call" | custom-call | flops 1342177280 | bytes 10485760 | tf_op jit(solution)/shard_map/inner/pallas_call | solution.py:206
  28.6 0.0 collective-permute-done.2
  28.6 0.0 copy-done.8
  28.6 1.2 %fusion.3.prefix_ref = bf16[8,128,128]{2,1,0:T(8,128)(2,1)S(1)} fusion(f32[8,128,128]{2,1,0:T(8,128)S(1)} %copy-done.8, f32[4,128,128]{2,1,0:T(8,128)} %collective-permute-done.2, f32[4,128,128]{2,1,0:T(8,128)S(1)} %collective-permute-done.1, f32[8,128,128]{2,1,0:T(8,128)} %collective-permute-done, pred[]{:T(512)S(6)} %eq.7, pred[]{:T(512)S(6)} %gt.2), kind=kLoop, calls=%fused_computation.4 | loop fusion | flops 1048576 | bytes 1835010 | tf_op jit(solution)/shard_map/convert_element_type | solution.py:215
  29.8 0.0 copy-done.7
  29.8 0.0 copy-start.6
  29.8 7.0 %norm.1 = (bf16[1024,1024]{1,0:T(8,128)(2,1)}, bf16[1024,1024]{1,0:T(8,128)(2,1)S(1)}, f32[8,128,128]{2,1,0:T(8,128)S(1)}, bf16[8,4,128,128]{3,2,1,0:T(8,128)(2,1)S(1)}) custom-call(f32[1024,1024]{1,0:T(8,128)S(1)} %inner.1.att_ref, bf16[1024,1024]{1,0:T(8,128)(2,1)S(1)} %copy-done.5, bf16[1024,1024]{1,0:T(8,128)(2,1)S(1)} %copy-done.7, ...), custom_call_target="tpu_custom_call" | custom-call | flops 536870912 | bytes 12582912 | tf_op jit(solution)/shard_map/norm/pallas_call | solution.py:216
  36.8 0.0 copy-start.4
  36.8 0.7 %collective-permute-start.3 = (f32[8,128,128]{2,1,0:T(8,128)S(1)}, f32[8,128,128]{2,1,0:T(8,128)S(1)}, u32[]{:S(2)}, u32[]{:S(2)}) collective-permute-start(f32[8,128,128]{2,1,0:T(8,128)S(1)} %get-tuple-element.22), channel_id=1, source_target_pairs={{0,4},{4,0},{8,12},{12,8},{1,5},{5,1},{9,13},{13,9},{2,6},{6,2},{1... | collective-permute-start | bytes 1572872 | tf_op jit(solution)/shard_map/ppermute | solution.py:142
  37.5 1.5 %collective-permute-done.3 = f32[8,128,128]{2,1,0:T(8,128)S(1)} collective-permute-done((f32[8,128,128]{2,1,0:T(8,128)S(1)}, f32[8,128,128]{2,1,0:T(8,128)S(1)}, u32[]{:S(2)}, u32[]{:S(2)}) %collective-permute-start.3) | collective-permute-done | bytes 524320 | tf_op jit(solution)/shard_map/ppermute | solution.py:142
  39.0 0.1 add.34
  39.1 1.8 %collective-permute-start.4 = (f32[4,128,128]{2,1,0:T(8,128)S(1)}, f32[4,128,128]{2,1,0:T(8,128)S(1)}, u32[]{:S(2)}, u32[]{:S(2)}) collective-permute-start(f32[4,128,128]{2,1,0:T(8,128)S(1)} %slice_select_fusion), channel_id=1, source_target_pairs={{0,8},{4,12},{8,0},{12,4},{1,9},{5,13},{9,1},{13,5},{2,10},{6,14},... | collective-permute-start | bytes 786440 | tf_op jit(solution)/shard_map/ppermute | solution.py:147
  41.0 6.8 %collective-permute-done.4 = f32[4,128,128]{2,1,0:T(8,128)S(1)} collective-permute-done((f32[4,128,128]{2,1,0:T(8,128)S(1)}, f32[4,128,128]{2,1,0:T(8,128)S(1)}, u32[]{:S(2)}, u32[]{:S(2)}) %collective-permute-start.4) | collective-permute-done | bytes 262176 | tf_op jit(solution)/shard_map/ppermute | solution.py:147
  47.8 0.0 collective-permute-start.5
  47.8 0.0 copy-done.6
  47.8 0.0 copy-done.4
  47.8 12.2 %back.1 = (bf16[1024,1024]{1,0:T(8,128)(2,1)}, f32[1024,1024]{1,0:T(8,128)S(1)}, f32[1024,1024]{1,0:T(8,128)S(1)}) custom-call(bf16[1024,1024]{1,0:T(8,128)(2,1)S(1)} %copy-done.6, bf16[1024,1024]{1,0:T(8,128)(2,1)S(1)} %copy-done.1, bf16[1024,1024]{1,0:T(8,128)(2,1)S(1)} %copy-done.4, bf16[1024,1024]{1,0:T(8,128)(2,1)S(1)} %get-tuple-element.19.ga_ref, ...), custom_call_target="tpu_custom_call" | custom-call | flops 3489660928 | bytes 18874368 | tf_op jit(solution)/shard_map/back/pallas_call | solution.py:227
  60.0 0.0 collective-permute-done.5
  60.0 1.0 %add_add_fusion = (f32[8,128,128]{2,1,0:T(8,128)}, bf16[8,128,128]{2,1,0:T(8,128)(2,1)S(1)}) fusion(f32[8,128,128]{2,1,0:T(8,128)S(1)} %get-tuple-element.22, f32[8,128,128]{2,1,0:T(8,128)S(1)} %collective-permute-done.3, f32[4,128,128]{2,1,0:T(8,128)S(1)} %collective-permute-done.4, f32[4,128,128]{2,1,0:T(8,128)S(1)} %collective-permute-done.5, pred[]{:T(512)S(6)} %eq.7, ...), kind=kLoop, calls=%fused_computation.6 | loop fusion | flops 1572864 | bytes 2359298 | tf_op jit(solution)/shard_map/add | solution.py:225
  61.0 4.2 %last.1 = (bf16[1024,1024]{1,0:T(8,128)(2,1)}, bf16[1024,1024]{1,0:T(8,128)(2,1)}) custom-call(bf16[1024,1024]{1,0:T(8,128)(2,1)S(1)} %copy-done.1, bf16[1024,1024]{1,0:T(8,128)(2,1)S(1)} %copy-done.4, bf16[8,128,128]{2,1,0:T(8,128)(2,1)S(1)} %get-tuple-element.28.suffix_ref, f32[1024,1024]{1,0:T(8,128)S(1)} %get-tuple-element.23.kp_ref, ...), custom_call_target="tpu_custom_call" | custom-call | flops 536870912 | bytes 16777216 | tf_op jit(solution)/shard_map/last/pallas_call | solution.py:236
  (2 shorter events, 0.1 us)
Async XLA Ops:
  0.6 1.6 %copy-start = (bf16[1024,1024]{1,0:T(8,128)(2,1)S(1)}, bf16[1024,1024]{1,0:T(8,128)(2,1)}, u32[]{:S(2)}) copy-start(bf16[1024,1024]{1,0:T(8,128)(2,1)} %k_ref.7) | copy-start | bytes 6291460
  2.2 1.6 %copy-start.2 = (bf16[1024,1024]{1,0:T(8,128)(2,1)S(1)}, bf16[1024,1024]{1,0:T(8,128)(2,1)}, u32[]{:S(2)}) copy-start(bf16[1024,1024]{1,0:T(8,128)(2,1)} %v_ref.7) | copy-start | bytes 6291460
  6.6 13.2 %copy-start.1 = (bf16[1024,1024]{1,0:T(8,128)(2,1)S(1)}, bf16[1024,1024]{1,0:T(8,128)(2,1)}, u32[]{:S(2)}) copy-start(bf16[1024,1024]{1,0:T(8,128)(2,1)} %k_ref.7) | copy-start | bytes 6291460
  6.6 2.3 %collective-permute-start = (f32[8,128,128]{2,1,0:T(8,128)}, f32[8,128,128]{2,1,0:T(8,128)}, u32[]{:S(2)}, u32[]{:S(2)}) collective-permute-start(f32[8,128,128]{2,1,0:T(8,128)} %get-tuple-element.17), channel_id=1, source_target_pairs={{0,4},{4,0},{8,12},{12,8},{1,5},{5,1},{9,13},{13,9},{2,6},{6,2},{1... | collective-permute-start | bytes 1572872 | tf_op jit(solution)/shard_map/ppermute | solution.py:142
  10.2 9.6 %collective-permute-start.1 = (f32[4,128,128]{2,1,0:T(8,128)S(1)}, f32[4,128,128]{2,1,0:T(8,128)S(1)}, u32[]{:S(2)}, u32[]{:S(2)}) collective-permute-start(f32[4,128,128]{2,1,0:T(8,128)S(1)} %slice_select_fusion.1), channel_id=1, source_target_pairs={{0,8},{4,12},{8,0},{12,4},{1,9},{5,13},{9,1},{13,5},{2,10},{6,14},... | collective-permute-start | bytes 786440 | tf_op jit(solution)/shard_map/ppermute | solution.py:147
  19.8 8.8 %collective-permute-start.2 = (f32[4,128,128]{2,1,0:T(8,128)S(1)}, f32[4,128,128]{2,1,0:T(8,128)}, u32[]{:S(2)}, u32[]{:S(2)}) collective-permute-start(f32[4,128,128]{2,1,0:T(8,128)S(1)} %collective-permute-done.1), channel_id=1, source_target_pairs={{0,4},{4,0},{8,12},{12,8},{1,5},{5,1},{9,13},{13,9},{2,6},{6,2},{1... | collective-permute-start | bytes 786440 | tf_op jit(solution)/shard_map/ppermute | solution.py:151
  19.8 1.6 %copy-start.3 = (bf16[1024,1024]{1,0:T(8,128)(2,1)S(1)}, bf16[1024,1024]{1,0:T(8,128)(2,1)}, u32[]{:S(2)}) copy-start(bf16[1024,1024]{1,0:T(8,128)(2,1)} %v_ref.7) | copy-start | bytes 6291460
  21.4 1.6 %copy-start.5 = (bf16[1024,1024]{1,0:T(8,128)(2,1)S(1)}, bf16[1024,1024]{1,0:T(8,128)(2,1)}, u32[]{:S(2)}) copy-start(bf16[1024,1024]{1,0:T(8,128)(2,1)} %q_ref.5) | copy-start | bytes 6291460
  23.0 5.6 %copy-start.8 = (f32[8,128,128]{2,1,0:T(8,128)S(1)}, f32[8,128,128]{2,1,0:T(8,128)}, u32[]{:S(2)}) copy-start(f32[8,128,128]{2,1,0:T(8,128)} %param.8) | copy-start | bytes 1572868
  23.0 6.8 %copy-start.7 = (bf16[1024,1024]{1,0:T(8,128)(2,1)S(1)}, bf16[1024,1024]{1,0:T(8,128)(2,1)}, u32[]{:S(2)}) copy-start(bf16[1024,1024]{1,0:T(8,128)(2,1)} %g_ref.1) | copy-start | bytes 6291460
  29.8 18.0 %copy-start.6 = (bf16[1024,1024]{1,0:T(8,128)(2,1)S(1)}, bf16[1024,1024]{1,0:T(8,128)(2,1)}, u32[]{:S(2)}) copy-start(bf16[1024,1024]{1,0:T(8,128)(2,1)} %q_ref.5) | copy-start | bytes 6291460
  36.8 11.0 %copy-start.4 = (bf16[1024,1024]{1,0:T(8,128)(2,1)S(1)}, bf16[1024,1024]{1,0:T(8,128)(2,1)}, u32[]{:S(2)}) copy-start(bf16[1024,1024]{1,0:T(8,128)(2,1)} %v_ref.7) | copy-start | bytes 6291460
  36.8 2.2 %collective-permute-start.3 = (f32[8,128,128]{2,1,0:T(8,128)S(1)}, f32[8,128,128]{2,1,0:T(8,128)S(1)}, u32[]{:S(2)}, u32[]{:S(2)}) collective-permute-start(f32[8,128,128]{2,1,0:T(8,128)S(1)} %get-tuple-element.22), channel_id=1, source_target_pairs={{0,4},{4,0},{8,12},{12,8},{1,5},{5,1},{9,13},{13,9},{2,6},{6,2},{1... | collective-permute-start | bytes 1572872 | tf_op jit(solution)/shard_map/ppermute | solution.py:142
  39.1 8.7 %collective-permute-start.4 = (f32[4,128,128]{2,1,0:T(8,128)S(1)}, f32[4,128,128]{2,1,0:T(8,128)S(1)}, u32[]{:S(2)}, u32[]{:S(2)}) collective-permute-start(f32[4,128,128]{2,1,0:T(8,128)S(1)} %slice_select_fusion), channel_id=1, source_target_pairs={{0,8},{4,12},{8,0},{12,4},{1,9},{5,13},{9,1},{13,5},{2,10},{6,14},... | collective-permute-start | bytes 786440 | tf_op jit(solution)/shard_map/ppermute | solution.py:147
  47.8 12.3 %collective-permute-start.5 = (f32[4,128,128]{2,1,0:T(8,128)S(1)}, f32[4,128,128]{2,1,0:T(8,128)S(1)}, u32[]{:S(2)}, u32[]{:S(2)}) collective-permute-start(f32[4,128,128]{2,1,0:T(8,128)S(1)} %collective-permute-done.4), channel_id=1, source_target_pairs={{0,4},{4,0},{8,12},{12,8},{1,5},{5,1},{9,13},{13,9},{2,6},{6,2},{1... | collective-permute-start | bytes 786440 | tf_op jit(solution)/shard_map/ppermute | solution.py:151

commit v2 on v0

v2 whole, which is shorter than its diff:
```python
import functools

import jax
import jax.numpy as jnp
from jax import lax
from jax.experimental import pallas as pl
from jax.experimental.pallas import tpu as pltpu
from jax.sharding import PartitionSpec as P

F32 = jnp.float32
BF16 = jnp.bfloat16
EPS = 1e-06
VM = pl.BlockSpec(memory_space=pltpu.VMEM)
HB = pl.BlockSpec(memory_space=pltpu.HBM)


def mm(a, b):
    return lax.dot_general(a, b, (((1,), (0,)), ((), ())), preferred_element_type=F32)


def mm_rt(a, b):
    return lax.dot_general(a, b, (((1,), (1,)), ((), ())), preferred_element_type=F32)


def mm_lt(a, b):
    return lax.dot_general(a, b, (((0,), (0,)), ((), ())), preferred_element_type=F32)


def causal(size):
    return lax.broadcasted_iota(jnp.int32, (size, size), 0) >= lax.broadcasted_iota(
        jnp.int32, (size, size), 1
    )


class Cut:
    def __init__(self, rows, heads, dim, group, groups):
        self.rows, self.heads, self.dim = rows, heads, dim
        self.per = heads // groups
        self.base = group * self.per
        self.size = 256 if rows % 256 == 0 else rows
        self.chunks = rows // self.size

    def rng(self, c):
        return slice(c * self.size, (c + 1) * self.size)

    def cols(self, h):
        return slice(h * self.dim, (h + 1) * self.dim)

    def whole(self, h):
        return self.cols(self.base + h)

    def each(self):
        return [(h, c) for h in range(self.per) for c in range(self.chunks)]

    def span(self):
        return pl.ds(self.base * self.dim, self.per * self.dim)


def state_kernel(cut, k_hbm, v_hbm, q_hbm, total_ref, before_ref, k_ref, v_ref, q_ref, sems, q_sem):
    width = 2 * cut.dim
    pieces = k_ref.shape[1] // width

    def copy(i, j):
        src, dst = ((k_hbm, k_ref), (v_hbm, v_ref))[j]
        at = pl.ds(i * width, width)
        return pltpu.make_async_copy(src.at[:, at], dst.at[:, at], sems.at[j, i])

    for i in range(pieces):
        copy(i, 0).start()
        copy(i, 1).start()
    last = pltpu.make_async_copy(q_hbm, q_ref, q_sem)
    last.start()
    for h in range(cut.per):
        if h % 2 == 0:
            copy(h // 2, 0).wait()
            copy(h // 2, 1).wait()
        terms = [
            mm_lt(k_ref[cut.rng(c), cut.whole(h)], v_ref[cut.rng(c), cut.whole(h)])
            for c in range(cut.chunks)
        ]
        run = jnp.zeros((cut.dim, cut.dim), F32)
        for c in range(cut.chunks):
            before_ref[h, c] = run
            run = run + terms[c]
        total_ref[h] = run
    last.wait()


def inner_kernel(
    cut, q_ref, k_ref, v_ref, before_ref, side_hbm, att_ref, scores_ref, side_ref, side_sem
):
    side = pltpu.make_async_copy(side_hbm, side_ref, side_sem)
    side.start()
    keep = causal(cut.size)
    each = cut.each()
    q = {j: q_ref[cut.rng(j[1]), cut.whole(j[0])] for j in each}
    k = {j: k_ref[cut.rng(j[1]), cut.whole(j[0])] for j in each}
    v = {j: v_ref[cut.rng(j[1]), cut.whole(j[0])] for j in each}
    scores = {j: jnp.where(keep, mm_rt(q[j], k[j]), 0.0).astype(BF16) for j in each}
    att = {j: mm(scores[j], v[j]) for j in each}
    for h, c in each:
        if c > 0:
            before = before_ref[cut.base + h, c].astype(BF16)
            att[h, c] = att[h, c] + mm(q[h, c], before)
    for h, c in each:
        scores_ref[h, c] = scores[h, c]
        att_ref[cut.rng(c), cut.cols(h)] = att[h, c]
    side.wait()


def far_of(per, h, own_half, other_half):
    half = per // 2
    first = lax.rem(lax.axis_index("ctx"), 2) == 0
    mine, other = own_half[h % half], other_half[h % half]
    return jnp.where(first == (h < half), mine, other)


def norm_kernel(cut, masked, *refs):
    att_ref, q_ref, g_ref, init_ref, near_ref, far_ref, other_ref = refs[:7]
    out_hbm, ga_ref, total_ref, after_ref, prefix_ref, out_ref, sems = refs[-7:]
    place = lax.axis_index("ctx")
    add_near = lax.rem(place, 2) == 1
    add_far = place >= 2
    copies = []
    for h in range(cut.per):
        full = far_of(cut.per, h, far_ref, other_ref)
        if not masked:
            full = jnp.where(add_far, full, 0.0)
        prefix_ref[h] = init_ref[cut.base + h] + (full + jnp.where(add_near, near_ref[cut.base + h], 0.0))
    ga = {}
    for h, c in cut.each():
        q = q_ref[cut.rng(c), cut.whole(h)]
        att = att_ref[cut.rng(c), cut.cols(h)] + mm(q, prefix_ref[h].astype(BF16))
        up = g_ref[cut.rng(c), cut.whole(h)].astype(F32)
        square = jnp.sum(att * att, axis=-1, keepdims=True)
        along = jnp.sum(up * att, axis=-1, keepdims=True)
        inv = lax.rsqrt(square * (1.0 / cut.dim) + EPS)
        normed = att * inv
        ga[h, c] = (inv * (up - normed * (along * (inv * (1.0 / cut.dim))))).astype(BF16)
        out_ref[cut.rng(c), cut.cols(h)] = normed.astype(BF16)
        ga_ref[cut.rng(c), cut.cols(h)] = ga[h, c]
        if h % 2 == 1 and c == cut.chunks - 1:
            i = h // 2
            copies.append(
                pltpu.make_async_copy(
                    out_ref.at[:, pl.ds(2 * i * cut.dim, 2 * cut.dim)],
                    out_hbm.at[:, pl.ds((cut.base + 2 * i) * cut.dim, 2 * cut.dim)],
                    sems.at[i],
                )
            )
            copies[-1].start()
    terms = {(h, c): mm_lt(q_ref[cut.rng(c), cut.whole(h)], ga[h, c]) for h, c in cut.each()}
    for h in range(cut.per):
        run = jnp.zeros((cut.dim, cut.dim), F32)
        for c in reversed(range(cut.chunks)):
            after_ref[h, c] = run
            run = run + terms[h, c]
        total_ref[h] = run
    for copy in copies:
        copy.wait()


def back_kernel(cut, *refs):
    q_ref, k_ref, v_ref, ga_ref, prefix_ref, before_ref, scores_ref = refs[:7]
    qg_hbm, kg_ref, vg_ref, qg_ref, sems = refs[-5:]
    keep = causal(cut.size)
    each = cut.each()
    q = {j: q_ref[cut.rng(j[1]), cut.whole(j[0])] for j in each}
    k = {j: k_ref[cut.rng(j[1]), cut.whole(j[0])] for j in each}
    v = {j: v_ref[cut.rng(j[1]), cut.whole(j[0])] for j in each}
    ga = {j: ga_ref[cut.rng(j[1]), cut.cols(j[0])] for j in each}
    state = {(h, c): (prefix_ref[h] + before_ref[cut.base + h, c]).astype(BF16) for h, c in each}
    scores = {j: scores_ref[j[0], j[1]] for j in each}
    grad = {j: jnp.where(keep, mm_rt(ga[j], v[j]), 0.0).astype(BF16) for j in each}
    qg = {j: mm(grad[j], k[j]) + mm_rt(ga[j], state[j]) for j in each}
    for h, c in each:
        qg_ref[cut.rng(c), cut.cols(h)] = qg[h, c].astype(BF16)
    copies = []
    for i in range(cut.per // 2):
        copies.append(
            pltpu.make_async_copy(
                qg_ref.at[:, pl.ds(2 * i * cut.dim, 2 * cut.dim)],
                qg_hbm.at[:, pl.ds((cut.base + 2 * i) * cut.dim, 2 * cut.dim)],
                sems.at[i],
            )
        )
        copies[-1].start()
    vg = {j: mm_lt(scores[j], ga[j]) for j in each}
    kg = {j: mm_lt(grad[j], q[j]) for j in each}
    for h, c in each:
        kg_ref[cut.rng(c), cut.cols(h)] = kg[h, c]
        vg_ref[cut.rng(c), cut.cols(h)] = vg[h, c]
    for copy in copies:
        copy.wait()


def last_kernel(cut, masked, *refs):
    k_ref, v_ref, kp_ref, vp_ref, after_ref, own_ref, near_ref = refs[:7]
    far_ref, other_ref, all_ref, all_other_ref = refs[7:11]
    kg_hbm, vg_hbm, sg_hbm, kg_ref, vg_ref, sg_ref, sems, sg_sem = refs[-8:]
    place = lax.axis_index("ctx")
    add_near = lax.rem(place, 2) == 0
    add_far = place < 2
    copies = []
    for h in range(cut.per):
        near = near_ref[h]
        full = far_of(cut.per, h, far_ref, other_ref)
        every = far_of(cut.per, h, all_ref, all_other_ref)
        sg_ref[h] = every + (own_ref[h] + near)
        if not masked:
            full = jnp.where(add_far, full, 0.0)
        suffix = full + jnp.where(add_near, near, 0.0)
        cols, whole = cut.cols(h), cut.whole(h)
        for c in range(cut.chunks):
            rows = cut.rng(c)
            state = (suffix + after_ref[h, c]).astype(BF16)
            kg_ref[rows, cols] = (kp_ref[rows, cols] + mm_rt(v_ref[rows, whole], state)).astype(BF16)
            vg_ref[rows, cols] = (vp_ref[rows, cols] + mm(k_ref[rows, whole], state)).astype(BF16)
        if h % 2 == 1:
            i = h // 2
            for j, (src, dst) in enumerate(((kg_ref, kg_hbm), (vg_ref, vg_hbm))):
                copies.append(
                    pltpu.make_async_copy(
                        src.at[:, pl.ds(2 * i * cut.dim, 2 * cut.dim)],
                        dst.at[:, pl.ds((cut.base + 2 * i) * cut.dim, 2 * cut.dim)],
                        sems.at[j, i],
                    )
                )
                copies[-1].start()
    copies.append(
        pltpu.make_async_copy(sg_ref, sg_hbm.at[pl.ds(cut.base, cut.per)], sg_sem)
    )
    copies[-1].start()
    for copy in copies:
        copy.wait()


def half_kernel(per, own_ref, near_ref, *mine_refs):
    half = per // 2
    first = lax.rem(lax.axis_index("ctx"), 2) == 0
    for g, mine_ref in enumerate(mine_refs):
        for h in range(half):
            low, high = g * per + h, g * per + half + h
            mine_ref[h] = jnp.where(
                first, own_ref[low] + near_ref[low], own_ref[high] + near_ref[high]
            )


def shards(n, groups, queries, keys, values, init_state, out_grad):
    rows, width = queries.shape
    heads, dim = init_state.shape[:2]
    pairs = n // 2
    swap_pairs = [(i, i ^ 1) for i in range(n)]
    shift_pairs = [(i, (i + 2) % n) for i in range(n)]
    swap = lambda x: lax.ppermute(x, "ctx", swap_pairs)
    shift = lambda x: lax.ppermute(x, "ctx", shift_pairs)
    cuts = [Cut(rows, heads, dim, g, groups) for g in range(groups)]
    per, chunks, size = cuts[0].per, cuts[0].chunks, cuts[0].size
    wide_b = jax.ShapeDtypeStruct((rows, width), BF16)
    all_b = pltpu.VMEM((rows, width), BF16)
    part_b = pltpu.VMEM((rows, per * dim), BF16)
    part_f = pltpu.VMEM((rows, per * dim), F32)
    state_f = pltpu.VMEM((per, dim, dim), F32)
    states_f = pltpu.VMEM((per, chunks, dim, dim), F32)
    scores_b = pltpu.VMEM((per, chunks, size, size), BF16)
    small = 2 * per * rows * dim * dim
    square = 2 * per * rows * size * dim
    piece = rows * per * dim * 2
    dma = pltpu.SemaphoreType.DMA

    def call(body, name, ins, outs, scratch, flops, nbytes, kept=()):
        ins = list(ins)
        aliases = {len(ins) + i: i for i in range(len(kept))}
        specs = [VM] * len(ins) + [HB] * len(kept)
        out_specs = [VM if isinstance(o, type(all_b)) else HB for o in outs]
        return pl.pallas_call(
            body,
            in_specs=specs,
            out_specs=out_specs,
            out_shape=list(outs),
            scratch_shapes=scratch,
            input_output_aliases=aliases,
            compiler_params=pltpu.CompilerParams(vmem_limit_bytes=16 * 1024 * 1024),
            cost_estimate=pl.CostEstimate(flops=flops, bytes_accessed=nbytes, transcendentals=0),
            name=name,
        )(*ins, *kept)

    def far_sums(mine, later):
        if pairs == 2:
            far = shift(mine)
            return far, far
        pair = lax.axis_index("ctx") // 2
        moving = mine
        used, every = jnp.zeros_like(mine), jnp.zeros_like(mine)
        for j in range(1, pairs):
            moving = shift(moving)
            wrapped = pair < j
            used = used + jnp.where(wrapped == later, moving, 0.0)
            every = every + moving
        return used, every

    def halves(own, near, count):
        return pl.pallas_call(
            functools.partial(half_kernel, per),
            in_specs=[VM] * 2,
            out_specs=[VM] * count,
            out_shape=[pltpu.VMEM((per // 2, dim, dim), F32)] * count,
            compiler_params=pltpu.CompilerParams(vmem_limit_bytes=4 * 1024 * 1024),
            name="half",
        )(own, near)

    masked = pairs != 2

    def call_inner(g, side):
        return pl.pallas_call(
            functools.partial(inner_kernel, cuts[g]),
            in_specs=[VM] * 4 + [HB],
            out_specs=[VM] * 3,
            out_shape=[part_f, scores_b, pltpu.VMEM(side.shape, side.dtype)],
            scratch_shapes=[dma],
            compiler_params=pltpu.CompilerParams(vmem_limit_bytes=16 * 1024 * 1024),
            cost_estimate=pl.CostEstimate(
                flops=2 * square + small, bytes_accessed=piece, transcendentals=0
            ),
            name="inner%d" % g,
        )(queries_v, keys_v, values_v, before, in_hbm(side))

    in_hbm = lambda x: pltpu.with_memory_space_constraint(x, pltpu.HBM)
    every = Cut(rows, heads, dim, 0, 1)
    own, before, keys_v, values_v, queries_v = pl.pallas_call(
        functools.partial(state_kernel, every),
        in_specs=[HB] * 3,
        out_specs=[VM] * 5,
        out_shape=[
            pltpu.VMEM((heads, dim, dim), F32),
            pltpu.VMEM((heads, chunks, dim, dim), F32),
            all_b,
            all_b,
            all_b,
        ],
        scratch_shapes=[dma((2, heads // 2)), dma],
        compiler_params=pltpu.CompilerParams(vmem_limit_bytes=16 * 1024 * 1024),
        cost_estimate=pl.CostEstimate(
            flops=2 * small, bytes_accessed=6 * piece, transcendentals=0
        ),
        name="states",
    )(in_hbm(keys), in_hbm(values), in_hbm(queries))
    att, scores, far, other = {}, {}, {}, {}
    near = swap(own)
    att[0], scores[0], out_grad_v = call_inner(0, out_grad)
    near, att[0] = lax.optimization_barrier((near, att[0]))
    mine = halves(own, near, groups)
    for g in range(groups):
        far[g], _ = far_sums(mine[g], False)
    att[1], scores[1], init_v = call_inner(1, init_state)
    far[0], att[1] = lax.optimization_barrier((far[0], att[1]))
    for g in range(groups):
        other[g] = swap(far[g])
    ga, total, after, prefix = {}, {}, {}, {}
    output = ()
    gnear, gfar, gall = {}, {}, {}
    for g, cut in enumerate(cuts):
        out, ga[g], total[g], after[g], prefix[g] = call(
            functools.partial(norm_kernel, cut, masked),
            "norm%d" % g,
            [att[g], queries_v, out_grad_v, init_v, near, far[g], other[g]],
            [wide_b, part_b, state_f, states_f, state_f],
            [pltpu.VMEM((rows, per * dim), BF16), dma((per // 2,))],
            2 * small,
            piece,
            output,
        )
        output = (out,)
        gnear[g] = swap(total[g])
    gnear[0], total[1] = lax.optimization_barrier((gnear[0], total[1]))
    for g, cut in enumerate(cuts):
        gfar[g], gall[g] = far_sums(halves(total[g], gnear[g], 1)[0], True)
    kp, vp = {}, {}
    query_grad = ()
    for g, cut in enumerate(cuts):
        out, kp[g], vp[g] = call(
            functools.partial(back_kernel, cut),
            "back%d" % g,
            [queries_v, keys_v, values_v, ga[g], prefix[g], before, scores[g]],
            [wide_b, part_f, part_f],
            [pltpu.VMEM((rows, per * dim), BF16), dma((per // 2,))],
            4 * square + small,
            piece,
            query_grad,
        )
        query_grad = (out,)
        gfar[g], gall[g], kp[g] = lax.optimization_barrier((gfar[g], gall[g], kp[g]))
    ends = ()
    for g, cut in enumerate(cuts):
        used = swap(gfar[g])
        total_far = used if pairs == 2 else swap(gall[g])
        ends = call(
            functools.partial(last_kernel, cut, masked),
            "last%d" % g,
            [
                keys_v, values_v, kp[g], vp[g], after[g], total[g], gnear[g],
                gfar[g], used, gall[g], total_far,
            ],
            [wide_b, wide_b, jax.ShapeDtypeStruct(init_state.shape, F32)],
            [
                pltpu.VMEM((rows, per * dim), BF16),
                pltpu.VMEM((rows, per * dim), BF16),
                pltpu.VMEM((per, dim, dim), F32),
                dma((2, per // 2)),
                dma,
            ],
            2 * small,
            2 * piece,
            ends,
        )
    key_grad, value_grad, state_grad = ends
    return output[0], query_grad[0], key_grad, value_grad, state_grad


def solution(mesh):
    wide = P(("grp", "ctx"), "head")
    deep = P(("grp", "head"), None, None)
    return jax.shard_map(
        functools.partial(shards, mesh.shape["ctx"], 2),
        mesh=mesh,
        in_specs=(wide, wide, wide, deep, wide),
        out_specs=(wide, wide, wide, wide, deep),
        check_vma=False,
    )
```

time: 148 us -> 35.8 us (0.24)
  matrix products: 79.7 us -> 0 us
  local copies, waits for them, and re-layouts: 31.8 us -> 0 us
  Pallas kernels: 0 us -> 21.6 us
  between operations: 14.1 us -> 0.92 us
  other arithmetic: 11.3 us -> 0 us
  starting transfers between devices: 0.08 us -> 8.03 us
  waiting for transfers between devices: 10.7 us -> 5.1 us
    dot_general x12 -> x0, matrix products: 79.7 us -> none  [the longest x1 11.8 us: shards(): jnp.einsum('hts,shd->thd', grad_scores, k_loc, preferred_element_type=jnp...]
    unnamed x25 -> x0, local copies, waits for them, and re-layouts: 22.6 us -> none
    pallas_call x0 -> x12, Pallas kernels: none -> 21.6 us  [the longest x6 15.3 us: call(): pl.pallas_call(body, in_specs=specs, out_specs=out_specs, out_shape=list(...]
    all_gather x2 -> x0, waiting for transfers between devices: 10.7 us -> none  [the longest x1 10.7 us: shards(): every_state = lax.all_gather(block_state[None], 'ctx', axis=0, tiled=True)]
    reduce_sum x3 -> x0, other arithmetic: 8.24 us -> none  [the longest x1 3.45 us: shards(): jnp.mean(upstream * normed, axis=-1, keepdims=True)]
    ppermute x0 -> x11, starting transfers between devices: none -> 8.03 us  [the longest x4 6.2 us: shards(): shift = lambda x: lax.ppermute(x, 'ctx', shift_pairs)]
    ppermute x0 -> x11, waiting for transfers between devices: none -> 5.1 us  [the longest x4 5.08 us: shards(): shift = lambda x: lax.ppermute(x, 'ctx', shift_pairs)]
    convert_element_type x1 -> x0, local copies, waits for them, and re-layouts: 4.13 us -> none  [shards(): upstream = out_grad.reshape(rows, heads, dim).astype(jnp.float32)]
  transfers between devices with their start and end apart: 2 -> 11, of which waited for: 1 -> 2; matrix products, arithmetic and copies ran while one was open for 31% -> 0% of each run, Pallas kernels for 0% -> 47%
where the time goes in v2:
time: 35.8 us; the launch traced here: 35.6 us
  Pallas kernels  21.6 us (60%)
  starting transfers between devices  8.03 us (22%)
  waiting for transfers between devices  5.1 us (14%)
  between operations  0.92 us (3%)
    pallas_call x6, Pallas kernels, call(): pl.pallas_call(body, in_specs=specs, out_specs=out_specs, out_shape=list(...  15.3 us
    ppermute x4, starting transfers between devices, shards(): shift = lambda x: lax.ppermute(x, 'ctx', shift_pairs)  6.2 us
    ppermute x4, waiting for transfers between devices, shards(): shift = lambda x: lax.ppermute(x, 'ctx', shift_pairs)  5.08 us
    pallas_call x2, Pallas kernels, call_inner(): pl.pallas_call(functools.partial(inner_kernel, cuts[g]), in_specs=[VM] *...  3.13 us
    pallas_call x1, Pallas kernels, shards(): pl.pallas_call(functools.partial(state_kernel, every), in_specs=[HB] * 3,...  3.03 us
    ppermute x7, starting transfers between devices, shards(): swap = lambda x: lax.ppermute(x, 'ctx', swap_pairs)  1.82 us
  transfers between devices with their start and end apart: 11, of which 2 were waited for; matrix products, arithmetic and copies ran while one was open for 0% of the time, Pallas kernels for 47%

profile of v2, /device:TPU:0, one launch (start us, length us, event | category | flops | bytes accessed | tf_op | source)
XLA Modules:
  0.0 35.6 jit_solution(1037682165353593275)
XLA Ops:
  0.6 3.0 %states.1 = (f32[8,128,128]{2,1,0:T(8,128)S(1)}, f32[8,4,128,128]{3,2,1,0:T(8,128)S(1)}, bf16[1024,1024]{1,0:T(8,128)(2,1)S(1)}, bf16[1024,1024]{1,0:T(8,128)(2,1)S(1)}, bf16[1024,1024]{1,0:T(8,128)(2,1)S(1)}) custom-call(bf16[1024,1024]{1,0:T(8,128)(2,1)} %k_hbm.1, bf16[1024,1024]{1,0:T(8,128)(2,1)} %v_hbm.1, bf16[1024,1024]{1,0:T(8,128)(2,1)} %q_hbm.1), custom_call_target="tpu_custom_call" | custom-call | flops 268435456 | bytes 6291456 | tf_op jit(solution)/shard_map/states/pallas_call | solution.py:330
  3.7 0.5 %collective-permute-start = (f32[8,128,128]{2,1,0:T(8,128)S(1)}, f32[8,128,128]{2,1,0:T(8,128)S(1)}, u32[]{:S(2)}, u32[]{:S(2)}) collective-permute-start(f32[8,128,128]{2,1,0:T(8,128)S(1)} %get-tuple-element.52.own_ref), channel_id=1, source_target_pairs={{0,4},{4,0},{8,12},{12,8},{1,5},{5,1},{9,13},{13,9},{2,6},{6,2},{1... | collective-permute-start | bytes 1572872 | tf_op jit(solution)/shard_map/ppermute | solution.py:255
  4.2 1.6 %inner0.1 = (f32[1024,512]{1,0:T(8,128)S(1)}, bf16[4,4,256,256]{3,2,1,0:T(8,128)(2,1)S(1)}, bf16[1024,1024]{1,0:T(8,128)(2,1)S(1)}) custom-call(bf16[1024,1024]{1,0:T(8,128)(2,1)S(1)} %get-tuple-element.53.q_ref.refs_1_.refs_0_, bf16[1024,1024]{1,0:T(8,128)(2,1)S(1)} %get-tuple-element.54.k_ref.refs_1_.refs_0_, ...), custom_call_target="tpu_custom_call" | custom-call | flops 671088640 | bytes 1048576 | tf_op jit(solution)/shard_map/inner0/pallas_call | solution.py:315
  5.8 0.0 collective-permute-done.near_ref.refs_4_
  5.8 0.1 half.3
  5.9 2.9 %collective-permute-start.1 = (f32[2,128,128]{2,1,0:T(8,128)S(1)}, f32[2,128,128]{2,1,0:T(8,128)S(1)}, u32[]{:S(2)}, u32[]{:S(2)}) collective-permute-start(f32[2,128,128]{2,1,0:T(8,128)S(1)} %get-tuple-element.59), channel_id=1, source_target_pairs={{0,8},{4,12},{8,0},{12,4},{1,9},{5,13},{9,1},{13,5},{2,10},{6,14},... | collective-permute-start | bytes 393224 | tf_op jit(solution)/shard_map/ppermute | solution.py:256
  8.7 0.1 collective-permute-start.2
  8.8 1.5 %inner1.1 = (f32[1024,512]{1,0:T(8,128)S(1)}, bf16[4,4,256,256]{3,2,1,0:T(8,128)(2,1)S(1)}, f32[8,128,128]{2,1,0:T(8,128)S(1)}) custom-call(bf16[1024,1024]{1,0:T(8,128)(2,1)S(1)} %get-tuple-element.53.q_ref.refs_1_.refs_0_, bf16[1024,1024]{1,0:T(8,128)(2,1)S(1)} %get-tuple-element.54.k_ref.refs_1_.refs_0_, ...), custom_call_target="tpu_custom_call" | custom-call | flops 671088640 | bytes 1048576 | tf_op jit(solution)/shard_map/inner1/pallas_call | solution.py:315
  10.3 2.7 %collective-permute-done.1.refs_5_ = f32[2,128,128]{2,1,0:T(8,128)S(1)} collective-permute-done((f32[2,128,128]{2,1,0:T(8,128)S(1)}, f32[2,128,128]{2,1,0:T(8,128)S(1)}, u32[]{:S(2)}, u32[]{:S(2)}) %collective-permute-start.1) | collective-permute-done | bytes 131104 | tf_op jit(solution)/shard_map/ppermute | solution.py:256
  13.0 0.0 collective-permute-start.4
  13.0 2.4 %collective-permute-done.2.refs_5_ = f32[2,128,128]{2,1,0:T(8,128)S(1)} collective-permute-done((f32[2,128,128]{2,1,0:T(8,128)S(1)}, f32[2,128,128]{2,1,0:T(8,128)S(1)}, u32[]{:S(2)}, u32[]{:S(2)}) %collective-permute-start.2) | collective-permute-done | bytes 131104 | tf_op jit(solution)/shard_map/ppermute | solution.py:256
  15.4 0.0 collective-permute-start.3
  15.4 0.0 collective-permute-done.4.refs_6_
  15.4 2.3 %norm0.1 = (bf16[1024,1024]{1,0:T(8,128)(2,1)}, bf16[1024,512]{1,0:T(8,128)(2,1)S(1)}, f32[4,128,128]{2,1,0:T(8,128)S(1)}, f32[4,4,128,128]{3,2,1,0:T(8,128)S(1)}, f32[4,128,128]{2,1,0:T(8,128)S(1)}) custom-call(f32[1024,512]{1,0:T(8,128)S(1)} %get-tuple-element.65.refs_0_, bf16[1024,1024]{1,0:T(8,128)(2,1)S(1)} %get-tuple-element.53.q_ref.refs_1_.refs_0_, ...), custom_call_target="tpu_custom_call" | custom-call | flops 268435456 | bytes 1048576 | tf_op jit(solution)/shard_map/norm0/pallas_call | solution.py:276
  17.7 0.6 %collective-permute-start.5 = (f32[4,128,128]{2,1,0:T(8,128)S(1)}, f32[4,128,128]{2,1,0:T(8,128)S(1)}, u32[]{:S(2)}, u32[]{:S(2)}) collective-permute-start(f32[4,128,128]{2,1,0:T(8,128)S(1)} %get-tuple-element.77.own_ref.refs_5_), channel_id=1, source_target_pairs={{0,4},{4,0},{8,12},{12,8},{1,5},{5,1},{9,13},{13,9},{2,6},{6,2},{1... | collective-permute-start | bytes 786440 | tf_op jit(solution)/shard_map/ppermute | solution.py:255
  18.3 0.0 collective-permute-done.3.refs_6_
  18.3 2.3 %norm1.1 = (bf16[1024,1024]{1,0:T(8,128)(2,1)}, bf16[1024,512]{1,0:T(8,128)(2,1)S(1)}, f32[4,128,128]{2,1,0:T(8,128)S(1)}, f32[4,4,128,128]{3,2,1,0:T(8,128)S(1)}, f32[4,128,128]{2,1,0:T(8,128)S(1)}) custom-call(f32[1024,512]{1,0:T(8,128)S(1)} %get-tuple-element.61.refs_0_, ...), custom_call_target="tpu_custom_call", output_to_operand_aliasing={{0}: (7, {})} | custom-call | flops 268435456 | bytes 1048576 | tf_op jit(solution)/shard_map/norm1/pallas_call | solution.py:276
  20.6 0.1 collective-permute-start.6
  20.7 0.0 collective-permute-done.5.near_ref.refs_6_
  20.8 1.8 %collective-permute-start.9 = (f32[2,128,128]{2,1,0:T(8,128)S(1)}, f32[2,128,128]{2,1,0:T(8,128)S(1)}, u32[]{:S(2)}, u32[]{:S(2)}) collective-permute-start(f32[2,128,128]{2,1,0:T(8,128)S(1)} %half.5), channel_id=1, source_target_pairs={{0,8},{4,12},{8,0},{12,4},{1,9},{5,13},{9,1},{13,5},{2,10},{6,14},... | collective-permute-start | bytes 393224 | tf_op jit(solution)/shard_map/ppermute | solution.py:256
  22.6 0.0 collective-permute-done.6.near_ref.refs_6_
  22.6 1.5 %collective-permute-start.7 = (f32[2,128,128]{2,1,0:T(8,128)S(1)}, f32[2,128,128]{2,1,0:T(8,128)S(1)}, u32[]{:S(2)}, u32[]{:S(2)}) collective-permute-start(f32[2,128,128]{2,1,0:T(8,128)S(1)} %half.4), channel_id=1, source_target_pairs={{0,8},{4,12},{8,0},{12,4},{1,9},{5,13},{9,1},{13,5},{2,10},{6,14},... | collective-permute-start | bytes 393224 | tf_op jit(solution)/shard_map/ppermute | solution.py:256
  24.1 3.1 %back0.1 = (bf16[1024,1024]{1,0:T(8,128)(2,1)}, f32[1024,512]{1,0:T(8,128)S(1)}, f32[1024,512]{1,0:T(8,128)S(1)}) custom-call(bf16[1024,1024]{1,0:T(8,128)(2,1)S(1)} %get-tuple-element.53.q_ref.refs_1_.refs_0_, bf16[1024,1024]{1,0:T(8,128)(2,1)S(1)} %get-tuple-element.54.k_ref.refs_1_.refs_0_, ...), custom_call_target="tpu_custom_call" | custom-call | flops 1207959552 | bytes 1048576 | tf_op jit(solution)/shard_map/back0/pallas_call | solution.py:276
  27.1 0.0 collective-permute-done.9.refs_7_.refs_9_
  27.1 0.1 collective-permute-start.10
  27.2 3.6 %back1.1 = (bf16[1024,1024]{1,0:T(8,128)(2,1)}, f32[1024,512]{1,0:T(8,128)S(1)}, f32[1024,512]{1,0:T(8,128)S(1)}) custom-call(bf16[1024,1024]{1,0:T(8,128)(2,1)S(1)} %get-tuple-element.53.q_ref.refs_1_.refs_0_, bf16[1024,1024]{1,0:T(8,128)(2,1)S(1)} %get-tuple-element.54.k_ref.refs_1_.refs_0_, ...), custom_call_target="tpu_custom_call", output_to_operand_aliasing={{0}: (7, {})} | custom-call | flops 1207959552 | bytes 1048576 | tf_op jit(solution)/shard_map/back1/pallas_call | solution.py:276
  30.8 0.0 collective-permute-done.7.refs_7_.refs_9_
  30.8 0.6 %collective-permute-start.8 = (f32[2,128,128]{2,1,0:T(8,128)S(1)}, f32[2,128,128]{2,1,0:T(8,128)S(1)}, u32[]{:S(2)}, u32[]{:S(2)}) collective-permute-start(f32[2,128,128]{2,1,0:T(8,128)S(1)} %collective-permute-done.7.refs_7_.refs_9_), channel_id=1, source_target_pairs={{0,4},{4,0},{8,12},{12,8},{1,5},{5,1},{9,13},{13,9},{2,6},{6,2},{1... | collective-permute-start | bytes 393224 | tf_op jit(solution)/shard_map/ppermute | solution.py:255
  31.4 0.0 collective-permute-done.10.refs_8_.refs_10_
  31.4 2.2 %last0.1 = (bf16[1024,1024]{1,0:T(8,128)(2,1)}, bf16[1024,1024]{1,0:T(8,128)(2,1)}, f32[8,128,128]{2,1,0:T(8,128)}) custom-call(bf16[1024,1024]{1,0:T(8,128)(2,1)S(1)} %get-tuple-element.54.k_ref.refs_1_.refs_0_, bf16[1024,1024]{1,0:T(8,128)(2,1)S(1)} %get-tuple-element.55.v_ref.refs_2_.refs_1_, f32[1024,512]{1,0:T(8,128)S(1)} %get-tuple-element.88.refs_2_, ...), custom_call_target="tpu_custom_call" | custom-call | flops 268435456 | bytes 2097152 | tf_op jit(solution)/shard_map/last0/pallas_call | solution.py:276
  33.5 0.0 collective-permute-done.8.refs_8_.refs_10_
  33.5 1.9 %last1.1 = (bf16[1024,1024]{1,0:T(8,128)(2,1)}, bf16[1024,1024]{1,0:T(8,128)(2,1)}, f32[8,128,128]{2,1,0:T(8,128)}) custom-call(bf16[1024,1024]{1,0:T(8,128)(2,1)S(1)} %get-tuple-element.54.k_ref.refs_1_.refs_0_, bf16[1024,1024]{1,0:T(8,128)(2,1)S(1)} %get-tuple-element.55.v_ref.refs_2_.refs_1_, ...), custom_call_target="tpu_custom_call", output_to_operand_aliasing={{0}: (11, {}), {1}: (12, {}), {2}: (13, {})} | custom-call | flops 268435456 | bytes 2097152 | tf_op jit(solution)/shard_map/last1/pallas_call | solution.py:276
  (2 shorter events, 0.1 us)
Async XLA Ops:
  3.7 2.1 %collective-permute-start = (f32[8,128,128]{2,1,0:T(8,128)S(1)}, f32[8,128,128]{2,1,0:T(8,128)S(1)}, u32[]{:S(2)}, u32[]{:S(2)}) collective-permute-start(f32[8,128,128]{2,1,0:T(8,128)S(1)} %get-tuple-element.52.own_ref), channel_id=1, source_target_pairs={{0,4},{4,0},{8,12},{12,8},{1,5},{5,1},{9,13},{13,9},{2,6},{6,2},{1... | collective-permute-start | bytes 1572872 | tf_op jit(solution)/shard_map/ppermute | solution.py:255
  5.9 7.1 %collective-permute-start.1 = (f32[2,128,128]{2,1,0:T(8,128)S(1)}, f32[2,128,128]{2,1,0:T(8,128)S(1)}, u32[]{:S(2)}, u32[]{:S(2)}) collective-permute-start(f32[2,128,128]{2,1,0:T(8,128)S(1)} %get-tuple-element.59), channel_id=1, source_target_pairs={{0,8},{4,12},{8,0},{12,4},{1,9},{5,13},{9,1},{13,5},{2,10},{6,14},... | collective-permute-start | bytes 393224 | tf_op jit(solution)/shard_map/ppermute | solution.py:256
  8.7 6.7 %collective-permute-start.2 = (f32[2,128,128]{2,1,0:T(8,128)S(1)}, f32[2,128,128]{2,1,0:T(8,128)S(1)}, u32[]{:S(2)}, u32[]{:S(2)}) collective-permute-start(f32[2,128,128]{2,1,0:T(8,128)S(1)} %get-tuple-element.64), channel_id=1, source_target_pairs={{0,8},{4,12},{8,0},{12,4},{1,9},{5,13},{9,1},{13,5},{2,10},{6,14},... | collective-permute-start | bytes 393224 | tf_op jit(solution)/shard_map/ppermute | solution.py:256
  13.0 2.4 %collective-permute-start.4 = (f32[2,128,128]{2,1,0:T(8,128)S(1)}, f32[2,128,128]{2,1,0:T(8,128)S(1)}, u32[]{:S(2)}, u32[]{:S(2)}) collective-permute-start(f32[2,128,128]{2,1,0:T(8,128)S(1)} %collective-permute-done.1.refs_5_), channel_id=1, source_target_pairs={{0,4},{4,0},{8,12},{12,8},{1,5},{5,1},{9,13},{13,9},{2,6},{6,2},{1... | collective-permute-start | bytes 393224 | tf_op jit(solution)/shard_map/ppermute | solution.py:255
  15.4 2.9 %collective-permute-start.3 = (f32[2,128,128]{2,1,0:T(8,128)S(1)}, f32[2,128,128]{2,1,0:T(8,128)S(1)}, u32[]{:S(2)}, u32[]{:S(2)}) collective-permute-start(f32[2,128,128]{2,1,0:T(8,128)S(1)} %collective-permute-done.2.refs_5_), channel_id=1, source_target_pairs={{0,4},{4,0},{8,12},{12,8},{1,5},{5,1},{9,13},{13,9},{2,6},{6,2},{1... | collective-permute-start | bytes 393224 | tf_op jit(solution)/shard_map/ppermute | solution.py:255
  17.7 3.0 %collective-permute-start.5 = (f32[4,128,128]{2,1,0:T(8,128)S(1)}, f32[4,128,128]{2,1,0:T(8,128)S(1)}, u32[]{:S(2)}, u32[]{:S(2)}) collective-permute-start(f32[4,128,128]{2,1,0:T(8,128)S(1)} %get-tuple-element.77.own_ref.refs_5_), channel_id=1, source_target_pairs={{0,4},{4,0},{8,12},{12,8},{1,5},{5,1},{9,13},{13,9},{2,6},{6,2},{1... | collective-permute-start | bytes 786440 | tf_op jit(solution)/shard_map/ppermute | solution.py:255
  20.6 1.9 %collective-permute-start.6 = (f32[4,128,128]{2,1,0:T(8,128)S(1)}, f32[4,128,128]{2,1,0:T(8,128)S(1)}, u32[]{:S(2)}, u32[]{:S(2)}) collective-permute-start(f32[4,128,128]{2,1,0:T(8,128)S(1)} %get-tuple-element.79.own_ref.refs_5_), channel_id=1, source_target_pairs={{0,4},{4,0},{8,12},{12,8},{1,5},{5,1},{9,13},{13,9},{2,6},{6,2},{1... | collective-permute-start | bytes 786440 | tf_op jit(solution)/shard_map/ppermute | solution.py:255
  20.8 6.4 %collective-permute-start.9 = (f32[2,128,128]{2,1,0:T(8,128)S(1)}, f32[2,128,128]{2,1,0:T(8,128)S(1)}, u32[]{:S(2)}, u32[]{:S(2)}) collective-permute-start(f32[2,128,128]{2,1,0:T(8,128)S(1)} %half.5), channel_id=1, source_target_pairs={{0,8},{4,12},{8,0},{12,4},{1,9},{5,13},{9,1},{13,5},{2,10},{6,14},... | collective-permute-start | bytes 393224 | tf_op jit(solution)/shard_map/ppermute | solution.py:256
  22.6 8.2 %collective-permute-start.7 = (f32[2,128,128]{2,1,0:T(8,128)S(1)}, f32[2,128,128]{2,1,0:T(8,128)S(1)}, u32[]{:S(2)}, u32[]{:S(2)}) collective-permute-start(f32[2,128,128]{2,1,0:T(8,128)S(1)} %half.4), channel_id=1, source_target_pairs={{0,8},{4,12},{8,0},{12,4},{1,9},{5,13},{9,1},{13,5},{2,10},{6,14},... | collective-permute-start | bytes 393224 | tf_op jit(solution)/shard_map/ppermute | solution.py:256
  27.1 4.2 %collective-permute-start.10 = (f32[2,128,128]{2,1,0:T(8,128)S(1)}, f32[2,128,128]{2,1,0:T(8,128)S(1)}, u32[]{:S(2)}, u32[]{:S(2)}) collective-permute-start(f32[2,128,128]{2,1,0:T(8,128)S(1)} %collective-permute-done.9.refs_7_.refs_9_), channel_id=1, source_target_pairs={{0,4},{4,0},{8,12},{12,8},{1,5},{5,1},{9,13},{13,9},{2,6},{6,2},{1... | collective-permute-start | bytes 393224 | tf_op jit(solution)/shard_map/ppermute | solution.py:255
  30.8 2.7 %collective-permute-start.8 = (f32[2,128,128]{2,1,0:T(8,128)S(1)}, f32[2,128,128]{2,1,0:T(8,128)S(1)}, u32[]{:S(2)}, u32[]{:S(2)}) collective-permute-start(f32[2,128,128]{2,1,0:T(8,128)S(1)} %collective-permute-done.7.refs_7_.refs_9_), channel_id=1, source_target_pairs={{0,4},{4,0},{8,12},{12,8},{1,5},{5,1},{9,13},{13,9},{2,6},{6,2},{1... | collective-permute-start | bytes 393224 | tf_op jit(solution)/shard_map/ppermute | solution.py:255

commit v3 on v2

v3 whole, which is shorter than its diff:
```python
import functools

import jax
import jax.numpy as jnp
from jax import lax
from jax.experimental import pallas as pl
from jax.experimental.pallas import tpu as pltpu
from jax.sharding import PartitionSpec as P

F32 = jnp.float32
BF16 = jnp.bfloat16
EPS = 1e-06
VM = pl.BlockSpec(memory_space=pltpu.VMEM)
HB = pl.BlockSpec(memory_space=pltpu.HBM)


def mm(a, b):
    return lax.dot_general(a, b, (((1,), (0,)), ((), ())), preferred_element_type=F32)


def mm_rt(a, b):
    return lax.dot_general(a, b, (((1,), (1,)), ((), ())), preferred_element_type=F32)


def mm_lt(a, b):
    return lax.dot_general(a, b, (((0,), (0,)), ((), ())), preferred_element_type=F32)


def causal(size):
    return lax.broadcasted_iota(jnp.int32, (size, size), 0) >= lax.broadcasted_iota(
        jnp.int32, (size, size), 1
    )


class Cut:
    def __init__(self, rows, heads, dim, group, groups):
        self.rows, self.heads, self.dim = rows, heads, dim
        self.per = heads // groups
        self.base = group * self.per
        self.size = 256 if rows % 256 == 0 else rows
        self.chunks = rows // self.size

    def rng(self, c):
        return slice(c * self.size, (c + 1) * self.size)

    def cols(self, h):
        return slice(h * self.dim, (h + 1) * self.dim)

    def whole(self, h):
        return self.cols(self.base + h)

    def each(self):
        return [(h, c) for h in range(self.per) for c in range(self.chunks)]

    def span(self):
        return pl.ds(self.base * self.dim, self.per * self.dim)


def column_copies(pairs, sems):
    copies = [pltpu.make_async_copy(src, dst, sems.at[i]) for i, (src, dst) in enumerate(pairs)]
    for copy in copies:
        copy.start()
    return copies


def state_kernel(cut, k_hbm, v_hbm, _, total_ref, before_ref, k_ref, v_ref, sems):
    width = 2 * cut.dim

    def copy(i, j):
        src, dst = ((k_hbm, k_ref), (v_hbm, v_ref))[j]
        from_at = pl.ds(cut.base * cut.dim + i * width, width)
        return pltpu.make_async_copy(
            src.at[:, from_at], dst.at[:, pl.ds(i * width, width)], sems.at[j, i]
        )

    for i in range(cut.per // 2):
        copy(i, 0).start()
        copy(i, 1).start()
    for h in range(cut.per):
        if h % 2 == 0:
            copy(h // 2, 0).wait()
            copy(h // 2, 1).wait()
        terms = [
            mm_lt(k_ref[cut.rng(c), cut.cols(h)], v_ref[cut.rng(c), cut.cols(h)])
            for c in range(cut.chunks)
        ]
        run = jnp.zeros((cut.dim, cut.dim), F32)
        for c in range(cut.chunks):
            before_ref[h, c] = run
            run = run + terms[c]
        total_ref[h] = run


def inner_kernel(cut, q_ref, k_ref, v_ref, before_ref, att_ref, scores_ref):
    keep = causal(cut.size)
    each = cut.each()
    q = {(h, c): q_ref[cut.rng(c), cut.whole(h)] for h, c in each}
    k = {(h, c): k_ref[cut.rng(c), cut.cols(h)] for h, c in each}
    v = {(h, c): v_ref[cut.rng(c), cut.cols(h)] for h, c in each}
    scores = {j: jnp.where(keep, mm_rt(q[j], k[j]), 0.0).astype(BF16) for j in each}
    att = {j: mm(scores[j], v[j]) for j in each}
    for h, c in each:
        if c > 0:
            att[h, c] = att[h, c] + mm(q[h, c], before_ref[h, c].astype(BF16))
    for h, c in each:
        scores_ref[h, c] = scores[h, c]
        att_ref[cut.rng(c), cut.cols(h)] = att[h, c]


def far_of(per, h, own_half, other_half):
    half = per // 2
    first = lax.rem(lax.axis_index("ctx"), 2) == 0
    mine, other = own_half[h % half], other_half[h % half]
    return jnp.where(first == (h < half), mine, other)


def norm_kernel(cut, masked, *refs):
    att_ref, q_ref, g_ref, init_ref, near_ref, far_ref, other_ref = refs[:7]
    out_ref, ga_ref, total_ref, after_ref, prefix_ref = refs[7:]
    place = lax.axis_index("ctx")
    add_near = lax.rem(place, 2) == 1
    add_far = place >= 2
    for h in range(cut.per):
        full = far_of(cut.per, h, far_ref, other_ref)
        if not masked:
            full = jnp.where(add_far, full, 0.0)
        prefix_ref[h] = init_ref[cut.base + h] + (full + jnp.where(add_near, near_ref[h], 0.0))
    ga = {}
    for h, c in cut.each():
        q = q_ref[cut.rng(c), cut.whole(h)]
        att = att_ref[cut.rng(c), cut.cols(h)] + mm(q, prefix_ref[h].astype(BF16))
        up = g_ref[cut.rng(c), cut.whole(h)].astype(F32)
        square = jnp.sum(att * att, axis=-1, keepdims=True)
        along = jnp.sum(up * att, axis=-1, keepdims=True)
        inv = lax.rsqrt(square * (1.0 / cut.dim) + EPS)
        normed = att * inv
        ga[h, c] = (inv * (up - normed * (along * (inv * (1.0 / cut.dim))))).astype(BF16)
        out_ref[cut.rng(c), cut.cols(h)] = normed.astype(BF16)
        ga_ref[cut.rng(c), cut.cols(h)] = ga[h, c]
    terms = {(h, c): mm_lt(q_ref[cut.rng(c), cut.whole(h)], ga[h, c]) for h, c in cut.each()}
    for h in range(cut.per):
        run = jnp.zeros((cut.dim, cut.dim), F32)
        for c in reversed(range(cut.chunks)):
            after_ref[h, c] = run
            run = run + terms[h, c]
        total_ref[h] = run


def back_kernel(cuts, g, *refs):
    cut = cuts[g]
    count = len(cuts) if g == 0 else 0
    q_ref, k_ref, v_ref, ga_ref, prefix_ref, before_ref, scores_ref = refs[:7]
    ready = refs[7 : 7 + count]
    qg_ref, kg_ref, vg_ref = refs[7 + count : 10 + count]
    copies = []
    if g == 0:
        hbm, sems = refs[10 + count :]
        copies = column_copies([(r, hbm.at[:, cuts[i].span()]) for i, r in enumerate(ready)], sems)
    keep = causal(cut.size)
    each = cut.each()
    q = {j: q_ref[cut.rng(j[1]), cut.whole(j[0])] for j in each}
    k = {j: k_ref[cut.rng(j[1]), cut.cols(j[0])] for j in each}
    v = {j: v_ref[cut.rng(j[1]), cut.cols(j[0])] for j in each}
    ga = {j: ga_ref[cut.rng(j[1]), cut.cols(j[0])] for j in each}
    state = {
        (h, c): (prefix_ref[h] + before_ref[h, c]).astype(BF16) for h, c in each
    }
    scores = {j: scores_ref[j[0], j[1]] for j in each}
    grad = {j: jnp.where(keep, mm_rt(ga[j], v[j]), 0.0).astype(BF16) for j in each}
    qg = {j: mm(grad[j], k[j]) + mm_rt(ga[j], state[j]) for j in each}
    for h, c in each:
        qg_ref[cut.rng(c), cut.cols(h)] = qg[h, c].astype(BF16)
    vg = {j: mm(ga[j].T, scores[j]) for j in each}
    kg = {j: mm(q[j].T, grad[j]) for j in each}
    for h, c in each:
        kg_ref[cut.cols(h), cut.rng(c)] = kg[h, c]
        vg_ref[cut.cols(h), cut.rng(c)] = vg[h, c]
    for copy in copies:
        copy.wait()


def last_kernel(cuts, g, masked, *refs):
    cut = cuts[g]
    k_ref, v_ref, kp_ref, vp_ref, after_ref, own_ref, near_ref = refs[:7]
    far_ref, other_ref, all_ref, all_other_ref = refs[7:11]
    final = g == len(cuts) - 1
    if g == 0:
        grads, refs = refs[11 : 11 + len(cuts)], refs[11 + len(cuts) :]
    else:
        ready, refs = [refs[11 + 3 * i : 14 + 3 * i] for i in range(g)], refs[11 + 3 * g :]
    if final:
        kg_hbm, vg_hbm, sg_hbm, kg_ref, vg_ref, sg_ref, ready_sems, sems, sg_sem = refs
    else:
        kg_ref, vg_ref, sg_ref = refs[:3]
    place = lax.axis_index("ctx")
    add_near = lax.rem(place, 2) == 0
    add_far = place < 2
    copies = []
    if g == 0:
        hbm, qg_sems = refs[3:]
        copies += column_copies(
            [(r, hbm.at[:, cuts[i].span()]) for i, r in enumerate(grads)], qg_sems
        )
    if final:
        pairs = []
        for i, (kg, vg, sg) in enumerate(ready):
            at = cuts[i].span()
            pairs += [(kg, kg_hbm.at[:, at]), (vg, vg_hbm.at[:, at])]
            pairs += [(sg, sg_hbm.at[pl.ds(cuts[i].base, cut.per)])]
        copies += column_copies(pairs, ready_sems)
    for h in range(cut.per):
        near = near_ref[h]
        full = far_of(cut.per, h, far_ref, other_ref)
        every = far_of(cut.per, h, all_ref, all_other_ref)
        sg_ref[h] = every + (own_ref[h] + near)
        if not masked:
            full = jnp.where(add_far, full, 0.0)
        suffix = full + jnp.where(add_near, near, 0.0)
        cols = cut.cols(h)
        for c in range(cut.chunks):
            rows = cut.rng(c)
            state = (suffix + after_ref[h, c]).astype(BF16)
            kg = kp_ref[cols, rows] + mm_rt(state, v_ref[rows, cols])
            vg = vp_ref[cols, rows] + mm_rt(state.T, k_ref[rows, cols])
            kg_ref[rows, cols] = kg.astype(BF16).T
            vg_ref[rows, cols] = vg.astype(BF16).T
        if final:
            at, to = pl.ds(h * cut.dim, cut.dim), pl.ds((cut.base + h) * cut.dim, cut.dim)
            copies += column_copies(
                [(kg_ref.at[:, at], kg_hbm.at[:, to]), (vg_ref.at[:, at], vg_hbm.at[:, to])],
                sems.at[h],
            )
    if final:
        copies += column_copies([(sg_ref, sg_hbm.at[pl.ds(cut.base, cut.per)])], sg_sem)
    for copy in copies:
        copy.wait()


def half_kernel(own_ref, near_ref, mine_ref):
    half = mine_ref.shape[0]
    first = lax.rem(lax.axis_index("ctx"), 2) == 0
    for h in range(half):
        mine_ref[h] = jnp.where(
            first, own_ref[h] + near_ref[h], own_ref[half + h] + near_ref[half + h]
        )


def shards(n, groups, queries, keys, values, init_state, out_grad):
    rows, width = queries.shape
    heads, dim = init_state.shape[:2]
    pairs = n // 2
    swap_pairs = [(i, i ^ 1) for i in range(n)]
    shift_pairs = [(i, (i + 2) % n) for i in range(n)]
    swap = lambda x: lax.ppermute(x, "ctx", swap_pairs)
    shift = lambda x: lax.ppermute(x, "ctx", shift_pairs)
    cuts = [Cut(rows, heads, dim, g, groups) for g in range(groups)]
    per, chunks, size = cuts[0].per, cuts[0].chunks, cuts[0].size
    wide_b = jax.ShapeDtypeStruct((rows, width), BF16)
    all_b = pltpu.VMEM((rows, width), BF16)
    part_b = pltpu.VMEM((rows, per * dim), BF16)
    part_f = pltpu.VMEM((rows, per * dim), F32)
    part_ft = pltpu.VMEM((per * dim, rows), F32)
    state_f = pltpu.VMEM((per, dim, dim), F32)
    states_f = pltpu.VMEM((per, chunks, dim, dim), F32)
    scores_b = pltpu.VMEM((per, chunks, size, size), BF16)
    small = 2 * per * rows * dim * dim
    square = 2 * per * rows * size * dim
    piece = rows * per * dim * 2
    dma = pltpu.SemaphoreType.DMA

    def call(body, name, ins, outs, scratch, flops, nbytes):
        return pl.pallas_call(
            body,
            in_specs=[VM] * len(ins),
            out_specs=[HB if isinstance(o, jax.ShapeDtypeStruct) else VM for o in outs],
            out_shape=list(outs),
            scratch_shapes=scratch,
            compiler_params=pltpu.CompilerParams(vmem_limit_bytes=16 * 1024 * 1024),
            cost_estimate=pl.CostEstimate(flops=flops, bytes_accessed=nbytes, transcendentals=0),
            name=name,
        )(*ins)

    def far_sums(mine, later):
        if pairs == 2:
            far = shift(mine)
            return far, far
        pair = lax.axis_index("ctx") // 2
        moving = mine
        used, every = jnp.zeros_like(mine), jnp.zeros_like(mine)
        for j in range(1, pairs):
            moving = shift(moving)
            wrapped = pair < j
            used = used + jnp.where(wrapped == later, moving, 0.0)
            every = every + moving
        return used, every

    def half_of(own, near):
        return pl.pallas_call(
            half_kernel,
            in_specs=[VM] * 2,
            out_specs=VM,
            out_shape=pltpu.VMEM((per // 2, dim, dim), F32),
            compiler_params=pltpu.CompilerParams(vmem_limit_bytes=4 * 1024 * 1024),
            name="half",
        )(own, near)

    masked = pairs != 2

    def state_call(g):
        order = keys if g == 0 else own[g - 1]
        return pl.pallas_call(
            functools.partial(state_kernel, cuts[g]),
            in_specs=[HB, HB, HB if g == 0 else VM],
            out_specs=[VM] * 4,
            out_shape=[state_f, states_f, part_b, part_b],
            scratch_shapes=[dma((2, per // 2))],
            compiler_params=pltpu.CompilerParams(vmem_limit_bytes=16 * 1024 * 1024),
            cost_estimate=pl.CostEstimate(
                flops=small, bytes_accessed=2 * piece, transcendentals=0
            ),
            name="states%d" % g,
        )(in_hbm(keys), in_hbm(values), in_hbm(order) if g == 0 else order)

    in_hbm = lambda x: pltpu.with_memory_space_constraint(x, pltpu.HBM)
    own, before, near, keys_v, values_v = {}, {}, {}, {}, {}
    for g, cut in enumerate(cuts):
        own[g], before[g], keys_v[g], values_v[g] = state_call(g)
        near[g] = swap(own[g])
    att, scores, far, other = {}, {}, {}, {}
    for g in range(groups):
        mine = half_of(own[g], near[g])
        far[g], _ = far_sums(mine, False)
        if g == groups - 1:
            mine, before[0] = lax.optimization_barrier((mine, before[0]))
    for g, cut in enumerate(cuts):
        att[g], scores[g] = call(
            functools.partial(inner_kernel, cut),
            "inner%d" % g,
            [queries, keys_v[g], values_v[g], before[g]],
            [part_f, scores_b],
            [],
            2 * square + small,
            0,
        )
    far[0], att[0], att[1] = lax.optimization_barrier((far[0], att[0], att[1]))
    for g in range(groups):
        other[g] = swap(far[g])
    out, ga, total, after, prefix = {}, {}, {}, {}, {}
    gnear, gfar, gall = {}, {}, {}
    for g, cut in enumerate(cuts):
        out[g], ga[g], total[g], after[g], prefix[g] = call(
            functools.partial(norm_kernel, cut, masked),
            "norm%d" % g,
            [att[g], queries, out_grad, init_state, near[g], far[g], other[g]],
            [part_b, part_b, state_f, states_f, state_f],
            [],
            2 * small,
            piece,
        )
        gnear[g] = swap(total[g])
    gnear[0], total[1] = lax.optimization_barrier((gnear[0], total[1]))
    for g, cut in enumerate(cuts):
        gfar[g], gall[g] = far_sums(half_of(total[g], gnear[g]), True)
    kp, vp, qg = {}, {}, {}
    for g, cut in enumerate(cuts):
        ready = list(out.values()) if g == 0 else []
        qg[g], kp[g], vp[g], *written = call(
            functools.partial(back_kernel, cuts, g),
            "back%d" % g,
            [queries, keys_v[g], values_v[g], ga[g], prefix[g], before[g], scores[g], *ready],
            [part_b, part_ft, part_ft] + [wide_b] * (g == 0),
            [dma((groups,))] if g == 0 else [],
            4 * square + small,
            piece,
        )
        if g == 0:
            (output,) = written
        gfar[g], gall[g], kp[g] = lax.optimization_barrier((gfar[g], gall[g], kp[g]))
    ready = list(qg.values())
    for g, cut in enumerate(cuts):
        used = swap(gfar[g])
        total_far = used if pairs == 2 else swap(gall[g])
        ins = [
            keys_v[g], values_v[g], kp[g], vp[g], after[g], total[g], gnear[g],
            gfar[g], used, gall[g], total_far,
        ]
        outs, scratch = [part_b, part_b, state_f], []
        if g == groups - 1:
            scratch = outs + [dma((3 * g,)), dma((per, 2)), dma((1,))]
            outs = [wide_b, wide_b, jax.ShapeDtypeStruct(init_state.shape, F32)]
        elif g == 0:
            outs, scratch = outs + [wide_b], [dma((groups,))]
        ends = list(
            call(
                functools.partial(last_kernel, cuts, g, masked),
                "last%d" % g,
                ins + ready,
                outs,
                scratch,
                2 * small,
                2 * piece,
            )
        )
        if g == 0:
            ready, query_grad = [], ends.pop()
        ready += ends
    key_grad, value_grad, state_grad = ends
    return output, query_grad, key_grad, value_grad, state_grad


def solution(mesh):
    wide = P(("grp", "ctx"), "head")
    deep = P(("grp", "head"), None, None)
    return jax.shard_map(
        functools.partial(shards, mesh.shape["ctx"], 2),
        mesh=mesh,
        in_specs=(wide, wide, wide, deep, wide),
        out_specs=(wide, wide, wide, wide, deep),
        check_vma=False,
    )
```

time: 35.8 us -> 33.5 us (0.936)
  waiting for transfers between devices: 5.1 us -> 2.53 us
  starting transfers between devices: 8.03 us -> 9.21 us
  Pallas kernels: 21.6 us -> 20.6 us
    ppermute x4, waiting for transfers between devices: 5.08 us -> 2.51 us  [shards(): shift = lambda x: lax.ppermute(x, 'ctx', shift_pairs)]
    ppermute x4, starting transfers between devices: 6.2 us -> 7.32 us  [shards(): shift = lambda x: lax.ppermute(x, 'ctx', shift_pairs)]
    pallas_call x12 -> x14, Pallas kernels: 21.6 us -> 20.6 us  [the longest x8 16.5 us: call(): pl.pallas_call(body, in_specs=[VM] * len(ins), out_specs=[HB if isinstanc...]
    ppermute x7 -> x8, starting transfers between devices: 1.82 us -> 1.89 us  [shards(): swap = lambda x: lax.ppermute(x, 'ctx', swap_pairs)]
  transfers between devices with their start and end apart: 11 -> 12, of which waited for: 2 -> 4; matrix products, arithmetic and copies ran while one was open for 0% -> 0% of each run, Pallas kernels for 47% -> 48%
where the time goes in v3:
time: 33.5 us; the launch traced here: 33.3 us
  Pallas kernels  20.6 us (61%)
  starting transfers between devices  9.21 us (27%)
  waiting for transfers between devices  2.53 us (8%)
  between operations  0.94 us (3%)
    pallas_call x8, Pallas kernels, call(): pl.pallas_call(body, in_specs=[VM] * len(ins), out_specs=[HB if isinstanc...  16.5 us
    ppermute x4, starting transfers between devices, shards(): shift = lambda x: lax.ppermute(x, 'ctx', shift_pairs)  7.32 us
    pallas_call x2, Pallas kernels, state_call(): pl.pallas_call(functools.partial(state_kernel, cuts[g]), in_specs=[HB, HB...  4 us
    ppermute x4, waiting for transfers between devices, shards(): shift = lambda x: lax.ppermute(x, 'ctx', shift_pairs)  2.51 us
    ppermute x8, starting transfers between devices, shards(): swap = lambda x: lax.ppermute(x, 'ctx', swap_pairs)  1.89 us
  transfers between devices with their start and end apart: 12, of which 4 were waited for; matrix products, arithmetic and copies ran while one was open for 0% of the time, Pallas kernels for 48%

profile of v3, /device:TPU:0, one launch (start us, length us, event | category | flops | bytes accessed | tf_op | source)
XLA Modules:
  0.0 33.3 jit_solution(13742530069023163722)
XLA Ops:
  0.6 2.0 %states0.1 = (f32[4,128,128]{2,1,0:T(8,128)S(1)}, f32[4,4,128,128]{3,2,1,0:T(8,128)S(1)}, bf16[1024,512]{1,0:T(8,128)(2,1)S(1)}, bf16[1024,512]{1,0:T(8,128)(2,1)S(1)}) custom-call(bf16[1024,1024]{1,0:T(8,128)(2,1)} %k_hbm.3, bf16[1024,1024]{1,0:T(8,128)(2,1)} %v_hbm.3, bf16[1024,1024]{1,0:T(8,128)(2,1)} %k_hbm.3), custom_call_target="tpu_custom_call" | custom-call | flops 134217728 | bytes 2097152 | tf_op jit(solution)/shard_map/states0/pallas_call | solution.py:311
  2.6 0.0 copy-start
  2.6 0.5 %collective-permute-start = (f32[4,128,128]{2,1,0:T(8,128)S(1)}, f32[4,128,128]{2,1,0:T(8,128)S(1)}, u32[]{:S(2)}, u32[]{:S(2)}) collective-permute-start(f32[4,128,128]{2,1,0:T(8,128)S(1)} %get-tuple-element.55.own_ref._), channel_id=1, source_target_pairs={{0,4},{4,0},{8,12},{12,8},{1,5},{5,1},{9,13},{13,9},{2,6},{6,2},{1... | collective-permute-start | bytes 786440 | tf_op jit(solution)/shard_map/ppermute | solution.py:254
  3.1 2.0 %states1.1 = (f32[4,128,128]{2,1,0:T(8,128)S(1)}, f32[4,4,128,128]{3,2,1,0:T(8,128)S(1)}, bf16[1024,512]{1,0:T(8,128)(2,1)S(1)}, bf16[1024,512]{1,0:T(8,128)(2,1)S(1)}) custom-call(bf16[1024,1024]{1,0:T(8,128)(2,1)} %k_hbm.3, bf16[1024,1024]{1,0:T(8,128)(2,1)} %v_hbm.3, f32[4,128,128]{2,1,0:T(8,128)S(1)} %get-tuple-element.55.own_ref._), custom_call_target="tpu_custom_call" | custom-call | flops 134217728 | bytes 2097152 | tf_op jit(solution)/shard_map/states1/pallas_call | solution.py:311
  5.2 0.1 collective-permute-start.2
  5.3 0.0 collective-permute-done.near_ref.refs_4_
  5.4 2.9 %collective-permute-start.1 = (f32[2,128,128]{2,1,0:T(8,128)S(1)}, f32[2,128,128]{2,1,0:T(8,128)S(1)}, u32[]{:S(2)}, u32[]{:S(2)}) collective-permute-start(f32[2,128,128]{2,1,0:T(8,128)S(1)} %half.4), channel_id=1, source_target_pairs={{0,8},{4,12},{8,0},{12,4},{1,9},{5,13},{9,1},{13,5},{2,10},{6,14},... | collective-permute-start | bytes 393224 | tf_op jit(solution)/shard_map/ppermute | solution.py:255
  8.3 0.0 collective-permute-done.2.near_ref.refs_4_
  8.3 1.2 %collective-permute-start.4 = (f32[2,128,128]{2,1,0:T(8,128)S(1)}, f32[2,128,128]{2,1,0:T(8,128)S(1)}, u32[]{:S(2)}, u32[]{:S(2)}) collective-permute-start(f32[2,128,128]{2,1,0:T(8,128)S(1)} %half.5), channel_id=1, source_target_pairs={{0,8},{4,12},{8,0},{12,4},{1,9},{5,13},{9,1},{13,5},{2,10},{6,14},... | collective-permute-start | bytes 393224 | tf_op jit(solution)/shard_map/ppermute | solution.py:255
  9.5 0.0 copy-done
  9.5 1.5 %inner1.1 = (f32[1024,512]{1,0:T(8,128)S(1)}, bf16[4,4,256,256]{3,2,1,0:T(8,128)(2,1)S(1)}) custom-call(bf16[1024,1024]{1,0:T(8,128)(2,1)S(1)} %copy-done, bf16[1024,512]{1,0:T(8,128)(2,1)S(1)} %get-tuple-element.60.k_ref.refs_1_.refs_0_, bf16[1024,512]{1,0:T(8,128)(2,1)S(1)} %get-tuple-element.61.v_ref.refs_2_.refs_1_, ...), custom_call_target="tpu_custom_call" | custom-call | flops 671088640 | tf_op jit(solution)/shard_map/inner1/pallas_call | solution.py:272
  10.9 0.0 copy-start.1
  11.0 0.0 copy-start.2
  11.0 1.5 %inner0.1 = (f32[1024,512]{1,0:T(8,128)S(1)}, bf16[4,4,256,256]{3,2,1,0:T(8,128)(2,1)S(1)}) custom-call(bf16[1024,1024]{1,0:T(8,128)(2,1)S(1)} %copy-done, bf16[1024,512]{1,0:T(8,128)(2,1)S(1)} %get-tuple-element.53.k_ref.refs_1_.refs_0_, bf16[1024,512]{1,0:T(8,128)(2,1)S(1)} %get-tuple-element.54.v_ref.refs_2_.refs_1_, ...), custom_call_target="tpu_custom_call" | custom-call | flops 671088640 | tf_op jit(solution)/shard_map/inner0/pallas_call | solution.py:272
  12.5 0.1 collective-permute-done.1.refs_5_
  12.6 0.0 collective-permute-start.3
  12.6 2.3 %collective-permute-done.4.refs_5_ = f32[2,128,128]{2,1,0:T(8,128)S(1)} collective-permute-done((f32[2,128,128]{2,1,0:T(8,128)S(1)}, f32[2,128,128]{2,1,0:T(8,128)S(1)}, u32[]{:S(2)}, u32[]{:S(2)}) %collective-permute-start.4) | collective-permute-done | bytes 131104 | tf_op jit(solution)/shard_map/ppermute | solution.py:255
  14.9 0.0 collective-permute-start.5
  14.9 0.0 collective-permute-done.3.refs_6_
  14.9 0.0 copy-done.1
  14.9 0.0 copy-done.2
  14.9 2.0 %norm0.1 = (bf16[1024,512]{1,0:T(8,128)(2,1)S(1)}, bf16[1024,512]{1,0:T(8,128)(2,1)S(1)}, f32[4,128,128]{2,1,0:T(8,128)S(1)}, f32[4,4,128,128]{3,2,1,0:T(8,128)S(1)}, f32[4,128,128]{2,1,0:T(8,128)S(1)}) custom-call(f32[1024,512]{1,0:T(8,128)S(1)} %get-tuple-element.64.refs_0_, bf16[1024,1024]{1,0:T(8,128)(2,1)S(1)} %copy-done, ...), custom_call_target="tpu_custom_call" | custom-call | flops 268435456 | bytes 1048576 | tf_op jit(solution)/shard_map/norm0/pallas_call | solution.py:272
  16.9 0.6 %collective-permute-start.6 = (f32[4,128,128]{2,1,0:T(8,128)S(1)}, f32[4,128,128]{2,1,0:T(8,128)S(1)}, u32[]{:S(2)}, u32[]{:S(2)}) collective-permute-start(f32[4,128,128]{2,1,0:T(8,128)S(1)} %get-tuple-element.73.own_ref.refs_5_), channel_id=1, source_target_pairs={{0,4},{4,0},{8,12},{12,8},{1,5},{5,1},{9,13},{13,9},{2,6},{6,2},{1... | collective-permute-start | bytes 786440 | tf_op jit(solution)/shard_map/ppermute | solution.py:254
  17.5 0.0 collective-permute-done.5.refs_6_
  17.5 2.0 %norm1.1 = (bf16[1024,512]{1,0:T(8,128)(2,1)S(1)}, bf16[1024,512]{1,0:T(8,128)(2,1)S(1)}, f32[4,128,128]{2,1,0:T(8,128)S(1)}, f32[4,4,128,128]{3,2,1,0:T(8,128)S(1)}, f32[4,128,128]{2,1,0:T(8,128)S(1)}) custom-call(f32[1024,512]{1,0:T(8,128)S(1)} %get-tuple-element.70.refs_0_, bf16[1024,1024]{1,0:T(8,128)(2,1)S(1)} %copy-done, ...), custom_call_target="tpu_custom_call" | custom-call | flops 268435456 | bytes 1048576 | tf_op jit(solution)/shard_map/norm1/pallas_call | solution.py:272
  19.4 0.1 collective-permute-start.9
  19.5 0.0 collective-permute-done.6.near_ref.refs_6_
  19.5 1.8 %collective-permute-start.7 = (f32[2,128,128]{2,1,0:T(8,128)S(1)}, f32[2,128,128]{2,1,0:T(8,128)S(1)}, u32[]{:S(2)}, u32[]{:S(2)}) collective-permute-start(f32[2,128,128]{2,1,0:T(8,128)S(1)} %half.6), channel_id=1, source_target_pairs={{0,8},{4,12},{8,0},{12,4},{1,9},{5,13},{9,1},{13,5},{2,10},{6,14},... | collective-permute-start | bytes 393224 | tf_op jit(solution)/shard_map/ppermute | solution.py:255
  21.3 0.0 collective-permute-done.9.near_ref.refs_6_
  21.4 1.5 %collective-permute-start.10 = (f32[2,128,128]{2,1,0:T(8,128)S(1)}, f32[2,128,128]{2,1,0:T(8,128)S(1)}, u32[]{:S(2)}, u32[]{:S(2)}) collective-permute-start(f32[2,128,128]{2,1,0:T(8,128)S(1)} %half.7), channel_id=1, source_target_pairs={{0,8},{4,12},{8,0},{12,4},{1,9},{5,13},{9,1},{13,5},{2,10},{6,14},... | collective-permute-start | bytes 393224 | tf_op jit(solution)/shard_map/ppermute | solution.py:255
  22.8 3.0 %back0.1 = (bf16[1024,512]{1,0:T(8,128)(2,1)S(1)}, f32[512,1024]{1,0:T(8,128)S(1)}, f32[512,1024]{1,0:T(8,128)S(1)}, bf16[1024,1024]{1,0:T(8,128)(2,1)}) custom-call(bf16[1024,1024]{1,0:T(8,128)(2,1)S(1)} %copy-done, bf16[1024,512]{1,0:T(8,128)(2,1)S(1)} %get-tuple-element.53.k_ref.refs_1_.refs_0_, ...), custom_call_target="tpu_custom_call" | custom-call | flops 1207959552 | bytes 1048576 | tf_op jit(solution)/shard_map/back0/pallas_call | solution.py:272
  25.8 0.1 collective-permute-done.7.refs_7_.refs_9_
  25.9 0.0 collective-permute-start.8
  25.9 2.3 %back1.1 = (bf16[1024,512]{1,0:T(8,128)(2,1)S(1)}, f32[512,1024]{1,0:T(8,128)S(1)}, f32[512,1024]{1,0:T(8,128)S(1)}) custom-call(bf16[1024,1024]{1,0:T(8,128)(2,1)S(1)} %copy-done, bf16[1024,512]{1,0:T(8,128)(2,1)S(1)} %get-tuple-element.60.k_ref.refs_1_.refs_0_, bf16[1024,512]{1,0:T(8,128)(2,1)S(1)} %get-tuple-element.61.v_ref.refs_2_.refs_1_, ...), custom_call_target="tpu_custom_call" | custom-call | flops 1207959552 | bytes 1048576 | tf_op jit(solution)/shard_map/back1/pallas_call | solution.py:272
  28.2 0.1 collective-permute-done.10.refs_7_.refs_9_
  28.3 0.5 %collective-permute-start.11 = (f32[2,128,128]{2,1,0:T(8,128)S(1)}, f32[2,128,128]{2,1,0:T(8,128)S(1)}, u32[]{:S(2)}, u32[]{:S(2)}) collective-permute-start(f32[2,128,128]{2,1,0:T(8,128)S(1)} %collective-permute-done.10.refs_7_.refs_9_), channel_id=1, source_target_pairs={{0,4},{4,0},{8,12},{12,8},{1,5},{5,1},{9,13},{13,9},{2,6},{6,2},{1... | collective-permute-start | bytes 393224 | tf_op jit(solution)/shard_map/ppermute | solution.py:254
  28.8 0.0 collective-permute-done.8.refs_8_.refs_10_
  28.8 1.8 %last0.1 = (bf16[1024,512]{1,0:T(8,128)(2,1)S(1)}, bf16[1024,512]{1,0:T(8,128)(2,1)S(1)}, f32[4,128,128]{2,1,0:T(8,128)S(1)}, bf16[1024,1024]{1,0:T(8,128)(2,1)}) custom-call(bf16[1024,512]{1,0:T(8,128)(2,1)S(1)} %get-tuple-element.53.k_ref.refs_1_.refs_0_, bf16[1024,512]{1,0:T(8,128)(2,1)S(1)} %get-tuple-element.54.v_ref.refs_2_.refs_1_, ...), custom_call_target="tpu_custom_call" | custom-call | flops 268435456 | bytes 2097152 | tf_op jit(solution)/shard_map/last0/pallas_call | solution.py:272
  30.6 0.0 collective-permute-done.11.refs_8_.refs_10_
  30.6 2.6 %last1.1 = (bf16[1024,1024]{1,0:T(8,128)(2,1)}, bf16[1024,1024]{1,0:T(8,128)(2,1)}, f32[8,128,128]{2,1,0:T(8,128)}) custom-call(bf16[1024,512]{1,0:T(8,128)(2,1)S(1)} %get-tuple-element.60.k_ref.refs_1_.refs_0_, bf16[1024,512]{1,0:T(8,128)(2,1)S(1)} %get-tuple-element.61.v_ref.refs_2_.refs_1_, f32[512,1024]{1,0:T(8,128)S(1)} %get-tuple-element.90.refs_2_, ...), custom_call_target="tpu_custom_call" | custom-call | flops 268435456 | bytes 2097152 | tf_op jit(solution)/shard_map/last1/pallas_call | solution.py:272
  (4 shorter events, 0.1 us)
Async XLA Ops:
  2.6 6.9 %copy-start = (bf16[1024,1024]{1,0:T(8,128)(2,1)S(1)}, bf16[1024,1024]{1,0:T(8,128)(2,1)}, u32[]{:S(2)}) copy-start(bf16[1024,1024]{1,0:T(8,128)(2,1)} %refs_0_.3) | copy-start | bytes 6291460
  2.6 2.7 %collective-permute-start = (f32[4,128,128]{2,1,0:T(8,128)S(1)}, f32[4,128,128]{2,1,0:T(8,128)S(1)}, u32[]{:S(2)}, u32[]{:S(2)}) collective-permute-start(f32[4,128,128]{2,1,0:T(8,128)S(1)} %get-tuple-element.55.own_ref._), channel_id=1, source_target_pairs={{0,4},{4,0},{8,12},{12,8},{1,5},{5,1},{9,13},{13,9},{2,6},{6,2},{1... | collective-permute-start | bytes 786440 | tf_op jit(solution)/shard_map/ppermute | solution.py:254
  5.2 3.1 %collective-permute-start.2 = (f32[4,128,128]{2,1,0:T(8,128)S(1)}, f32[4,128,128]{2,1,0:T(8,128)S(1)}, u32[]{:S(2)}, u32[]{:S(2)}) collective-permute-start(f32[4,128,128]{2,1,0:T(8,128)S(1)} %get-tuple-element.56.own_ref), channel_id=1, source_target_pairs={{0,4},{4,0},{8,12},{12,8},{1,5},{5,1},{9,13},{13,9},{2,6},{6,2},{1... | collective-permute-start | bytes 786440 | tf_op jit(solution)/shard_map/ppermute | solution.py:254
  5.4 7.2 %collective-permute-start.1 = (f32[2,128,128]{2,1,0:T(8,128)S(1)}, f32[2,128,128]{2,1,0:T(8,128)S(1)}, u32[]{:S(2)}, u32[]{:S(2)}) collective-permute-start(f32[2,128,128]{2,1,0:T(8,128)S(1)} %half.4), channel_id=1, source_target_pairs={{0,8},{4,12},{8,0},{12,4},{1,9},{5,13},{9,1},{13,5},{2,10},{6,14},... | collective-permute-start | bytes 393224 | tf_op jit(solution)/shard_map/ppermute | solution.py:255
  8.3 6.6 %collective-permute-start.4 = (f32[2,128,128]{2,1,0:T(8,128)S(1)}, f32[2,128,128]{2,1,0:T(8,128)S(1)}, u32[]{:S(2)}, u32[]{:S(2)}) collective-permute-start(f32[2,128,128]{2,1,0:T(8,128)S(1)} %half.5), channel_id=1, source_target_pairs={{0,8},{4,12},{8,0},{12,4},{1,9},{5,13},{9,1},{13,5},{2,10},{6,14},... | collective-permute-start | bytes 393224 | tf_op jit(solution)/shard_map/ppermute | solution.py:255
  10.9 4.0 %copy-start.1 = (bf16[1024,1024]{1,0:T(8,128)(2,1)S(1)}, bf16[1024,1024]{1,0:T(8,128)(2,1)}, u32[]{:S(2)}) copy-start(bf16[1024,1024]{1,0:T(8,128)(2,1)} %refs_2_.3) | copy-start | bytes 6291460
  11.0 3.9 %copy-start.2 = (f32[8,128,128]{2,1,0:T(8,128)S(1)}, f32[8,128,128]{2,1,0:T(8,128)}, u32[]{:S(2)}) copy-start(f32[8,128,128]{2,1,0:T(8,128)} %refs_3_.3) | copy-start | bytes 1572868
  12.6 2.3 %collective-permute-start.3 = (f32[2,128,128]{2,1,0:T(8,128)S(1)}, f32[2,128,128]{2,1,0:T(8,128)S(1)}, u32[]{:S(2)}, u32[]{:S(2)}) collective-permute-start(f32[2,128,128]{2,1,0:T(8,128)S(1)} %collective-permute-done.1.refs_5_), channel_id=1, source_target_pairs={{0,4},{4,0},{8,12},{12,8},{1,5},{5,1},{9,13},{13,9},{2,6},{6,2},{1... | collective-permute-start | bytes 393224 | tf_op jit(solution)/shard_map/ppermute | solution.py:254
  14.9 2.6 %collective-permute-start.5 = (f32[2,128,128]{2,1,0:T(8,128)S(1)}, f32[2,128,128]{2,1,0:T(8,128)S(1)}, u32[]{:S(2)}, u32[]{:S(2)}) collective-permute-start(f32[2,128,128]{2,1,0:T(8,128)S(1)} %collective-permute-done.4.refs_5_), channel_id=1, source_target_pairs={{0,4},{4,0},{8,12},{12,8},{1,5},{5,1},{9,13},{13,9},{2,6},{6,2},{1... | collective-permute-start | bytes 393224 | tf_op jit(solution)/shard_map/ppermute | solution.py:254
  16.9 2.6 %collective-permute-start.6 = (f32[4,128,128]{2,1,0:T(8,128)S(1)}, f32[4,128,128]{2,1,0:T(8,128)S(1)}, u32[]{:S(2)}, u32[]{:S(2)}) collective-permute-start(f32[4,128,128]{2,1,0:T(8,128)S(1)} %get-tuple-element.73.own_ref.refs_5_), channel_id=1, source_target_pairs={{0,4},{4,0},{8,12},{12,8},{1,5},{5,1},{9,13},{13,9},{2,6},{6,2},{1... | collective-permute-start | bytes 786440 | tf_op jit(solution)/shard_map/ppermute | solution.py:254
  19.4 1.9 %collective-permute-start.9 = (f32[4,128,128]{2,1,0:T(8,128)S(1)}, f32[4,128,128]{2,1,0:T(8,128)S(1)}, u32[]{:S(2)}, u32[]{:S(2)}) collective-permute-start(f32[4,128,128]{2,1,0:T(8,128)S(1)} %get-tuple-element.88.own_ref.refs_5_), channel_id=1, source_target_pairs={{0,4},{4,0},{8,12},{12,8},{1,5},{5,1},{9,13},{13,9},{2,6},{6,2},{1... | collective-permute-start | bytes 786440 | tf_op jit(solution)/shard_map/ppermute | solution.py:254
  19.5 6.4 %collective-permute-start.7 = (f32[2,128,128]{2,1,0:T(8,128)S(1)}, f32[2,128,128]{2,1,0:T(8,128)S(1)}, u32[]{:S(2)}, u32[]{:S(2)}) collective-permute-start(f32[2,128,128]{2,1,0:T(8,128)S(1)} %half.6), channel_id=1, source_target_pairs={{0,8},{4,12},{8,0},{12,4},{1,9},{5,13},{9,1},{13,5},{2,10},{6,14},... | collective-permute-start | bytes 393224 | tf_op jit(solution)/shard_map/ppermute | solution.py:255
  21.4 6.9 %collective-permute-start.10 = (f32[2,128,128]{2,1,0:T(8,128)S(1)}, f32[2,128,128]{2,1,0:T(8,128)S(1)}, u32[]{:S(2)}, u32[]{:S(2)}) collective-permute-start(f32[2,128,128]{2,1,0:T(8,128)S(1)} %half.7), channel_id=1, source_target_pairs={{0,8},{4,12},{8,0},{12,4},{1,9},{5,13},{9,1},{13,5},{2,10},{6,14},... | collective-permute-start | bytes 393224 | tf_op jit(solution)/shard_map/ppermute | solution.py:255
  25.9 2.9 %collective-permute-start.8 = (f32[2,128,128]{2,1,0:T(8,128)S(1)}, f32[2,128,128]{2,1,0:T(8,128)S(1)}, u32[]{:S(2)}, u32[]{:S(2)}) collective-permute-start(f32[2,128,128]{2,1,0:T(8,128)S(1)} %collective-permute-done.7.refs_7_.refs_9_), channel_id=1, source_target_pairs={{0,4},{4,0},{8,12},{12,8},{1,5},{5,1},{9,13},{13,9},{2,6},{6,2},{1... | collective-permute-start | bytes 393224 | tf_op jit(solution)/shard_map/ppermute | solution.py:254
  28.3 2.3 %collective-permute-start.11 = (f32[2,128,128]{2,1,0:T(8,128)S(1)}, f32[2,128,128]{2,1,0:T(8,128)S(1)}, u32[]{:S(2)}, u32[]{:S(2)}) collective-permute-start(f32[2,128,128]{2,1,0:T(8,128)S(1)} %collective-permute-done.10.refs_7_.refs_9_), channel_id=1, source_target_pairs={{0,4},{4,0},{8,12},{12,8},{1,5},{5,1},{9,13},{13,9},{2,6},{6,2},{1... | collective-permute-start | bytes 393224 | tf_op jit(solution)/shard_map/ppermute | solution.py:254

commit v4 on v3

--- a/solution.py
+++ b/solution.py
@@ -91,7 +91,7 @@
         total_ref[h] = run
 
 
-def inner_kernel(cut, q_ref, k_ref, v_ref, before_ref, att_ref, scores_ref):
+def inner_kernel(cut, q_ref, k_ref, v_ref, before_ref, att_ref, scores_ref, qt_ref):
     keep = causal(cut.size)
     each = cut.each()
     q = {(h, c): q_ref[cut.rng(c), cut.whole(h)] for h, c in each}
@@ -105,6 +105,7 @@
     for h, c in each:
         scores_ref[h, c] = scores[h, c]
         att_ref[cut.rng(c), cut.cols(h)] = att[h, c]
+        qt_ref[cut.cols(h), cut.rng(c)] = q[h, c].T
 
 
 def far_of(per, h, own_half, other_half):
@@ -115,8 +116,8 @@
 
 
 def norm_kernel(cut, masked, *refs):
-    att_ref, q_ref, g_ref, init_ref, near_ref, far_ref, other_ref = refs[:7]
-    out_ref, ga_ref, total_ref, after_ref, prefix_ref = refs[7:]
+    att_ref, q_ref, qt_ref, g_ref, init_ref, near_ref, far_ref, other_ref = refs[:8]
+    out_ref, ga_ref, total_ref, after_ref, prefix_ref = refs[8:]
     place = lax.axis_index("ctx")
     add_near = lax.rem(place, 2) == 1
     add_far = place >= 2
@@ -125,31 +126,30 @@
         if not masked:
             full = jnp.where(add_far, full, 0.0)
         prefix_ref[h] = init_ref[cut.base + h] + (full + jnp.where(add_near, near_ref[h], 0.0))
-    ga = {}
-    for h, c in cut.each():
-        q = q_ref[cut.rng(c), cut.whole(h)]
-        att = att_ref[cut.rng(c), cut.cols(h)] + mm(q, prefix_ref[h].astype(BF16))
-        up = g_ref[cut.rng(c), cut.whole(h)].astype(F32)
-        square = jnp.sum(att * att, axis=-1, keepdims=True)
-        along = jnp.sum(up * att, axis=-1, keepdims=True)
-        inv = lax.rsqrt(square * (1.0 / cut.dim) + EPS)
-        normed = att * inv
-        ga[h, c] = (inv * (up - normed * (along * (inv * (1.0 / cut.dim))))).astype(BF16)
-        out_ref[cut.rng(c), cut.cols(h)] = normed.astype(BF16)
-        ga_ref[cut.rng(c), cut.cols(h)] = ga[h, c]
-    terms = {(h, c): mm_lt(q_ref[cut.rng(c), cut.whole(h)], ga[h, c]) for h, c in cut.each()}
     for h in range(cut.per):
+        att = att_ref[:, cut.cols(h)] + mm(q_ref[:, cut.whole(h)], prefix_ref[h].astype(BF16))
+        ga = []
+        for c in range(cut.chunks):
+            x = att[cut.rng(c)]
+            up = g_ref[cut.rng(c), cut.whole(h)].astype(F32)
+            square = jnp.sum(x * x, axis=-1, keepdims=True)
+            along = jnp.sum(up * x, axis=-1, keepdims=True)
+            inv = lax.rsqrt(square * (1.0 / cut.dim) + EPS)
+            normed = x * inv
+            ga.append((inv * (up - normed * (along * (inv * (1.0 / cut.dim))))).astype(BF16))
+            out_ref[cut.rng(c), cut.cols(h)] = normed.astype(BF16)
+            ga_ref[cut.rng(c), cut.cols(h)] = ga[c]
         run = jnp.zeros((cut.dim, cut.dim), F32)
         for c in reversed(range(cut.chunks)):
             after_ref[h, c] = run
-            run = run + terms[h, c]
+            run = run + mm(qt_ref[cut.cols(h), cut.rng(c)], ga[c])
         total_ref[h] = run
 
 
 def back_kernel(cuts, g, *refs):
     cut = cuts[g]
     count = len(cuts) if g == 0 else 0
-    q_ref, k_ref, v_ref, ga_ref, prefix_ref, before_ref, scores_ref = refs[:7]
+    qt_ref, k_ref, v_ref, ga_ref, prefix_ref, before_ref, scores_ref = refs[:7]
     ready = refs[7 : 7 + count]
     qg_ref, kg_ref, vg_ref = refs[7 + count : 10 + count]
     copies = []
@@ -158,7 +158,7 @@
         copies = column_copies([(r, hbm.at[:, cuts[i].span()]) for i, r in enumerate(ready)], sems)
     keep = causal(cut.size)
     each = cut.each()
-    q = {j: q_ref[cut.rng(j[1]), cut.whole(j[0])] for j in each}
+    qt = {j: qt_ref[cut.cols(j[0]), cut.rng(j[1])] for j in each}
     k = {j: k_ref[cut.rng(j[1]), cut.cols(j[0])] for j in each}
     v = {j: v_ref[cut.rng(j[1]), cut.cols(j[0])] for j in each}
     ga = {j: ga_ref[cut.rng(j[1]), cut.cols(j[0])] for j in each}
@@ -171,7 +171,7 @@
     for h, c in each:
         qg_ref[cut.rng(c), cut.cols(h)] = qg[h, c].astype(BF16)
     vg = {j: mm(ga[j].T, scores[j]) for j in each}
-    kg = {j: mm(q[j].T, grad[j]) for j in each}
+    kg = {j: mm(qt[j], grad[j]) for j in each}
     for h, c in each:
         kg_ref[cut.cols(h), cut.rng(c)] = kg[h, c]
         vg_ref[cut.cols(h), cut.rng(c)] = vg[h, c]
@@ -326,18 +326,18 @@
     for g, cut in enumerate(cuts):
         own[g], before[g], keys_v[g], values_v[g] = state_call(g)
         near[g] = swap(own[g])
-    att, scores, far, other = {}, {}, {}, {}
+    att, scores, queries_t, far, other = {}, {}, {}, {}, {}
     for g in range(groups):
         mine = half_of(own[g], near[g])
         far[g], _ = far_sums(mine, False)
         if g == groups - 1:
             mine, before[0] = lax.optimization_barrier((mine, before[0]))
     for g, cut in enumerate(cuts):
-        att[g], scores[g] = call(
+        att[g], scores[g], queries_t[g] = call(
             functools.partial(inner_kernel, cut),
             "inner%d" % g,
             [queries, keys_v[g], values_v[g], before[g]],
-            [part_f, scores_b],
+            [part_f, scores_b, pltpu.VMEM((per * dim, rows), BF16)],
             [],
             2 * square + small,
             0,
@@ -351,7 +351,7 @@
         out[g], ga[g], total[g], after[g], prefix[g] = call(
             functools.partial(norm_kernel, cut, masked),
             "norm%d" % g,
-            [att[g], queries, out_grad, init_state, near[g], far[g], other[g]],
+            [att[g], queries, queries_t[g], out_grad, init_state, near[g], far[g], other[g]],
             [part_b, part_b, state_f, states_f, state_f],
             [],
             2 * small,
@@ -367,7 +367,7 @@
         qg[g], kp[g], vp[g], *written = call(
             functools.partial(back_kernel, cuts, g),
             "back%d" % g,
-            [queries, keys_v[g], values_v[g], ga[g], prefix[g], before[g], scores[g], *ready],
+            [queries_t[g], keys_v[g], values_v[g], ga[g], prefix[g], before[g], scores[g], *ready],
             [part_b, part_ft, part_ft] + [wide_b] * (g == 0),
             [dma((groups,))] if g == 0 else [],
             4 * square + small,

time: 33.5 us -> 33.2 us (level)
  Pallas kernels: 20.6 us -> 19.4 us
  waiting for transfers between devices: 2.53 us -> 3.43 us
    pallas_call x8, Pallas kernels: 16.5 us -> 15.3 us  [call(): pl.pallas_call(body, in_specs=[VM] * len(ins), out_specs=[HB if isinstanc...]
    ppermute x4, waiting for transfers between devices: 2.51 us -> 3.41 us  [shards(): shift = lambda x: lax.ppermute(x, 'ctx', shift_pairs)]
  transfers between devices with their start and end apart: 12 -> 12, of which waited for: 4 -> 4; matrix products, arithmetic and copies ran while one was open for 0% -> 0% of each run, Pallas kernels for 48% -> 45%
where the time goes in v4:
time: 33.2 us; the launch traced here: 33 us
  Pallas kernels  19.4 us (58%)
  starting transfers between devices  9.2 us (28%)
  waiting for transfers between devices  3.43 us (10%)
  between operations  0.93 us (3%)
    pallas_call x8, Pallas kernels, call(): pl.pallas_call(body, in_specs=[VM] * len(ins), out_specs=[HB if isinstanc...  15.3 us
    ppermute x4, starting transfers between devices, shards(): shift = lambda x: lax.ppermute(x, 'ctx', shift_pairs)  7.33 us
    pallas_call x2, Pallas kernels, state_call(): pl.pallas_call(functools.partial(state_kernel, cuts[g]), in_specs=[HB, HB...  4 us
    ppermute x4, waiting for transfers between devices, shards(): shift = lambda x: lax.ppermute(x, 'ctx', shift_pairs)  3.41 us
    ppermute x8, starting transfers between devices, shards(): swap = lambda x: lax.ppermute(x, 'ctx', swap_pairs)  1.86 us
  transfers between devices with their start and end apart: 12, of which 4 were waited for; matrix products, arithmetic and copies ran while one was open for 0% of the time, Pallas kernels for 45%

profile of v4, /device:TPU:0, one launch (start us, length us, event | category | flops | bytes accessed | tf_op | source)
XLA Modules:
  0.0 33.0 jit_solution(9686418735259363625)
XLA Ops:
  0.6 2.0 %states0.1 = (f32[4,128,128]{2,1,0:T(8,128)S(1)}, f32[4,4,128,128]{3,2,1,0:T(8,128)S(1)}, bf16[1024,512]{1,0:T(8,128)(2,1)S(1)}, bf16[1024,512]{1,0:T(8,128)(2,1)S(1)}) custom-call(bf16[1024,1024]{1,0:T(8,128)(2,1)} %k_hbm.3, bf16[1024,1024]{1,0:T(8,128)(2,1)} %v_hbm.3, bf16[1024,1024]{1,0:T(8,128)(2,1)} %k_hbm.3), custom_call_target="tpu_custom_call" | custom-call | flops 134217728 | bytes 2097152 | tf_op jit(solution)/shard_map/states0/pallas_call | solution.py:311
  2.6 0.0 copy-start
  2.6 0.5 %collective-permute-start.1 = (f32[4,128,128]{2,1,0:T(8,128)S(1)}, f32[4,128,128]{2,1,0:T(8,128)S(1)}, u32[]{:S(2)}, u32[]{:S(2)}) collective-permute-start(f32[4,128,128]{2,1,0:T(8,128)S(1)} %get-tuple-element.57._.own_ref), channel_id=1, source_target_pairs={{0,4},{4,0},{8,12},{12,8},{1,5},{5,1},{9,13},{13,9},{2,6},{6,2},{1... | collective-permute-start | bytes 786440 | tf_op jit(solution)/shard_map/ppermute | solution.py:254
  3.1 2.0 %states1.1 = (f32[4,128,128]{2,1,0:T(8,128)S(1)}, f32[4,4,128,128]{3,2,1,0:T(8,128)S(1)}, bf16[1024,512]{1,0:T(8,128)(2,1)S(1)}, bf16[1024,512]{1,0:T(8,128)(2,1)S(1)}) custom-call(bf16[1024,1024]{1,0:T(8,128)(2,1)} %k_hbm.3, bf16[1024,1024]{1,0:T(8,128)(2,1)} %v_hbm.3, f32[4,128,128]{2,1,0:T(8,128)S(1)} %get-tuple-element.57._.own_ref), custom_call_target="tpu_custom_call" | custom-call | flops 134217728 | bytes 2097152 | tf_op jit(solution)/shard_map/states1/pallas_call | solution.py:311
  5.2 0.1 collective-permute-start
  5.3 0.0 collective-permute-done.1.near_ref.refs_5_
  5.4 2.9 %collective-permute-start.2 = (f32[2,128,128]{2,1,0:T(8,128)S(1)}, f32[2,128,128]{2,1,0:T(8,128)S(1)}, u32[]{:S(2)}, u32[]{:S(2)}) collective-permute-start(f32[2,128,128]{2,1,0:T(8,128)S(1)} %half.5), channel_id=1, source_target_pairs={{0,8},{4,12},{8,0},{12,4},{1,9},{5,13},{9,1},{13,5},{2,10},{6,14},... | collective-permute-start | bytes 393224 | tf_op jit(solution)/shard_map/ppermute | solution.py:255
  8.3 0.0 collective-permute-done.near_ref.refs_5_
  8.3 1.2 %collective-permute-start.4 = (f32[2,128,128]{2,1,0:T(8,128)S(1)}, f32[2,128,128]{2,1,0:T(8,128)S(1)}, u32[]{:S(2)}, u32[]{:S(2)}) collective-permute-start(f32[2,128,128]{2,1,0:T(8,128)S(1)} %half.4), channel_id=1, source_target_pairs={{0,8},{4,12},{8,0},{12,4},{1,9},{5,13},{9,1},{13,5},{2,10},{6,14},... | collective-permute-start | bytes 393224 | tf_op jit(solution)/shard_map/ppermute | solution.py:255
  9.5 0.0 copy-done
  9.5 1.5 %inner1.1 = (f32[1024,512]{1,0:T(8,128)S(1)}, bf16[4,4,256,256]{3,2,1,0:T(8,128)(2,1)S(1)}, bf16[512,1024]{1,0:T(8,128)(2,1)S(1)}) custom-call(bf16[1024,1024]{1,0:T(8,128)(2,1)S(1)} %copy-done, bf16[1024,512]{1,0:T(8,128)(2,1)S(1)} %get-tuple-element.63.k_ref.refs_1_.refs_0_, bf16[1024,512]{1,0:T(8,128)(2,1)S(1)} %get-tuple-element.64.v_ref.refs_2_.refs_1_, ...), custom_call_target="tpu_custom_call" | custom-call | flops 671088640 | tf_op jit(solution)/shard_map/inner1/pallas_call | solution.py:272
  11.0 0.0 copy-start.1
  11.0 0.0 copy-start.2
  11.0 1.5 %inner0.1 = (f32[1024,512]{1,0:T(8,128)S(1)}, bf16[4,4,256,256]{3,2,1,0:T(8,128)(2,1)S(1)}, bf16[512,1024]{1,0:T(8,128)(2,1)S(1)}) custom-call(bf16[1024,1024]{1,0:T(8,128)(2,1)S(1)} %copy-done, bf16[1024,512]{1,0:T(8,128)(2,1)S(1)} %get-tuple-element.55.k_ref.refs_1_.refs_0_, bf16[1024,512]{1,0:T(8,128)(2,1)S(1)} %get-tuple-element.56.v_ref.refs_2_.refs_1_, ...), custom_call_target="tpu_custom_call" | custom-call | flops 671088640 | tf_op jit(solution)/shard_map/inner0/pallas_call | solution.py:272
  12.5 0.1 collective-permute-done.2.refs_6_
  12.6 0.1 collective-permute-start.3
  12.6 2.3 %collective-permute-done.4.refs_6_ = f32[2,128,128]{2,1,0:T(8,128)S(1)} collective-permute-done((f32[2,128,128]{2,1,0:T(8,128)S(1)}, f32[2,128,128]{2,1,0:T(8,128)S(1)}, u32[]{:S(2)}, u32[]{:S(2)}) %collective-permute-start.4) | collective-permute-done | bytes 131104 | tf_op jit(solution)/shard_map/ppermute | solution.py:255
  14.9 0.0 collective-permute-start.5
  14.9 0.0 collective-permute-done.3.refs_7_
  14.9 0.0 copy-done.1
  14.9 0.0 copy-done.2
  14.9 1.8 %norm0.1 = (bf16[1024,512]{1,0:T(8,128)(2,1)S(1)}, bf16[1024,512]{1,0:T(8,128)(2,1)S(1)}, f32[4,128,128]{2,1,0:T(8,128)S(1)}, f32[4,4,128,128]{3,2,1,0:T(8,128)S(1)}, f32[4,128,128]{2,1,0:T(8,128)S(1)}) custom-call(f32[1024,512]{1,0:T(8,128)S(1)} %get-tuple-element.67.refs_0_, bf16[1024,1024]{1,0:T(8,128)(2,1)S(1)} %copy-done, ...), custom_call_target="tpu_custom_call" | custom-call | flops 268435456 | bytes 1048576 | tf_op jit(solution)/shard_map/norm0/pallas_call | solution.py:272
  16.7 0.6 %collective-permute-start.6 = (f32[4,128,128]{2,1,0:T(8,128)S(1)}, f32[4,128,128]{2,1,0:T(8,128)S(1)}, u32[]{:S(2)}, u32[]{:S(2)}) collective-permute-start(f32[4,128,128]{2,1,0:T(8,128)S(1)} %get-tuple-element.77.own_ref.refs_5_), channel_id=1, source_target_pairs={{0,4},{4,0},{8,12},{12,8},{1,5},{5,1},{9,13},{13,9},{2,6},{6,2},{1... | collective-permute-start | bytes 786440 | tf_op jit(solution)/shard_map/ppermute | solution.py:254
  17.3 0.0 collective-permute-done.5.refs_7_
  17.3 1.8 %norm1.1 = (bf16[1024,512]{1,0:T(8,128)(2,1)S(1)}, bf16[1024,512]{1,0:T(8,128)(2,1)S(1)}, f32[4,128,128]{2,1,0:T(8,128)S(1)}, f32[4,4,128,128]{3,2,1,0:T(8,128)S(1)}, f32[4,128,128]{2,1,0:T(8,128)S(1)}) custom-call(f32[1024,512]{1,0:T(8,128)S(1)} %get-tuple-element.73.refs_0_, bf16[1024,1024]{1,0:T(8,128)(2,1)S(1)} %copy-done, ...), custom_call_target="tpu_custom_call" | custom-call | flops 268435456 | bytes 1048576 | tf_op jit(solution)/shard_map/norm1/pallas_call | solution.py:272
  19.1 0.1 collective-permute-start.9
  19.2 0.0 collective-permute-done.6.near_ref.refs_6_
  19.2 1.8 %collective-permute-start.7 = (f32[2,128,128]{2,1,0:T(8,128)S(1)}, f32[2,128,128]{2,1,0:T(8,128)S(1)}, u32[]{:S(2)}, u32[]{:S(2)}) collective-permute-start(f32[2,128,128]{2,1,0:T(8,128)S(1)} %half.6), channel_id=1, source_target_pairs={{0,8},{4,12},{8,0},{12,4},{1,9},{5,13},{9,1},{13,5},{2,10},{6,14},... | collective-permute-start | bytes 393224 | tf_op jit(solution)/shard_map/ppermute | solution.py:255
  21.0 0.0 collective-permute-done.9.near_ref.refs_6_
  21.1 1.5 %collective-permute-start.10 = (f32[2,128,128]{2,1,0:T(8,128)S(1)}, f32[2,128,128]{2,1,0:T(8,128)S(1)}, u32[]{:S(2)}, u32[]{:S(2)}) collective-permute-start(f32[2,128,128]{2,1,0:T(8,128)S(1)} %half.7), channel_id=1, source_target_pairs={{0,8},{4,12},{8,0},{12,4},{1,9},{5,13},{9,1},{13,5},{2,10},{6,14},... | collective-permute-start | bytes 393224 | tf_op jit(solution)/shard_map/ppermute | solution.py:255
  22.5 2.1 %back0.1 = (bf16[1024,512]{1,0:T(8,128)(2,1)S(1)}, f32[512,1024]{1,0:T(8,128)S(1)}, f32[512,1024]{1,0:T(8,128)S(1)}, bf16[1024,1024]{1,0:T(8,128)(2,1)}) custom-call(bf16[512,1024]{1,0:T(8,128)(2,1)S(1)} %get-tuple-element.61.refs_2_.refs_0_, bf16[1024,512]{1,0:T(8,128)(2,1)S(1)} %get-tuple-element.55.k_ref.refs_1_.refs_0_, ...), custom_call_target="tpu_custom_call" | custom-call | flops 1207959552 | bytes 1048576 | tf_op jit(solution)/shard_map/back0/pallas_call | solution.py:272
  24.6 0.9 %collective-permute-done.7.refs_7_.refs_9_ = f32[2,128,128]{2,1,0:T(8,128)S(1)} collective-permute-done((f32[2,128,128]{2,1,0:T(8,128)S(1)}, f32[2,128,128]{2,1,0:T(8,128)S(1)}, u32[]{:S(2)}, u32[]{:S(2)}) %collective-permute-start.7) | collective-permute-done | bytes 131104 | tf_op jit(solution)/shard_map/ppermute | solution.py:255
  25.6 0.0 collective-permute-start.8
  25.6 2.3 %back1.1 = (bf16[1024,512]{1,0:T(8,128)(2,1)S(1)}, f32[512,1024]{1,0:T(8,128)S(1)}, f32[512,1024]{1,0:T(8,128)S(1)}) custom-call(bf16[512,1024]{1,0:T(8,128)(2,1)S(1)} %get-tuple-element.74.refs_2_.refs_0_, bf16[1024,512]{1,0:T(8,128)(2,1)S(1)} %get-tuple-element.63.k_ref.refs_1_.refs_0_, bf16[1024,512]{1,0:T(8,128)(2,1)S(1)} %get-tuple-element.64.v_ref.refs_2_.refs_1_, ...), custom_call_target="tpu_custom_call" | custom-call | flops 1207959552 | bytes 1048576 | tf_op jit(solution)/shard_map/back1/pallas_call | solution.py:272
  27.9 0.1 collective-permute-done.10.refs_7_.refs_9_
  28.0 0.5 %collective-permute-start.11 = (f32[2,128,128]{2,1,0:T(8,128)S(1)}, f32[2,128,128]{2,1,0:T(8,128)S(1)}, u32[]{:S(2)}, u32[]{:S(2)}) collective-permute-start(f32[2,128,128]{2,1,0:T(8,128)S(1)} %collective-permute-done.10.refs_7_.refs_9_), channel_id=1, source_target_pairs={{0,4},{4,0},{8,12},{12,8},{1,5},{5,1},{9,13},{13,9},{2,6},{6,2},{1... | collective-permute-start | bytes 393224 | tf_op jit(solution)/shard_map/ppermute | solution.py:254
  28.5 0.0 collective-permute-done.8.refs_8_.refs_10_
  28.5 1.8 %last0.1 = (bf16[1024,512]{1,0:T(8,128)(2,1)S(1)}, bf16[1024,512]{1,0:T(8,128)(2,1)S(1)}, f32[4,128,128]{2,1,0:T(8,128)S(1)}, bf16[1024,1024]{1,0:T(8,128)(2,1)}) custom-call(bf16[1024,512]{1,0:T(8,128)(2,1)S(1)} %get-tuple-element.55.k_ref.refs_1_.refs_0_, bf16[1024,512]{1,0:T(8,128)(2,1)S(1)} %get-tuple-element.56.v_ref.refs_2_.refs_1_, ...), custom_call_target="tpu_custom_call" | custom-call | flops 268435456 | bytes 2097152 | tf_op jit(solution)/shard_map/last0/pallas_call | solution.py:272
  30.3 0.0 collective-permute-done.11.refs_8_.refs_10_
  30.3 2.6 %last1.1 = (bf16[1024,1024]{1,0:T(8,128)(2,1)}, bf16[1024,1024]{1,0:T(8,128)(2,1)}, f32[8,128,128]{2,1,0:T(8,128)}) custom-call(bf16[1024,512]{1,0:T(8,128)(2,1)S(1)} %get-tuple-element.63.k_ref.refs_1_.refs_0_, bf16[1024,512]{1,0:T(8,128)(2,1)S(1)} %get-tuple-element.64.v_ref.refs_2_.refs_1_, f32[512,1024]{1,0:T(8,128)S(1)} %get-tuple-element.94.refs_2_, ...), custom_call_target="tpu_custom_call" | custom-call | flops 268435456 | bytes 2097152 | tf_op jit(solution)/shard_map/last1/pallas_call | solution.py:272
  (4 shorter events, 0.1 us)
Async XLA Ops:
  2.6 6.9 %copy-start = (bf16[1024,1024]{1,0:T(8,128)(2,1)S(1)}, bf16[1024,1024]{1,0:T(8,128)(2,1)}, u32[]{:S(2)}) copy-start(bf16[1024,1024]{1,0:T(8,128)(2,1)} %refs_1_.3) | copy-start | bytes 6291460
  2.6 2.7 %collective-permute-start.1 = (f32[4,128,128]{2,1,0:T(8,128)S(1)}, f32[4,128,128]{2,1,0:T(8,128)S(1)}, u32[]{:S(2)}, u32[]{:S(2)}) collective-permute-start(f32[4,128,128]{2,1,0:T(8,128)S(1)} %get-tuple-element.57._.own_ref), channel_id=1, source_target_pairs={{0,4},{4,0},{8,12},{12,8},{1,5},{5,1},{9,13},{13,9},{2,6},{6,2},{1... | collective-permute-start | bytes 786440 | tf_op jit(solution)/shard_map/ppermute | solution.py:254
  5.2 3.1 %collective-permute-start = (f32[4,128,128]{2,1,0:T(8,128)S(1)}, f32[4,128,128]{2,1,0:T(8,128)S(1)}, u32[]{:S(2)}, u32[]{:S(2)}) collective-permute-start(f32[4,128,128]{2,1,0:T(8,128)S(1)} %get-tuple-element.58.own_ref), channel_id=1, source_target_pairs={{0,4},{4,0},{8,12},{12,8},{1,5},{5,1},{9,13},{13,9},{2,6},{6,2},{1... | collective-permute-start | bytes 786440 | tf_op jit(solution)/shard_map/ppermute | solution.py:254
  5.4 7.2 %collective-permute-start.2 = (f32[2,128,128]{2,1,0:T(8,128)S(1)}, f32[2,128,128]{2,1,0:T(8,128)S(1)}, u32[]{:S(2)}, u32[]{:S(2)}) collective-permute-start(f32[2,128,128]{2,1,0:T(8,128)S(1)} %half.5), channel_id=1, source_target_pairs={{0,8},{4,12},{8,0},{12,4},{1,9},{5,13},{9,1},{13,5},{2,10},{6,14},... | collective-permute-start | bytes 393224 | tf_op jit(solution)/shard_map/ppermute | solution.py:255
  8.3 6.6 %collective-permute-start.4 = (f32[2,128,128]{2,1,0:T(8,128)S(1)}, f32[2,128,128]{2,1,0:T(8,128)S(1)}, u32[]{:S(2)}, u32[]{:S(2)}) collective-permute-start(f32[2,128,128]{2,1,0:T(8,128)S(1)} %half.4), channel_id=1, source_target_pairs={{0,8},{4,12},{8,0},{12,4},{1,9},{5,13},{9,1},{13,5},{2,10},{6,14},... | collective-permute-start | bytes 393224 | tf_op jit(solution)/shard_map/ppermute | solution.py:255
  11.0 4.0 %copy-start.1 = (bf16[1024,1024]{1,0:T(8,128)(2,1)S(1)}, bf16[1024,1024]{1,0:T(8,128)(2,1)}, u32[]{:S(2)}) copy-start(bf16[1024,1024]{1,0:T(8,128)(2,1)} %refs_3_.3) | copy-start | bytes 6291460
  11.0 3.9 %copy-start.2 = (f32[8,128,128]{2,1,0:T(8,128)S(1)}, f32[8,128,128]{2,1,0:T(8,128)}, u32[]{:S(2)}) copy-start(f32[8,128,128]{2,1,0:T(8,128)} %refs_4_.3) | copy-start | bytes 1572868
  12.6 2.3 %collective-permute-start.3 = (f32[2,128,128]{2,1,0:T(8,128)S(1)}, f32[2,128,128]{2,1,0:T(8,128)S(1)}, u32[]{:S(2)}, u32[]{:S(2)}) collective-permute-start(f32[2,128,128]{2,1,0:T(8,128)S(1)} %collective-permute-done.2.refs_6_), channel_id=1, source_target_pairs={{0,4},{4,0},{8,12},{12,8},{1,5},{5,1},{9,13},{13,9},{2,6},{6,2},{1... | collective-permute-start | bytes 393224 | tf_op jit(solution)/shard_map/ppermute | solution.py:254
  14.9 2.4 %collective-permute-start.5 = (f32[2,128,128]{2,1,0:T(8,128)S(1)}, f32[2,128,128]{2,1,0:T(8,128)S(1)}, u32[]{:S(2)}, u32[]{:S(2)}) collective-permute-start(f32[2,128,128]{2,1,0:T(8,128)S(1)} %collective-permute-done.4.refs_6_), channel_id=1, source_target_pairs={{0,4},{4,0},{8,12},{12,8},{1,5},{5,1},{9,13},{13,9},{2,6},{6,2},{1... | collective-permute-start | bytes 393224 | tf_op jit(solution)/shard_map/ppermute | solution.py:254
  16.7 2.5 %collective-permute-start.6 = (f32[4,128,128]{2,1,0:T(8,128)S(1)}, f32[4,128,128]{2,1,0:T(8,128)S(1)}, u32[]{:S(2)}, u32[]{:S(2)}) collective-permute-start(f32[4,128,128]{2,1,0:T(8,128)S(1)} %get-tuple-element.77.own_ref.refs_5_), channel_id=1, source_target_pairs={{0,4},{4,0},{8,12},{12,8},{1,5},{5,1},{9,13},{13,9},{2,6},{6,2},{1... | collective-permute-start | bytes 786440 | tf_op jit(solution)/shard_map/ppermute | solution.py:254
  19.1 1.9 %collective-permute-start.9 = (f32[4,128,128]{2,1,0:T(8,128)S(1)}, f32[4,128,128]{2,1,0:T(8,128)S(1)}, u32[]{:S(2)}, u32[]{:S(2)}) collective-permute-start(f32[4,128,128]{2,1,0:T(8,128)S(1)} %get-tuple-element.92.own_ref.refs_5_), channel_id=1, source_target_pairs={{0,4},{4,0},{8,12},{12,8},{1,5},{5,1},{9,13},{13,9},{2,6},{6,2},{1... | collective-permute-start | bytes 786440 | tf_op jit(solution)/shard_map/ppermute | solution.py:254
  19.2 6.4 %collective-permute-start.7 = (f32[2,128,128]{2,1,0:T(8,128)S(1)}, f32[2,128,128]{2,1,0:T(8,128)S(1)}, u32[]{:S(2)}, u32[]{:S(2)}) collective-permute-start(f32[2,128,128]{2,1,0:T(8,128)S(1)} %half.6), channel_id=1, source_target_pairs={{0,8},{4,12},{8,0},{12,4},{1,9},{5,13},{9,1},{13,5},{2,10},{6,14},... | collective-permute-start | bytes 393224 | tf_op jit(solution)/shard_map/ppermute | solution.py:255
  21.1 6.9 %collective-permute-start.10 = (f32[2,128,128]{2,1,0:T(8,128)S(1)}, f32[2,128,128]{2,1,0:T(8,128)S(1)}, u32[]{:S(2)}, u32[]{:S(2)}) collective-permute-start(f32[2,128,128]{2,1,0:T(8,128)S(1)} %half.7), channel_id=1, source_target_pairs={{0,8},{4,12},{8,0},{12,4},{1,9},{5,13},{9,1},{13,5},{2,10},{6,14},... | collective-permute-start | bytes 393224 | tf_op jit(solution)/shard_map/ppermute | solution.py:255
  25.6 2.9 %collective-permute-start.8 = (f32[2,128,128]{2,1,0:T(8,128)S(1)}, f32[2,128,128]{2,1,0:T(8,128)S(1)}, u32[]{:S(2)}, u32[]{:S(2)}) collective-permute-start(f32[2,128,128]{2,1,0:T(8,128)S(1)} %collective-permute-done.7.refs_7_.refs_9_), channel_id=1, source_target_pairs={{0,4},{4,0},{8,12},{12,8},{1,5},{5,1},{9,13},{13,9},{2,6},{6,2},{1... | collective-permute-start | bytes 393224 | tf_op jit(solution)/shard_map/ppermute | solution.py:254
  28.0 2.3 %collective-permute-start.11 = (f32[2,128,128]{2,1,0:T(8,128)S(1)}, f32[2,128,128]{2,1,0:T(8,128)S(1)}, u32[]{:S(2)}, u32[]{:S(2)}) collective-permute-start(f32[2,128,128]{2,1,0:T(8,128)S(1)} %collective-permute-done.10.refs_7_.refs_9_), channel_id=1, source_target_pairs={{0,4},{4,0},{8,12},{12,8},{1,5},{5,1},{9,13},{13,9},{2,6},{6,2},{1... | collective-permute-start | bytes 393224 | tf_op jit(solution)/shard_map/ppermute | solution.py:254

commit v5 on v4

--- a/solution.py
+++ b/solution.py
@@ -184,20 +184,18 @@
     k_ref, v_ref, kp_ref, vp_ref, after_ref, own_ref, near_ref = refs[:7]
     far_ref, other_ref, all_ref, all_other_ref = refs[7:11]
     final = g == len(cuts) - 1
-    if g == 0:
-        grads, refs = refs[11 : 11 + len(cuts)], refs[11 + len(cuts) :]
+    ready, refs = [refs[11 + 3 * i : 14 + 3 * i] for i in range(g)], refs[11 + 3 * g :]
+    if final:
+        grads, refs = refs[: len(cuts)], refs[len(cuts) :]
+    if final:
+        kg_hbm, vg_hbm, sg_hbm, hbm, kg_ref, vg_ref, sg_ref, ready_sems, sems, sg_sem, qg_sems = refs
     else:
-        ready, refs = [refs[11 + 3 * i : 14 + 3 * i] for i in range(g)], refs[11 + 3 * g :]
-    if final:
-        kg_hbm, vg_hbm, sg_hbm, kg_ref, vg_ref, sg_ref, ready_sems, sems, sg_sem = refs
-    else:
-        kg_ref, vg_ref, sg_ref = refs[:3]
+        kg_ref, vg_ref, sg_ref = refs
     place = lax.axis_index("ctx")
     add_near = lax.rem(place, 2) == 0
     add_far = place < 2
     copies = []
-    if g == 0:
-        hbm, qg_sems = refs[3:]
+    if final:
         copies += column_copies(
             [(r, hbm.at[:, cuts[i].span()]) for i, r in enumerate(grads)], qg_sems
         )
@@ -376,7 +374,7 @@
         if g == 0:
             (output,) = written
         gfar[g], gall[g], kp[g] = lax.optimization_barrier((gfar[g], gall[g], kp[g]))
-    ready = list(qg.values())
+    ready = []
     for g, cut in enumerate(cuts):
         used = swap(gfar[g])
         total_far = used if pairs == 2 else swap(gall[g])
@@ -386,10 +384,9 @@
         ]
         outs, scratch = [part_b, part_b, state_f], []
         if g == groups - 1:
-            scratch = outs + [dma((3 * g,)), dma((per, 2)), dma((1,))]
-            outs = [wide_b, wide_b, jax.ShapeDtypeStruct(init_state.shape, F32)]
-        elif g == 0:
-            outs, scratch = outs + [wide_b], [dma((groups,))]
+            scratch = outs + [dma((3 * g,)), dma((per, 2)), dma((1,)), dma((groups,))]
+            outs = [wide_b, wide_b, jax.ShapeDtypeStruct(init_state.shape, F32), wide_b]
+            ready += list(qg.values())
         ends = list(
             call(
                 functools.partial(last_kernel, cuts, g, masked),
@@ -401,10 +398,8 @@
                 2 * piece,
             )
         )
-        if g == 0:
-            ready, query_grad = [], ends.pop()
         ready += ends
-    key_grad, value_grad, state_grad = ends
+    key_grad, value_grad, state_grad, query_grad = ends
     return output, query_grad, key_grad, value_grad, state_grad
 
 

time: 33.2 us -> 33 us (level)
  transfers between devices with their start and end apart: 12 -> 12, of which waited for: 4 -> 4; matrix products, arithmetic and copies ran while one was open for 0% -> 0% of each run, Pallas kernels for 45% -> 43%
where the time goes in v5:
time: 33 us; the launch traced here: 32.8 us
  Pallas kernels  19.2 us (58%)
  starting transfers between devices  9.2 us (28%)
  waiting for transfers between devices  3.44 us (10%)
  between operations  0.92 us (3%)
    pallas_call x8, Pallas kernels, call(): pl.pallas_call(body, in_specs=[VM] * len(ins), out_specs=[HB if isinstanc...  15.1 us
    ppermute x4, starting transfers between devices, shards(): shift = lambda x: lax.ppermute(x, 'ctx', shift_pairs)  7.33 us
    pallas_call x2, Pallas kernels, state_call(): pl.pallas_call(functools.partial(state_kernel, cuts[g]), in_specs=[HB, HB...  4 us
    ppermute x4, waiting for transfers between devices, shards(): shift = lambda x: lax.ppermute(x, 'ctx', shift_pairs)  3.41 us
    ppermute x8, starting transfers between devices, shards(): swap = lambda x: lax.ppermute(x, 'ctx', swap_pairs)  1.86 us
  transfers between devices with their start and end apart: 12, of which 4 were waited for; matrix products, arithmetic and copies ran while one was open for 0% of the time, Pallas kernels for 43%

profile of v5, /device:TPU:0, one launch (start us, length us, event | category | flops | bytes accessed | tf_op | source)
XLA Modules:
  0.0 32.8 jit_solution(3330513541468601048)
XLA Ops:
  0.6 2.0 %states0.1 = (f32[4,128,128]{2,1,0:T(8,128)S(1)}, f32[4,4,128,128]{3,2,1,0:T(8,128)S(1)}, bf16[1024,512]{1,0:T(8,128)(2,1)S(1)}, bf16[1024,512]{1,0:T(8,128)(2,1)S(1)}) custom-call(bf16[1024,1024]{1,0:T(8,128)(2,1)} %k_hbm.3, bf16[1024,1024]{1,0:T(8,128)(2,1)} %v_hbm.3, bf16[1024,1024]{1,0:T(8,128)(2,1)} %k_hbm.3), custom_call_target="tpu_custom_call" | custom-call | flops 134217728 | bytes 2097152 | tf_op jit(solution)/shard_map/states0/pallas_call | solution.py:309
  2.6 0.0 copy-start
  2.6 0.5 %collective-permute-start.1 = (f32[4,128,128]{2,1,0:T(8,128)S(1)}, f32[4,128,128]{2,1,0:T(8,128)S(1)}, u32[]{:S(2)}, u32[]{:S(2)}) collective-permute-start(f32[4,128,128]{2,1,0:T(8,128)S(1)} %get-tuple-element.57._.own_ref), channel_id=1, source_target_pairs={{0,4},{4,0},{8,12},{12,8},{1,5},{5,1},{9,13},{13,9},{2,6},{6,2},{1... | collective-permute-start | bytes 786440 | tf_op jit(solution)/shard_map/ppermute | solution.py:252
  3.1 2.0 %states1.1 = (f32[4,128,128]{2,1,0:T(8,128)S(1)}, f32[4,4,128,128]{3,2,1,0:T(8,128)S(1)}, bf16[1024,512]{1,0:T(8,128)(2,1)S(1)}, bf16[1024,512]{1,0:T(8,128)(2,1)S(1)}) custom-call(bf16[1024,1024]{1,0:T(8,128)(2,1)} %k_hbm.3, bf16[1024,1024]{1,0:T(8,128)(2,1)} %v_hbm.3, f32[4,128,128]{2,1,0:T(8,128)S(1)} %get-tuple-element.57._.own_ref), custom_call_target="tpu_custom_call" | custom-call | flops 134217728 | bytes 2097152 | tf_op jit(solution)/shard_map/states1/pallas_call | solution.py:309
  5.2 0.1 collective-permute-start
  5.3 0.0 collective-permute-done.1.near_ref.refs_5_
  5.4 2.9 %collective-permute-start.2 = (f32[2,128,128]{2,1,0:T(8,128)S(1)}, f32[2,128,128]{2,1,0:T(8,128)S(1)}, u32[]{:S(2)}, u32[]{:S(2)}) collective-permute-start(f32[2,128,128]{2,1,0:T(8,128)S(1)} %half.5), channel_id=1, source_target_pairs={{0,8},{4,12},{8,0},{12,4},{1,9},{5,13},{9,1},{13,5},{2,10},{6,14},... | collective-permute-start | bytes 393224 | tf_op jit(solution)/shard_map/ppermute | solution.py:253
  8.3 0.0 collective-permute-done.near_ref.refs_5_
  8.3 1.2 %collective-permute-start.4 = (f32[2,128,128]{2,1,0:T(8,128)S(1)}, f32[2,128,128]{2,1,0:T(8,128)S(1)}, u32[]{:S(2)}, u32[]{:S(2)}) collective-permute-start(f32[2,128,128]{2,1,0:T(8,128)S(1)} %half.4), channel_id=1, source_target_pairs={{0,8},{4,12},{8,0},{12,4},{1,9},{5,13},{9,1},{13,5},{2,10},{6,14},... | collective-permute-start | bytes 393224 | tf_op jit(solution)/shard_map/ppermute | solution.py:253
  9.5 0.0 copy-done
  9.5 1.5 %inner1.1 = (f32[1024,512]{1,0:T(8,128)S(1)}, bf16[4,4,256,256]{3,2,1,0:T(8,128)(2,1)S(1)}, bf16[512,1024]{1,0:T(8,128)(2,1)S(1)}) custom-call(bf16[1024,1024]{1,0:T(8,128)(2,1)S(1)} %copy-done, bf16[1024,512]{1,0:T(8,128)(2,1)S(1)} %get-tuple-element.63.k_ref.refs_1_.refs_0_, bf16[1024,512]{1,0:T(8,128)(2,1)S(1)} %get-tuple-element.64.v_ref.refs_2_.refs_1_, ...), custom_call_target="tpu_custom_call" | custom-call | flops 671088640 | tf_op jit(solution)/shard_map/inner1/pallas_call | solution.py:270
  11.0 0.0 copy-start.1
  11.0 0.0 copy-start.2
  11.0 1.5 %inner0.1 = (f32[1024,512]{1,0:T(8,128)S(1)}, bf16[4,4,256,256]{3,2,1,0:T(8,128)(2,1)S(1)}, bf16[512,1024]{1,0:T(8,128)(2,1)S(1)}) custom-call(bf16[1024,1024]{1,0:T(8,128)(2,1)S(1)} %copy-done, bf16[1024,512]{1,0:T(8,128)(2,1)S(1)} %get-tuple-element.55.k_ref.refs_1_.refs_0_, bf16[1024,512]{1,0:T(8,128)(2,1)S(1)} %get-tuple-element.56.v_ref.refs_2_.refs_1_, ...), custom_call_target="tpu_custom_call" | custom-call | flops 671088640 | tf_op jit(solution)/shard_map/inner0/pallas_call | solution.py:270
  12.5 0.1 collective-permute-done.2.refs_6_
  12.6 0.1 collective-permute-start.3
  12.6 2.3 %collective-permute-done.4.refs_6_ = f32[2,128,128]{2,1,0:T(8,128)S(1)} collective-permute-done((f32[2,128,128]{2,1,0:T(8,128)S(1)}, f32[2,128,128]{2,1,0:T(8,128)S(1)}, u32[]{:S(2)}, u32[]{:S(2)}) %collective-permute-start.4) | collective-permute-done | bytes 131104 | tf_op jit(solution)/shard_map/ppermute | solution.py:253
  14.9 0.0 collective-permute-start.5
  14.9 0.0 collective-permute-done.3.refs_7_
  14.9 0.0 copy-done.1
  14.9 0.0 copy-done.2
  14.9 1.8 %norm0.1 = (bf16[1024,512]{1,0:T(8,128)(2,1)S(1)}, bf16[1024,512]{1,0:T(8,128)(2,1)S(1)}, f32[4,128,128]{2,1,0:T(8,128)S(1)}, f32[4,4,128,128]{3,2,1,0:T(8,128)S(1)}, f32[4,128,128]{2,1,0:T(8,128)S(1)}) custom-call(f32[1024,512]{1,0:T(8,128)S(1)} %get-tuple-element.67.refs_0_, bf16[1024,1024]{1,0:T(8,128)(2,1)S(1)} %copy-done, ...), custom_call_target="tpu_custom_call" | custom-call | flops 268435456 | bytes 1048576 | tf_op jit(solution)/shard_map/norm0/pallas_call | solution.py:270
  16.7 0.6 %collective-permute-start.6 = (f32[4,128,128]{2,1,0:T(8,128)S(1)}, f32[4,128,128]{2,1,0:T(8,128)S(1)}, u32[]{:S(2)}, u32[]{:S(2)}) collective-permute-start(f32[4,128,128]{2,1,0:T(8,128)S(1)} %get-tuple-element.77.own_ref.refs_5_), channel_id=1, source_target_pairs={{0,4},{4,0},{8,12},{12,8},{1,5},{5,1},{9,13},{13,9},{2,6},{6,2},{1... | collective-permute-start | bytes 786440 | tf_op jit(solution)/shard_map/ppermute | solution.py:252
  17.3 0.0 collective-permute-done.5.refs_7_
  17.3 1.8 %norm1.1 = (bf16[1024,512]{1,0:T(8,128)(2,1)S(1)}, bf16[1024,512]{1,0:T(8,128)(2,1)S(1)}, f32[4,128,128]{2,1,0:T(8,128)S(1)}, f32[4,4,128,128]{3,2,1,0:T(8,128)S(1)}, f32[4,128,128]{2,1,0:T(8,128)S(1)}) custom-call(f32[1024,512]{1,0:T(8,128)S(1)} %get-tuple-element.73.refs_0_, bf16[1024,1024]{1,0:T(8,128)(2,1)S(1)} %copy-done, ...), custom_call_target="tpu_custom_call" | custom-call | flops 268435456 | bytes 1048576 | tf_op jit(solution)/shard_map/norm1/pallas_call | solution.py:270
  19.1 0.1 collective-permute-start.7
  19.2 0.0 collective-permute-done.6.near_ref.refs_6_
  19.2 1.8 %collective-permute-start.10 = (f32[2,128,128]{2,1,0:T(8,128)S(1)}, f32[2,128,128]{2,1,0:T(8,128)S(1)}, u32[]{:S(2)}, u32[]{:S(2)}) collective-permute-start(f32[2,128,128]{2,1,0:T(8,128)S(1)} %half.7), channel_id=1, source_target_pairs={{0,8},{4,12},{8,0},{12,4},{1,9},{5,13},{9,1},{13,5},{2,10},{6,14},... | collective-permute-start | bytes 393224 | tf_op jit(solution)/shard_map/ppermute | solution.py:253
  21.0 0.0 collective-permute-done.7.near_ref.refs_6_
  21.1 1.5 %collective-permute-start.8 = (f32[2,128,128]{2,1,0:T(8,128)S(1)}, f32[2,128,128]{2,1,0:T(8,128)S(1)}, u32[]{:S(2)}, u32[]{:S(2)}) collective-permute-start(f32[2,128,128]{2,1,0:T(8,128)S(1)} %half.6), channel_id=1, source_target_pairs={{0,8},{4,12},{8,0},{12,4},{1,9},{5,13},{9,1},{13,5},{2,10},{6,14},... | collective-permute-start | bytes 393224 | tf_op jit(solution)/shard_map/ppermute | solution.py:253
  22.5 2.1 %back0.1 = (bf16[1024,512]{1,0:T(8,128)(2,1)S(1)}, f32[512,1024]{1,0:T(8,128)S(1)}, f32[512,1024]{1,0:T(8,128)S(1)}, bf16[1024,1024]{1,0:T(8,128)(2,1)}) custom-call(bf16[512,1024]{1,0:T(8,128)(2,1)S(1)} %get-tuple-element.61.refs_2_.refs_0_, bf16[1024,512]{1,0:T(8,128)(2,1)S(1)} %get-tuple-element.55.k_ref.refs_1_.refs_0_, ...), custom_call_target="tpu_custom_call" | custom-call | flops 1207959552 | bytes 1048576 | tf_op jit(solution)/shard_map/back0/pallas_call | solution.py:270
  24.6 0.9 %collective-permute-done.10.refs_7_.refs_9_ = f32[2,128,128]{2,1,0:T(8,128)S(1)} collective-permute-done((f32[2,128,128]{2,1,0:T(8,128)S(1)}, f32[2,128,128]{2,1,0:T(8,128)S(1)}, u32[]{:S(2)}, u32[]{:S(2)}) %collective-permute-start.10) | collective-permute-done | bytes 131104 | tf_op jit(solution)/shard_map/ppermute | solution.py:253
  25.6 0.0 collective-permute-start.11
  25.6 2.3 %back1.1 = (bf16[1024,512]{1,0:T(8,128)(2,1)S(1)}, f32[512,1024]{1,0:T(8,128)S(1)}, f32[512,1024]{1,0:T(8,128)S(1)}) custom-call(bf16[512,1024]{1,0:T(8,128)(2,1)S(1)} %get-tuple-element.74.refs_2_.refs_0_, bf16[1024,512]{1,0:T(8,128)(2,1)S(1)} %get-tuple-element.63.k_ref.refs_1_.refs_0_, bf16[1024,512]{1,0:T(8,128)(2,1)S(1)} %get-tuple-element.64.v_ref.refs_2_.refs_1_, ...), custom_call_target="tpu_custom_call" | custom-call | flops 1207959552 | bytes 1048576 | tf_op jit(solution)/shard_map/back1/pallas_call | solution.py:270
  27.9 0.1 collective-permute-done.8.refs_7_.refs_9_
  28.0 0.5 %collective-permute-start.9 = (f32[2,128,128]{2,1,0:T(8,128)S(1)}, f32[2,128,128]{2,1,0:T(8,128)S(1)}, u32[]{:S(2)}, u32[]{:S(2)}) collective-permute-start(f32[2,128,128]{2,1,0:T(8,128)S(1)} %collective-permute-done.8.refs_7_.refs_9_), channel_id=1, source_target_pairs={{0,4},{4,0},{8,12},{12,8},{1,5},{5,1},{9,13},{13,9},{2,6},{6,2},{1... | collective-permute-start | bytes 393224 | tf_op jit(solution)/shard_map/ppermute | solution.py:252
  28.5 0.0 collective-permute-done.11.refs_8_.refs_10_
  28.5 1.0 %last0.1 = (bf16[1024,512]{1,0:T(8,128)(2,1)S(1)}, bf16[1024,512]{1,0:T(8,128)(2,1)S(1)}, f32[4,128,128]{2,1,0:T(8,128)S(1)}) custom-call(bf16[1024,512]{1,0:T(8,128)(2,1)S(1)} %get-tuple-element.55.k_ref.refs_1_.refs_0_, bf16[1024,512]{1,0:T(8,128)(2,1)S(1)} %get-tuple-element.56.v_ref.refs_2_.refs_1_, f32[512,1024]{1,0:T(8,128)S(1)} %get-tuple-element.91.refs_2_, ...), custom_call_target="tpu_custom_call" | custom-call | flops 268435456 | bytes 2097152 | tf_op jit(solution)/shard_map/last0/pallas_call | solution.py:270
  29.4 0.0 collective-permute-done.9.refs_8_.refs_10_
  29.5 3.2 %last1.1 = (bf16[1024,1024]{1,0:T(8,128)(2,1)}, bf16[1024,1024]{1,0:T(8,128)(2,1)}, f32[8,128,128]{2,1,0:T(8,128)}, bf16[1024,1024]{1,0:T(8,128)(2,1)}) custom-call(bf16[1024,512]{1,0:T(8,128)(2,1)S(1)} %get-tuple-element.63.k_ref.refs_1_.refs_0_, bf16[1024,512]{1,0:T(8,128)(2,1)S(1)} %get-tuple-element.64.v_ref.refs_2_.refs_1_, ...), custom_call_target="tpu_custom_call" | custom-call | flops 268435456 | bytes 2097152 | tf_op jit(solution)/shard_map/last1/pallas_call | solution.py:270
  (4 shorter events, 0.1 us)
Async XLA Ops:
  2.6 6.9 %copy-start = (bf16[1024,1024]{1,0:T(8,128)(2,1)S(1)}, bf16[1024,1024]{1,0:T(8,128)(2,1)}, u32[]{:S(2)}) copy-start(bf16[1024,1024]{1,0:T(8,128)(2,1)} %refs_1_.3) | copy-start | bytes 6291460
  2.6 2.7 %collective-permute-start.1 = (f32[4,128,128]{2,1,0:T(8,128)S(1)}, f32[4,128,128]{2,1,0:T(8,128)S(1)}, u32[]{:S(2)}, u32[]{:S(2)}) collective-permute-start(f32[4,128,128]{2,1,0:T(8,128)S(1)} %get-tuple-element.57._.own_ref), channel_id=1, source_target_pairs={{0,4},{4,0},{8,12},{12,8},{1,5},{5,1},{9,13},{13,9},{2,6},{6,2},{1... | collective-permute-start | bytes 786440 | tf_op jit(solution)/shard_map/ppermute | solution.py:252
  5.2 3.1 %collective-permute-start = (f32[4,128,128]{2,1,0:T(8,128)S(1)}, f32[4,128,128]{2,1,0:T(8,128)S(1)}, u32[]{:S(2)}, u32[]{:S(2)}) collective-permute-start(f32[4,128,128]{2,1,0:T(8,128)S(1)} %get-tuple-element.58.own_ref), channel_id=1, source_target_pairs={{0,4},{4,0},{8,12},{12,8},{1,5},{5,1},{9,13},{13,9},{2,6},{6,2},{1... | collective-permute-start | bytes 786440 | tf_op jit(solution)/shard_map/ppermute | solution.py:252
  5.4 7.2 %collective-permute-start.2 = (f32[2,128,128]{2,1,0:T(8,128)S(1)}, f32[2,128,128]{2,1,0:T(8,128)S(1)}, u32[]{:S(2)}, u32[]{:S(2)}) collective-permute-start(f32[2,128,128]{2,1,0:T(8,128)S(1)} %half.5), channel_id=1, source_target_pairs={{0,8},{4,12},{8,0},{12,4},{1,9},{5,13},{9,1},{13,5},{2,10},{6,14},... | collective-permute-start | bytes 393224 | tf_op jit(solution)/shard_map/ppermute | solution.py:253
  8.3 6.6 %collective-permute-start.4 = (f32[2,128,128]{2,1,0:T(8,128)S(1)}, f32[2,128,128]{2,1,0:T(8,128)S(1)}, u32[]{:S(2)}, u32[]{:S(2)}) collective-permute-start(f32[2,128,128]{2,1,0:T(8,128)S(1)} %half.4), channel_id=1, source_target_pairs={{0,8},{4,12},{8,0},{12,4},{1,9},{5,13},{9,1},{13,5},{2,10},{6,14},... | collective-permute-start | bytes 393224 | tf_op jit(solution)/shard_map/ppermute | solution.py:253
  11.0 4.0 %copy-start.1 = (bf16[1024,1024]{1,0:T(8,128)(2,1)S(1)}, bf16[1024,1024]{1,0:T(8,128)(2,1)}, u32[]{:S(2)}) copy-start(bf16[1024,1024]{1,0:T(8,128)(2,1)} %refs_3_.3) | copy-start | bytes 6291460
  11.0 3.9 %copy-start.2 = (f32[8,128,128]{2,1,0:T(8,128)S(1)}, f32[8,128,128]{2,1,0:T(8,128)}, u32[]{:S(2)}) copy-start(f32[8,128,128]{2,1,0:T(8,128)} %refs_4_.3) | copy-start | bytes 1572868
  12.6 2.3 %collective-permute-start.3 = (f32[2,128,128]{2,1,0:T(8,128)S(1)}, f32[2,128,128]{2,1,0:T(8,128)S(1)}, u32[]{:S(2)}, u32[]{:S(2)}) collective-permute-start(f32[2,128,128]{2,1,0:T(8,128)S(1)} %collective-permute-done.2.refs_6_), channel_id=1, source_target_pairs={{0,4},{4,0},{8,12},{12,8},{1,5},{5,1},{9,13},{13,9},{2,6},{6,2},{1... | collective-permute-start | bytes 393224 | tf_op jit(solution)/shard_map/ppermute | solution.py:252
  14.9 2.4 %collective-permute-start.5 = (f32[2,128,128]{2,1,0:T(8,128)S(1)}, f32[2,128,128]{2,1,0:T(8,128)S(1)}, u32[]{:S(2)}, u32[]{:S(2)}) collective-permute-start(f32[2,128,128]{2,1,0:T(8,128)S(1)} %collective-permute-done.4.refs_6_), channel_id=1, source_target_pairs={{0,4},{4,0},{8,12},{12,8},{1,5},{5,1},{9,13},{13,9},{2,6},{6,2},{1... | collective-permute-start | bytes 393224 | tf_op jit(solution)/shard_map/ppermute | solution.py:252
  16.7 2.5 %collective-permute-start.6 = (f32[4,128,128]{2,1,0:T(8,128)S(1)}, f32[4,128,128]{2,1,0:T(8,128)S(1)}, u32[]{:S(2)}, u32[]{:S(2)}) collective-permute-start(f32[4,128,128]{2,1,0:T(8,128)S(1)} %get-tuple-element.77.own_ref.refs_5_), channel_id=1, source_target_pairs={{0,4},{4,0},{8,12},{12,8},{1,5},{5,1},{9,13},{13,9},{2,6},{6,2},{1... | collective-permute-start | bytes 786440 | tf_op jit(solution)/shard_map/ppermute | solution.py:252
  19.1 1.9 %collective-permute-start.7 = (f32[4,128,128]{2,1,0:T(8,128)S(1)}, f32[4,128,128]{2,1,0:T(8,128)S(1)}, u32[]{:S(2)}, u32[]{:S(2)}) collective-permute-start(f32[4,128,128]{2,1,0:T(8,128)S(1)} %get-tuple-element.79.own_ref.refs_5_), channel_id=1, source_target_pairs={{0,4},{4,0},{8,12},{12,8},{1,5},{5,1},{9,13},{13,9},{2,6},{6,2},{1... | collective-permute-start | bytes 786440 | tf_op jit(solution)/shard_map/ppermute | solution.py:252
  19.2 6.4 %collective-permute-start.10 = (f32[2,128,128]{2,1,0:T(8,128)S(1)}, f32[2,128,128]{2,1,0:T(8,128)S(1)}, u32[]{:S(2)}, u32[]{:S(2)}) collective-permute-start(f32[2,128,128]{2,1,0:T(8,128)S(1)} %half.7), channel_id=1, source_target_pairs={{0,8},{4,12},{8,0},{12,4},{1,9},{5,13},{9,1},{13,5},{2,10},{6,14},... | collective-permute-start | bytes 393224 | tf_op jit(solution)/shard_map/ppermute | solution.py:253
  21.1 6.9 %collective-permute-start.8 = (f32[2,128,128]{2,1,0:T(8,128)S(1)}, f32[2,128,128]{2,1,0:T(8,128)S(1)}, u32[]{:S(2)}, u32[]{:S(2)}) collective-permute-start(f32[2,128,128]{2,1,0:T(8,128)S(1)} %half.6), channel_id=1, source_target_pairs={{0,8},{4,12},{8,0},{12,4},{1,9},{5,13},{9,1},{13,5},{2,10},{6,14},... | collective-permute-start | bytes 393224 | tf_op jit(solution)/shard_map/ppermute | solution.py:253
  25.6 2.9 %collective-permute-start.11 = (f32[2,128,128]{2,1,0:T(8,128)S(1)}, f32[2,128,128]{2,1,0:T(8,128)S(1)}, u32[]{:S(2)}, u32[]{:S(2)}) collective-permute-start(f32[2,128,128]{2,1,0:T(8,128)S(1)} %collective-permute-done.10.refs_7_.refs_9_), channel_id=1, source_target_pairs={{0,4},{4,0},{8,12},{12,8},{1,5},{5,1},{9,13},{13,9},{2,6},{6,2},{1... | collective-permute-start | bytes 393224 | tf_op jit(solution)/shard_map/ppermute | solution.py:252
  28.0 1.5 %collective-permute-start.9 = (f32[2,128,128]{2,1,0:T(8,128)S(1)}, f32[2,128,128]{2,1,0:T(8,128)S(1)}, u32[]{:S(2)}, u32[]{:S(2)}) collective-permute-start(f32[2,128,128]{2,1,0:T(8,128)S(1)} %collective-permute-done.8.refs_7_.refs_9_), channel_id=1, source_target_pairs={{0,4},{4,0},{8,12},{12,8},{1,5},{5,1},{9,13},{13,9},{2,6},{6,2},{1... | collective-permute-start | bytes 393224 | tf_op jit(solution)/shard_map/ppermute | solution.py:252

commit v6 on v5

--- a/solution.py
+++ b/solution.py
@@ -222,12 +222,18 @@
             vg = vp_ref[cols, rows] + mm_rt(state.T, k_ref[rows, cols])
             kg_ref[rows, cols] = kg.astype(BF16).T
             vg_ref[rows, cols] = vg.astype(BF16).T
-        if final:
-            at, to = pl.ds(h * cut.dim, cut.dim), pl.ds((cut.base + h) * cut.dim, cut.dim)
-            copies += column_copies(
-                [(kg_ref.at[:, at], kg_hbm.at[:, to]), (vg_ref.at[:, at], vg_hbm.at[:, to])],
-                sems.at[h],
-            )
+            if final and (c == cut.chunks - 1 or (h == cut.per - 1 and c == cut.chunks // 2 - 1)):
+                split = h == cut.per - 1 and cut.chunks > 1
+                start = cut.chunks // 2 if split and c == cut.chunks - 1 else 0
+                span = pl.ds(start * cut.size, (c + 1 - start) * cut.size)
+                at, to = pl.ds(h * cut.dim, cut.dim), pl.ds((cut.base + h) * cut.dim, cut.dim)
+                copies += column_copies(
+                    [
+                        (kg_ref.at[span, at], kg_hbm.at[span, to]),
+                        (vg_ref.at[span, at], vg_hbm.at[span, to]),
+                    ],
+                    sems.at[h + (start > 0)],
+                )
     if final:
         copies += column_copies([(sg_ref, sg_hbm.at[pl.ds(cut.base, cut.per)])], sg_sem)
     for copy in copies:
@@ -384,7 +390,7 @@
         ]
         outs, scratch = [part_b, part_b, state_f], []
         if g == groups - 1:
-            scratch = outs + [dma((3 * g,)), dma((per, 2)), dma((1,)), dma((groups,))]
+            scratch = outs + [dma((3 * g,)), dma((per + 1, 2)), dma((1,)), dma((groups,))]
             outs = [wide_b, wide_b, jax.ShapeDtypeStruct(init_state.shape, F32), wide_b]
             ready += list(qg.values())
         ends = list(

time: 33 us -> 32.8 us (level)
  no operation moved by 1% of the time
where the time goes in v6:
time: 32.8 us; the launch traced here: 32.6 us
  Pallas kernels  19 us (58%)
  starting transfers between devices  9.2 us (28%)
  waiting for transfers between devices  3.44 us (10%)
  between operations  0.92 us (3%)
    pallas_call x8, Pallas kernels, call(): pl.pallas_call(body, in_specs=[VM] * len(ins), out_specs=[HB if isinstanc...  14.9 us
    ppermute x4, starting transfers between devices, shards(): shift = lambda x: lax.ppermute(x, 'ctx', shift_pairs)  7.33 us
    pallas_call x2, Pallas kernels, state_call(): pl.pallas_call(functools.partial(state_kernel, cuts[g]), in_specs=[HB, HB...  4 us
    ppermute x4, waiting for transfers between devices, shards(): shift = lambda x: lax.ppermute(x, 'ctx', shift_pairs)  3.41 us
    ppermute x8, starting transfers between devices, shards(): swap = lambda x: lax.ppermute(x, 'ctx', swap_pairs)  1.86 us
  transfers between devices with their start and end apart: 12, of which 4 were waited for; matrix products, arithmetic and copies ran while one was open for 0% of the time, Pallas kernels for 43%

profile of v6, /device:TPU:0, one launch (start us, length us, event | category | flops | bytes accessed | tf_op | source)
XLA Modules:
  0.0 32.6 jit_solution(18250891177715221113)
XLA Ops:
  0.6 2.0 %states0.1 = (f32[4,128,128]{2,1,0:T(8,128)S(1)}, f32[4,4,128,128]{3,2,1,0:T(8,128)S(1)}, bf16[1024,512]{1,0:T(8,128)(2,1)S(1)}, bf16[1024,512]{1,0:T(8,128)(2,1)S(1)}) custom-call(bf16[1024,1024]{1,0:T(8,128)(2,1)} %k_hbm.3, bf16[1024,1024]{1,0:T(8,128)(2,1)} %v_hbm.3, bf16[1024,1024]{1,0:T(8,128)(2,1)} %k_hbm.3), custom_call_target="tpu_custom_call" | custom-call | flops 134217728 | bytes 2097152 | tf_op jit(solution)/shard_map/states0/pallas_call | solution.py:315
  2.6 0.0 copy-start
  2.6 0.5 %collective-permute-start.1 = (f32[4,128,128]{2,1,0:T(8,128)S(1)}, f32[4,128,128]{2,1,0:T(8,128)S(1)}, u32[]{:S(2)}, u32[]{:S(2)}) collective-permute-start(f32[4,128,128]{2,1,0:T(8,128)S(1)} %get-tuple-element.57._.own_ref), channel_id=1, source_target_pairs={{0,4},{4,0},{8,12},{12,8},{1,5},{5,1},{9,13},{13,9},{2,6},{6,2},{1... | collective-permute-start | bytes 786440 | tf_op jit(solution)/shard_map/ppermute | solution.py:258
  3.1 2.0 %states1.1 = (f32[4,128,128]{2,1,0:T(8,128)S(1)}, f32[4,4,128,128]{3,2,1,0:T(8,128)S(1)}, bf16[1024,512]{1,0:T(8,128)(2,1)S(1)}, bf16[1024,512]{1,0:T(8,128)(2,1)S(1)}) custom-call(bf16[1024,1024]{1,0:T(8,128)(2,1)} %k_hbm.3, bf16[1024,1024]{1,0:T(8,128)(2,1)} %v_hbm.3, f32[4,128,128]{2,1,0:T(8,128)S(1)} %get-tuple-element.57._.own_ref), custom_call_target="tpu_custom_call" | custom-call | flops 134217728 | bytes 2097152 | tf_op jit(solution)/shard_map/states1/pallas_call | solution.py:315
  5.2 0.1 collective-permute-start
  5.3 0.0 collective-permute-done.1.near_ref.refs_5_
  5.4 2.9 %collective-permute-start.2 = (f32[2,128,128]{2,1,0:T(8,128)S(1)}, f32[2,128,128]{2,1,0:T(8,128)S(1)}, u32[]{:S(2)}, u32[]{:S(2)}) collective-permute-start(f32[2,128,128]{2,1,0:T(8,128)S(1)} %half.5), channel_id=1, source_target_pairs={{0,8},{4,12},{8,0},{12,4},{1,9},{5,13},{9,1},{13,5},{2,10},{6,14},... | collective-permute-start | bytes 393224 | tf_op jit(solution)/shard_map/ppermute | solution.py:259
  8.3 0.0 collective-permute-done.near_ref.refs_5_
  8.3 1.2 %collective-permute-start.4 = (f32[2,128,128]{2,1,0:T(8,128)S(1)}, f32[2,128,128]{2,1,0:T(8,128)S(1)}, u32[]{:S(2)}, u32[]{:S(2)}) collective-permute-start(f32[2,128,128]{2,1,0:T(8,128)S(1)} %half.4), channel_id=1, source_target_pairs={{0,8},{4,12},{8,0},{12,4},{1,9},{5,13},{9,1},{13,5},{2,10},{6,14},... | collective-permute-start | bytes 393224 | tf_op jit(solution)/shard_map/ppermute | solution.py:259
  9.5 0.0 copy-done
  9.5 1.5 %inner1.1 = (f32[1024,512]{1,0:T(8,128)S(1)}, bf16[4,4,256,256]{3,2,1,0:T(8,128)(2,1)S(1)}, bf16[512,1024]{1,0:T(8,128)(2,1)S(1)}) custom-call(bf16[1024,1024]{1,0:T(8,128)(2,1)S(1)} %copy-done, bf16[1024,512]{1,0:T(8,128)(2,1)S(1)} %get-tuple-element.63.k_ref.refs_1_.refs_0_, bf16[1024,512]{1,0:T(8,128)(2,1)S(1)} %get-tuple-element.64.v_ref.refs_2_.refs_1_, ...), custom_call_target="tpu_custom_call" | custom-call | flops 671088640 | tf_op jit(solution)/shard_map/inner1/pallas_call | solution.py:276
  11.0 0.0 copy-start.1
  11.0 0.0 copy-start.2
  11.0 1.5 %inner0.1 = (f32[1024,512]{1,0:T(8,128)S(1)}, bf16[4,4,256,256]{3,2,1,0:T(8,128)(2,1)S(1)}, bf16[512,1024]{1,0:T(8,128)(2,1)S(1)}) custom-call(bf16[1024,1024]{1,0:T(8,128)(2,1)S(1)} %copy-done, bf16[1024,512]{1,0:T(8,128)(2,1)S(1)} %get-tuple-element.55.k_ref.refs_1_.refs_0_, bf16[1024,512]{1,0:T(8,128)(2,1)S(1)} %get-tuple-element.56.v_ref.refs_2_.refs_1_, ...), custom_call_target="tpu_custom_call" | custom-call | flops 671088640 | tf_op jit(solution)/shard_map/inner0/pallas_call | solution.py:276
  12.5 0.1 collective-permute-done.2.refs_6_
  12.6 0.1 collective-permute-start.3
  12.6 2.3 %collective-permute-done.4.refs_6_ = f32[2,128,128]{2,1,0:T(8,128)S(1)} collective-permute-done((f32[2,128,128]{2,1,0:T(8,128)S(1)}, f32[2,128,128]{2,1,0:T(8,128)S(1)}, u32[]{:S(2)}, u32[]{:S(2)}) %collective-permute-start.4) | collective-permute-done | bytes 131104 | tf_op jit(solution)/shard_map/ppermute | solution.py:259
  14.9 0.0 collective-permute-start.5
  14.9 0.0 collective-permute-done.3.refs_7_
  14.9 0.0 copy-done.1
  14.9 0.0 copy-done.2
  14.9 1.8 %norm0.1 = (bf16[1024,512]{1,0:T(8,128)(2,1)S(1)}, bf16[1024,512]{1,0:T(8,128)(2,1)S(1)}, f32[4,128,128]{2,1,0:T(8,128)S(1)}, f32[4,4,128,128]{3,2,1,0:T(8,128)S(1)}, f32[4,128,128]{2,1,0:T(8,128)S(1)}) custom-call(f32[1024,512]{1,0:T(8,128)S(1)} %get-tuple-element.67.refs_0_, bf16[1024,1024]{1,0:T(8,128)(2,1)S(1)} %copy-done, ...), custom_call_target="tpu_custom_call" | custom-call | flops 268435456 | bytes 1048576 | tf_op jit(solution)/shard_map/norm0/pallas_call | solution.py:276
  16.7 0.6 %collective-permute-start.6 = (f32[4,128,128]{2,1,0:T(8,128)S(1)}, f32[4,128,128]{2,1,0:T(8,128)S(1)}, u32[]{:S(2)}, u32[]{:S(2)}) collective-permute-start(f32[4,128,128]{2,1,0:T(8,128)S(1)} %get-tuple-element.77.own_ref.refs_5_), channel_id=1, source_target_pairs={{0,4},{4,0},{8,12},{12,8},{1,5},{5,1},{9,13},{13,9},{2,6},{6,2},{1... | collective-permute-start | bytes 786440 | tf_op jit(solution)/shard_map/ppermute | solution.py:258
  17.3 0.0 collective-permute-done.5.refs_7_
  17.3 1.8 %norm1.1 = (bf16[1024,512]{1,0:T(8,128)(2,1)S(1)}, bf16[1024,512]{1,0:T(8,128)(2,1)S(1)}, f32[4,128,128]{2,1,0:T(8,128)S(1)}, f32[4,4,128,128]{3,2,1,0:T(8,128)S(1)}, f32[4,128,128]{2,1,0:T(8,128)S(1)}) custom-call(f32[1024,512]{1,0:T(8,128)S(1)} %get-tuple-element.73.refs_0_, bf16[1024,1024]{1,0:T(8,128)(2,1)S(1)} %copy-done, ...), custom_call_target="tpu_custom_call" | custom-call | flops 268435456 | bytes 1048576 | tf_op jit(solution)/shard_map/norm1/pallas_call | solution.py:276
  19.1 0.1 collective-permute-start.7
  19.2 0.0 collective-permute-done.6.near_ref.refs_6_
  19.2 1.8 %collective-permute-start.10 = (f32[2,128,128]{2,1,0:T(8,128)S(1)}, f32[2,128,128]{2,1,0:T(8,128)S(1)}, u32[]{:S(2)}, u32[]{:S(2)}) collective-permute-start(f32[2,128,128]{2,1,0:T(8,128)S(1)} %half.7), channel_id=1, source_target_pairs={{0,8},{4,12},{8,0},{12,4},{1,9},{5,13},{9,1},{13,5},{2,10},{6,14},... | collective-permute-start | bytes 393224 | tf_op jit(solution)/shard_map/ppermute | solution.py:259
  21.0 0.0 collective-permute-done.7.near_ref.refs_6_
  21.1 1.5 %collective-permute-start.8 = (f32[2,128,128]{2,1,0:T(8,128)S(1)}, f32[2,128,128]{2,1,0:T(8,128)S(1)}, u32[]{:S(2)}, u32[]{:S(2)}) collective-permute-start(f32[2,128,128]{2,1,0:T(8,128)S(1)} %half.6), channel_id=1, source_target_pairs={{0,8},{4,12},{8,0},{12,4},{1,9},{5,13},{9,1},{13,5},{2,10},{6,14},... | collective-permute-start | bytes 393224 | tf_op jit(solution)/shard_map/ppermute | solution.py:259
  22.5 2.1 %back0.1 = (bf16[1024,512]{1,0:T(8,128)(2,1)S(1)}, f32[512,1024]{1,0:T(8,128)S(1)}, f32[512,1024]{1,0:T(8,128)S(1)}, bf16[1024,1024]{1,0:T(8,128)(2,1)}) custom-call(bf16[512,1024]{1,0:T(8,128)(2,1)S(1)} %get-tuple-element.61.refs_2_.refs_0_, bf16[1024,512]{1,0:T(8,128)(2,1)S(1)} %get-tuple-element.55.k_ref.refs_1_.refs_0_, ...), custom_call_target="tpu_custom_call" | custom-call | flops 1207959552 | bytes 1048576 | tf_op jit(solution)/shard_map/back0/pallas_call | solution.py:276
  24.6 0.9 %collective-permute-done.10.refs_7_.refs_9_ = f32[2,128,128]{2,1,0:T(8,128)S(1)} collective-permute-done((f32[2,128,128]{2,1,0:T(8,128)S(1)}, f32[2,128,128]{2,1,0:T(8,128)S(1)}, u32[]{:S(2)}, u32[]{:S(2)}) %collective-permute-start.10) | collective-permute-done | bytes 131104 | tf_op jit(solution)/shard_map/ppermute | solution.py:259
  25.6 0.0 collective-permute-start.11
  25.6 2.3 %back1.1 = (bf16[1024,512]{1,0:T(8,128)(2,1)S(1)}, f32[512,1024]{1,0:T(8,128)S(1)}, f32[512,1024]{1,0:T(8,128)S(1)}) custom-call(bf16[512,1024]{1,0:T(8,128)(2,1)S(1)} %get-tuple-element.74.refs_2_.refs_0_, bf16[1024,512]{1,0:T(8,128)(2,1)S(1)} %get-tuple-element.63.k_ref.refs_1_.refs_0_, bf16[1024,512]{1,0:T(8,128)(2,1)S(1)} %get-tuple-element.64.v_ref.refs_2_.refs_1_, ...), custom_call_target="tpu_custom_call" | custom-call | flops 1207959552 | bytes 1048576 | tf_op jit(solution)/shard_map/back1/pallas_call | solution.py:276
  27.9 0.1 collective-permute-done.8.refs_7_.refs_9_
  28.0 0.5 %collective-permute-start.9 = (f32[2,128,128]{2,1,0:T(8,128)S(1)}, f32[2,128,128]{2,1,0:T(8,128)S(1)}, u32[]{:S(2)}, u32[]{:S(2)}) collective-permute-start(f32[2,128,128]{2,1,0:T(8,128)S(1)} %collective-permute-done.8.refs_7_.refs_9_), channel_id=1, source_target_pairs={{0,4},{4,0},{8,12},{12,8},{1,5},{5,1},{9,13},{13,9},{2,6},{6,2},{1... | collective-permute-start | bytes 393224 | tf_op jit(solution)/shard_map/ppermute | solution.py:258
  28.5 0.0 collective-permute-done.11.refs_8_.refs_10_
  28.5 1.0 %last0.1 = (bf16[1024,512]{1,0:T(8,128)(2,1)S(1)}, bf16[1024,512]{1,0:T(8,128)(2,1)S(1)}, f32[4,128,128]{2,1,0:T(8,128)S(1)}) custom-call(bf16[1024,512]{1,0:T(8,128)(2,1)S(1)} %get-tuple-element.55.k_ref.refs_1_.refs_0_, bf16[1024,512]{1,0:T(8,128)(2,1)S(1)} %get-tuple-element.56.v_ref.refs_2_.refs_1_, f32[512,1024]{1,0:T(8,128)S(1)} %get-tuple-element.91.refs_2_, ...), custom_call_target="tpu_custom_call" | custom-call | flops 268435456 | bytes 2097152 | tf_op jit(solution)/shard_map/last0/pallas_call | solution.py:276
  29.4 0.0 collective-permute-done.9.refs_8_.refs_10_
  29.5 3.0 %last1.1 = (bf16[1024,1024]{1,0:T(8,128)(2,1)}, bf16[1024,1024]{1,0:T(8,128)(2,1)}, f32[8,128,128]{2,1,0:T(8,128)}, bf16[1024,1024]{1,0:T(8,128)(2,1)}) custom-call(bf16[1024,512]{1,0:T(8,128)(2,1)S(1)} %get-tuple-element.63.k_ref.refs_1_.refs_0_, bf16[1024,512]{1,0:T(8,128)(2,1)S(1)} %get-tuple-element.64.v_ref.refs_2_.refs_1_, ...), custom_call_target="tpu_custom_call" | custom-call | flops 268435456 | bytes 2097152 | tf_op jit(solution)/shard_map/last1/pallas_call | solution.py:276
  (4 shorter events, 0.1 us)
Async XLA Ops:
  2.6 6.9 %copy-start = (bf16[1024,1024]{1,0:T(8,128)(2,1)S(1)}, bf16[1024,1024]{1,0:T(8,128)(2,1)}, u32[]{:S(2)}) copy-start(bf16[1024,1024]{1,0:T(8,128)(2,1)} %refs_1_.3) | copy-start | bytes 6291460
  2.6 2.7 %collective-permute-start.1 = (f32[4,128,128]{2,1,0:T(8,128)S(1)}, f32[4,128,128]{2,1,0:T(8,128)S(1)}, u32[]{:S(2)}, u32[]{:S(2)}) collective-permute-start(f32[4,128,128]{2,1,0:T(8,128)S(1)} %get-tuple-element.57._.own_ref), channel_id=1, source_target_pairs={{0,4},{4,0},{8,12},{12,8},{1,5},{5,1},{9,13},{13,9},{2,6},{6,2},{1... | collective-permute-start | bytes 786440 | tf_op jit(solution)/shard_map/ppermute | solution.py:258
  5.2 3.1 %collective-permute-start = (f32[4,128,128]{2,1,0:T(8,128)S(1)}, f32[4,128,128]{2,1,0:T(8,128)S(1)}, u32[]{:S(2)}, u32[]{:S(2)}) collective-permute-start(f32[4,128,128]{2,1,0:T(8,128)S(1)} %get-tuple-element.58.own_ref), channel_id=1, source_target_pairs={{0,4},{4,0},{8,12},{12,8},{1,5},{5,1},{9,13},{13,9},{2,6},{6,2},{1... | collective-permute-start | bytes 786440 | tf_op jit(solution)/shard_map/ppermute | solution.py:258
  5.4 7.2 %collective-permute-start.2 = (f32[2,128,128]{2,1,0:T(8,128)S(1)}, f32[2,128,128]{2,1,0:T(8,128)S(1)}, u32[]{:S(2)}, u32[]{:S(2)}) collective-permute-start(f32[2,128,128]{2,1,0:T(8,128)S(1)} %half.5), channel_id=1, source_target_pairs={{0,8},{4,12},{8,0},{12,4},{1,9},{5,13},{9,1},{13,5},{2,10},{6,14},... | collective-permute-start | bytes 393224 | tf_op jit(solution)/shard_map/ppermute | solution.py:259
  8.3 6.6 %collective-permute-start.4 = (f32[2,128,128]{2,1,0:T(8,128)S(1)}, f32[2,128,128]{2,1,0:T(8,128)S(1)}, u32[]{:S(2)}, u32[]{:S(2)}) collective-permute-start(f32[2,128,128]{2,1,0:T(8,128)S(1)} %half.4), channel_id=1, source_target_pairs={{0,8},{4,12},{8,0},{12,4},{1,9},{5,13},{9,1},{13,5},{2,10},{6,14},... | collective-permute-start | bytes 393224 | tf_op jit(solution)/shard_map/ppermute | solution.py:259
  11.0 4.0 %copy-start.1 = (bf16[1024,1024]{1,0:T(8,128)(2,1)S(1)}, bf16[1024,1024]{1,0:T(8,128)(2,1)}, u32[]{:S(2)}) copy-start(bf16[1024,1024]{1,0:T(8,128)(2,1)} %refs_3_.3) | copy-start | bytes 6291460
  11.0 3.9 %copy-start.2 = (f32[8,128,128]{2,1,0:T(8,128)S(1)}, f32[8,128,128]{2,1,0:T(8,128)}, u32[]{:S(2)}) copy-start(f32[8,128,128]{2,1,0:T(8,128)} %refs_4_.3) | copy-start | bytes 1572868
  12.6 2.3 %collective-permute-start.3 = (f32[2,128,128]{2,1,0:T(8,128)S(1)}, f32[2,128,128]{2,1,0:T(8,128)S(1)}, u32[]{:S(2)}, u32[]{:S(2)}) collective-permute-start(f32[2,128,128]{2,1,0:T(8,128)S(1)} %collective-permute-done.2.refs_6_), channel_id=1, source_target_pairs={{0,4},{4,0},{8,12},{12,8},{1,5},{5,1},{9,13},{13,9},{2,6},{6,2},{1... | collective-permute-start | bytes 393224 | tf_op jit(solution)/shard_map/ppermute | solution.py:258
  14.9 2.4 %collective-permute-start.5 = (f32[2,128,128]{2,1,0:T(8,128)S(1)}, f32[2,128,128]{2,1,0:T(8,128)S(1)}, u32[]{:S(2)}, u32[]{:S(2)}) collective-permute-start(f32[2,128,128]{2,1,0:T(8,128)S(1)} %collective-permute-done.4.refs_6_), channel_id=1, source_target_pairs={{0,4},{4,0},{8,12},{12,8},{1,5},{5,1},{9,13},{13,9},{2,6},{6,2},{1... | collective-permute-start | bytes 393224 | tf_op jit(solution)/shard_map/ppermute | solution.py:258
  16.7 2.5 %collective-permute-start.6 = (f32[4,128,128]{2,1,0:T(8,128)S(1)}, f32[4,128,128]{2,1,0:T(8,128)S(1)}, u32[]{:S(2)}, u32[]{:S(2)}) collective-permute-start(f32[4,128,128]{2,1,0:T(8,128)S(1)} %get-tuple-element.77.own_ref.refs_5_), channel_id=1, source_target_pairs={{0,4},{4,0},{8,12},{12,8},{1,5},{5,1},{9,13},{13,9},{2,6},{6,2},{1... | collective-permute-start | bytes 786440 | tf_op jit(solution)/shard_map/ppermute | solution.py:258
  19.1 1.9 %collective-permute-start.7 = (f32[4,128,128]{2,1,0:T(8,128)S(1)}, f32[4,128,128]{2,1,0:T(8,128)S(1)}, u32[]{:S(2)}, u32[]{:S(2)}) collective-permute-start(f32[4,128,128]{2,1,0:T(8,128)S(1)} %get-tuple-element.79.own_ref.refs_5_), channel_id=1, source_target_pairs={{0,4},{4,0},{8,12},{12,8},{1,5},{5,1},{9,13},{13,9},{2,6},{6,2},{1... | collective-permute-start | bytes 786440 | tf_op jit(solution)/shard_map/ppermute | solution.py:258
  19.2 6.4 %collective-permute-start.10 = (f32[2,128,128]{2,1,0:T(8,128)S(1)}, f32[2,128,128]{2,1,0:T(8,128)S(1)}, u32[]{:S(2)}, u32[]{:S(2)}) collective-permute-start(f32[2,128,128]{2,1,0:T(8,128)S(1)} %half.7), channel_id=1, source_target_pairs={{0,8},{4,12},{8,0},{12,4},{1,9},{5,13},{9,1},{13,5},{2,10},{6,14},... | collective-permute-start | bytes 393224 | tf_op jit(solution)/shard_map/ppermute | solution.py:259
  21.1 6.9 %collective-permute-start.8 = (f32[2,128,128]{2,1,0:T(8,128)S(1)}, f32[2,128,128]{2,1,0:T(8,128)S(1)}, u32[]{:S(2)}, u32[]{:S(2)}) collective-permute-start(f32[2,128,128]{2,1,0:T(8,128)S(1)} %half.6), channel_id=1, source_target_pairs={{0,8},{4,12},{8,0},{12,4},{1,9},{5,13},{9,1},{13,5},{2,10},{6,14},... | collective-permute-start | bytes 393224 | tf_op jit(solution)/shard_map/ppermute | solution.py:259
  25.6 2.9 %collective-permute-start.11 = (f32[2,128,128]{2,1,0:T(8,128)S(1)}, f32[2,128,128]{2,1,0:T(8,128)S(1)}, u32[]{:S(2)}, u32[]{:S(2)}) collective-permute-start(f32[2,128,128]{2,1,0:T(8,128)S(1)} %collective-permute-done.10.refs_7_.refs_9_), channel_id=1, source_target_pairs={{0,4},{4,0},{8,12},{12,8},{1,5},{5,1},{9,13},{13,9},{2,6},{6,2},{1... | collective-permute-start | bytes 393224 | tf_op jit(solution)/shard_map/ppermute | solution.py:258
  28.0 1.5 %collective-permute-start.9 = (f32[2,128,128]{2,1,0:T(8,128)S(1)}, f32[2,128,128]{2,1,0:T(8,128)S(1)}, u32[]{:S(2)}, u32[]{:S(2)}) collective-permute-start(f32[2,128,128]{2,1,0:T(8,128)S(1)} %collective-permute-done.8.refs_7_.refs_9_), channel_id=1, source_target_pairs={{0,4},{4,0},{8,12},{12,8},{1,5},{5,1},{9,13},{13,9},{2,6},{6,2},{1... | collective-permute-start | bytes 393224 | tf_op jit(solution)/shard_map/ppermute | solution.py:258
